TPU v7x, 256 devices: a whole 4x4x8 slice. The times are simulated.
256 devices in a mesh: pool: 4 (over x), seq: 8 (over y, core), tp: 8 (over z).
Axes of the slice: x: 4, y: 4, z: 8, core: 2. Of those that a mesh axis runs over, the one named last changes fastest.
Arguments:
- prior_cache: bfloat16 [16, 8192, 8, 2, 128], P(None, ('pool', 'seq'), 'tp'), may hold values from -16 to 16
- prefix_length: int32 [16], replicated, may hold values from 2048 to 8192, as said below
- slot_trace: int32 [16], replicated, may hold values from 0 to 15, each once
- queries: bfloat16 [16, 128, 8, 8, 128], P('seq', None, 'tp', 'pool'), may hold values from -16 to 16
- new_token_cache: bfloat16 [16, 128, 8, 2, 128], P('seq', None, 'tp'), may hold values from -6 to 6
- boundaries: int32 [16, 16], P('seq'), may hold values from 0 to 127, as said below
- output_weight: bfloat16 [8, 8, 128, 8192], P('tp', 'pool'), may hold values from -0.75 to 0.75
- reward_weight: float32 [8192], P(('pool', 'tp')), may hold values from -0.0625 to 0.0625
Outputs:
- layer_out: bfloat16 [16, 128, 8192], P('seq', None, ('pool', 'tp'))
- rewards: float32 [16, 16], P('seq')
Inputs may be any that keep to these rules, and one draw needn't show every extreme that they name: `slot_trace`: a permutation; slot j belongs to scoring group j // 2. `prefix_length`: one trace has exactly 8192 valid positions and another exactly 2048. `boundaries`: each row rises strictly and ends with 127.
All inputs are finite; a program needn't handle non-finite values.
Results may differ from a plain program's by a relative error of at most 0.0085.
Values may be sent and summed in bfloat16 or wider, within the bound.
No kernel may reach another device: no remote copies, remote signals or barrier semaphores. Data moves between devices by JAX's collectives and lax.ppermute only.
A program may use at most 128 MiB of HBM per device.

v0:
```python
import jax
import jax.numpy as jnp
from jax import lax
from jax.sharding import PartitionSpec as P

negative_fill = -1e30


def score_rows(queried, keyed, usable):
    scaling = queried.shape[-1] ** (-0.5)
    scores = (
        jnp.einsum("ikgd,ckd->kgic", queried, keyed, preferred_element_type=jnp.float32) * scaling
    )
    return jnp.where(usable, scores, negative_fill)


def attend_whole(item):
    queried, prior, fresh, length = item
    usable = jnp.arange(prior.shape[0]) < length
    steps_seen = jnp.arange(fresh.shape[0])
    causal = steps_seen[None, :] <= steps_seen[:, None]
    prior_scores = score_rows(queried, prior[:, :, 0], usable)
    fresh_scores = score_rows(queried, fresh[:, :, 0], causal)
    peaks = jnp.maximum(jnp.max(prior_scores, -1), jnp.max(fresh_scores, -1))
    prior_weights = jnp.where(usable, jnp.exp(prior_scores - peaks[..., None]), 0.0)
    fresh_weights = jnp.where(causal, jnp.exp(fresh_scores - peaks[..., None]), 0.0)
    totals = jnp.sum(prior_weights, -1) + jnp.sum(fresh_weights, -1)
    blended = jnp.einsum(
        "kgic,ckd->ikgd",
        prior_weights.astype(jnp.bfloat16),
        prior[:, :, 1],
        preferred_element_type=jnp.float32,
    )
    blended = blended + jnp.einsum(
        "kgij,jkd->ikgd",
        fresh_weights.astype(jnp.bfloat16),
        fresh[:, :, 1],
        preferred_element_type=jnp.float32,
    )
    return (blended / jnp.transpose(totals, (2, 0, 1))[..., None]).astype(jnp.bfloat16)


def shards(
    prior_cache,
    prefix_length,
    slot_trace,
    queries,
    new_token_cache,
    boundaries,
    output_weight,
    reward_weight,
):
    group_index = lax.axis_index("seq")
    slot_count = queries.shape[0]
    new_len = queries.shape[1]
    lengths = prefix_length[slot_trace]
    ordered = prior_cache[slot_trace]
    own_lengths = lax.dynamic_slice_in_dim(lengths, group_index * slot_count, slot_count)
    moved = lax.all_to_all(ordered, "seq", split_axis=0, concat_axis=1, tiled=True)
    whole = lax.all_gather(moved, "pool", axis=1, tiled=True)
    attended = lax.map(attend_whole, (queries, whole, new_token_cache, own_lengths))
    token_rows = attended.reshape(slot_count * new_len, -1)
    weight_rows = output_weight.reshape(-1, output_weight.shape[-1])
    share = lax.psum_scatter(
        lax.dot_general(
            weight_rows, token_rows, (((0,), (1,)), ((), ())), preferred_element_type=jnp.float32
        ),
        ("pool", "tp"),
        scatter_dimension=0,
        tiled=True,
    )
    layer_out = jnp.transpose(share).reshape(slot_count, new_len, -1).astype(jnp.bfloat16)
    picked = jnp.take_along_axis(layer_out, boundaries[:, :, None], axis=1)
    partial_rewards = jnp.einsum("rsd,d->rs", picked.astype(jnp.float32), reward_weight)
    rewards = lax.psum(partial_rewards, ("pool", "tp"))
    return (layer_out, rewards)


def solution(mesh):
    placed = (
        P(None, ("pool", "seq"), "tp", None, None),
        P(),
        P(),
        P("seq", None, "tp", "pool", None),
        P("seq", None, "tp", None, None),
        P("seq", None),
        P("tp", "pool", None, None),
        P(("pool", "tp")),
    )
    return jax.shard_map(
        shards,
        mesh=mesh,
        in_specs=placed,
        out_specs=(P("seq", None, ("pool", "tp")), P("seq", None)),
        check_vma=False,
    )
```

profile of v0, /device:TPU:8, one launch (start us, length us, event | category | flops | bytes accessed | tf_op | source)
XLA Modules:
  0.0 479.6 jit_solution(6223805006140881517)
XLA Ops:
  7.2 0.0 copy-start
  7.2 0.0 all-gather.2.cloned.1.call-start
  7.2 0.8 compare_select_fusion.1
  8.0 0.7 copy-done
  8.8 5.9 %gather_fusion = bf16[16,256,2,128]{3,2,1,0:T(2,128)(2,1)} fusion(bf16[16,256,2,128]{3,2,1,0:T(2,128)(2,1)S(1)} %bitcast.132, s32[1024]{0:T(1024)S(1)} %pad_clamp_fusion), kind=kCustom, calls=%fused_computation | custom fusion | bytes 4194368 | tf_op jit(solution)/shard_map/gather | solution.py:57
  14.7 31.7 %all_to_all.18 = bf16[16,256,1,2,128]{4,3,1,2,0:T(2,128)(2,1)S(1)} all-to-all(bf16[16,256,1,2,128]{4,3,1,2,0:T(2,128)(2,1)} %bitcast.135), channel_id=1, replica_groups=mesh['pool'=4,'seq'=8,'tp'=8] {'seq'}, dimensions={0} | all-to-all | bytes 4194304 | tf_op jit(solution)/shard_map/all_to_all | solution.py:59
  46.4 1.9 copy.29
  48.3 0.0 all-gather.2.cloned.1.call-update
  48.3 0.0 reduce-scatter.2.cloned.1.call-start
  48.4 0.0 copy-done.1
  48.4 0.7 gather_fusion.1
  49.1 0.1 dynamic_slice.18
  49.1 86.0 %all-gather.2.cloned.1.call-done = bf16[2,8192,1,2,128]{4,1,3,2,0:T(8,128)(2,1)} async-done(((bf16[2,2048,1,2,128]{4,1,3,2,0:T(8,128)(2,1)}), bf16[2,8192,1,2,128]{4,1,3,2,0:T(8,128)(2,1)}) %all-gather.2.cloned.1.call-update) | async-done | bytes 8388624 | tf_op jit(solution)/shard_map/all_gather | solution.py:60
  135.2 0.0 copy-done.2
  135.2 0.0 copy-done.3
  135.2 25.1 %while.10 = (s32[]{:T(128)}, bf16[2,128,1,2,128]{4,3,1,0,2:T(2,128)(2,1)S(1)}, bf16[2,8192,1,2,128]{4,1,3,2,0:T(8,128)(2,1)}, s32[2]{0:T(128)S(1)}, bf16[2,128,1...) while((s32[]{:T(128)}, bf16[2,128,1,2,128]{4,3,1,0,2:T(2,128)(2,1)S(1)}, ...), condition=%wide.region_5.6_spmd, body=%wide.region_0.5_spmd.sunk | while | flops 1109810688 | bytes 39435376 | solution.py:61
  135.2 0.1 constant_dynamic-slice_fusion.3
  135.3 2.5 dynamic-slice_bitcast_fusion.2
  137.8 0.6 dynamic_slice.27
  138.3 0.7 iota_compare_fusion.4
  139.0 1.8 fusion.47
  140.9 0.2 fusion.48
  141.1 1.9 fusion.49
  142.9 4.3 fusion.50
  147.3 0.2 fusion.52
  147.5 0.1 copy.65
  147.7 0.1 constant_dynamic-update-slice_fusion.2
  147.7 0.1 constant_dynamic-slice_fusion.3
  147.8 2.5 dynamic-slice_bitcast_fusion.2
  150.3 0.6 dynamic_slice.27
  150.9 0.7 iota_compare_fusion.4
  151.6 1.8 fusion.47
  153.4 0.2 fusion.48
  153.6 1.9 fusion.49
  155.5 4.3 fusion.50
  159.9 0.2 fusion.52
  160.1 0.1 copy.65
  160.2 0.1 constant_dynamic-update-slice_fusion.2
  160.3 6.7 %convolution_bitcast_fusion = f32[8192,256]{0,1:T(8,128)} fusion(bf16[256,8192]{1,0:T(8,128)(2,1)} %bitcast.136, bf16[32,8,2,128]{3,2,1,0:T(2,128)(2,1)S(1)} %bitcast.141), kind=kOutput, calls=%fused_computation.45 | convolution fusion | flops 1073741824 | bytes 12713984 | tf_op jit(solution)/shard_map/dot_general | solution.py:65
  166.9 0.0 reduce-scatter.2.cloned.1.call-update
  167.0 0.7 copy-done.5
  167.6 0.1 reshape.111
  167.7 230.1 %reduce-scatter.2.cloned.1.call-done = f32[256,256]{0,1:T(8,128)} async-done(((f32[8192,256]{0,1:T(8,128)}), f32[256,256]{0,1:T(8,128)}) %reduce-scatter.2.cloned.1.call-update) | async-done | bytes 262160 | tf_op jit(solution)/shard_map/reduce_scatter | solution.py:64
  397.9 1.0 convert_element_type.19
  398.8 0.0 copy-start.4
  398.8 0.7 gather_fusion.2
  399.5 0.2 fusion.28
  399.7 73.0 %psum.7 = f32[2,16]{1,0:T(2,128)} all-reduce(f32[2,16]{1,0:T(2,128)S(1)} %bitcast.143), channel_id=1, replica_groups=mesh['pool'=4,'seq'=8,'tp'=8] {'pool','tp'}, use_global_device_ids=true, to_apply=%region_7.8 | all-reduce | flops 32 | bytes 256 | tf_op jit(solution)/shard_map/psum | solution.py:75
  (21 shorter events, 0.2 us)
Async XLA Ops:
  7.2 1.6 copy-start
  7.2 128.0 %all-gather.2.cloned.1.call-start = ((), (), s32[]{:S(2)}) async-start(), calls=%async_computation.2 | async-start | bytes 10485760 | tf_op jit(solution)/shard_map/all_gather | solution.py:60
  46.4 2.0 copy-start.1
  46.4 88.8 %copy-start.2 = (bf16[2,128,1,2,128]{4,3,2,1,0:T(2,128)(2,1)S(1)}, bf16[2,128,1,2,128]{4,3,2,1,0:T(2,128)(2,1)}, u32[]{:S(2)}) copy-start(bf16[2,128,1,2,128]{4,3,2,1,0:T(2,128)(2,1)} %param.13) | copy-start | bytes 393220
  46.4 88.8 %copy-start.3 = (bf16[2,128,1,2,128]{4,3,2,1,0:T(2,128)(2,1)S(1)}, bf16[2,128,1,2,128]{4,3,2,1,0:T(2,128)(2,1)}, u32[]{:S(2)}) copy-start(bf16[2,128,1,2,128]{4,3,2,1,0:T(2,128)(2,1)} %param.14) | copy-start | bytes 393220
  48.3 349.5 %reduce-scatter.2.cloned.1.call-start = ((), (), s32[]{:S(2)}) async-start(), calls=%async_computation.3 | async-start | bytes 8650752 | tf_op jit(solution)/shard_map/reduce_scatter | solution.py:64
  166.9 0.7 copy-start.5
  166.9 232.6 %copy-start.6 = (f32[256]{0:T(256)S(1)}, f32[256]{0:T(256)}, u32[]{:S(2)}) copy-start(f32[256]{0:T(256)} %param.17) | copy-start | bytes 3076
  398.8 73.9 %copy-start.4 = (bf16[256,256]{0,1:T(8,128)(2,1)}, bf16[256,256]{0,1:T(8,128)(2,1)S(1)}, u32[]{:S(2)}) copy-start(bf16[256,256]{0,1:T(8,128)(2,1)S(1)} %convert_element_type.19) | copy-start | bytes 393220
Sparse Core Ops, SparseCore 0:
  48.5 86.6 all-gather.1
  167.1 230.7 reduce-scatter.1
where the time goes:
time: 480 us
  waiting for transfers between devices  316 us (66%)
  blocking collectives  105 us (22%)
  local copies, waits for them, and re-layouts  17.4 us (4%)
  matrix products  15 us (3%)
  between operations  14.1 us (3%)
  other arithmetic  11.9 us (2%)
    reduce_scatter x1, waiting for transfers between devices, shards(): lax.psum_scatter(lax.dot_general(weight_rows, token_rows, (((0,), (1,)),...  230 us
    all_gather x1, waiting for transfers between devices, shards(): whole = lax.all_gather(moved, 'pool', axis=1, tiled=True)  86 us
    psum x1, blocking collectives, shards(): rewards = lax.psum(partial_rewards, ('pool', 'tp'))  73 us
    all_to_all x1, blocking collectives, shards(): lax.all_to_all(ordered, 'seq', split_axis=0, concat_axis=1, tiled=True)  31.7 us
  transfers between devices with their start and end apart: 2, of which 2 were waited for; matrix products, arithmetic and copies ran while one was open for 0% of the time, Pallas kernels for 0%

commit v1 on v0

v1 whole, which is shorter than its diff:
```python
import functools

import jax
import jax.numpy as jnp
from jax import lax
from jax.experimental import pallas as pl
from jax.experimental.pallas import tpu as pltpu
from jax.sharding import PartitionSpec as P

negative_fill = -1e30
peak_floor = -1e25
log2_e = 1.4426950408889634
VMEM = pl.BlockSpec(memory_space=pltpu.VMEM)
SMEM = pl.BlockSpec(memory_space=pltpu.SMEM)
ANY = pl.BlockSpec(memory_space=pl.ANY)
STAT_ROWS = 16


def kernel_params(mib):
    return pltpu.CompilerParams(vmem_limit_bytes=mib * 1024 * 1024)


def order_kernel(order_ref, cache_ref, *refs):
    outs, (held, wide, sems) = refs[:-3], refs[-3:]
    blocks, rows = held.shape[0], held.shape[1]
    per_part = blocks // len(outs)
    copies = [
        pltpu.make_async_copy(cache_ref.at[order_ref[n]], held.at[n], sems.at[n])
        for n in range(blocks)
    ]
    for copy in copies:
        copy.start()
    for n, copy in enumerate(copies):
        copy.wait()
        wide[...] = held[n].astype(jnp.float32)
        out = outs[n // per_part]
        for kind in range(2):
            out[n % per_part, kind] = wide[pl.ds(kind, rows // 2, stride=2), :].astype(jnp.bfloat16)


def order_blocks(prior_rows, order, parts):
    blocks, rows, size = prior_rows.shape
    return pl.pallas_call(
        order_kernel,
        out_shape=[
            jax.ShapeDtypeStruct((blocks // parts, 2, rows // 2, size), jnp.bfloat16)
            for _ in range(parts)
        ],
        in_specs=[SMEM, ANY],
        out_specs=[VMEM] * parts,
        scratch_shapes=[
            pltpu.VMEM((blocks, rows, size), jnp.bfloat16),
            pltpu.VMEM((rows, size), jnp.float32),
            pltpu.SemaphoreType.DMA((blocks,)),
        ],
        compiler_params=kernel_params(16),
    )(order, prior_rows)


def attend_kernel(info_ref, q0, q1, q2, q3, prior_ref, fresh_ref, p0, p1, p2, p3):
    valid = info_ref[0]
    sources, _, block, size = prior_ref.shape
    width = sources * block
    factor = size**-0.5 * log2_e
    keys = prior_ref[:, 0].reshape(width, size)
    values = prior_ref[:, 1].reshape(width, size)
    rows = q0.shape[0]
    usable = lax.broadcasted_iota(jnp.int32, (1, width), 1) < valid
    contract = (((1,), (1,)), ((), ()))
    for tile, (query, pay) in enumerate(((q0, p0), (q1, p1), (q2, p2), (q3, p3))):
        scores = lax.dot_general(query[...], keys, contract, preferred_element_type=jnp.float32)
        scores = jnp.where(usable, scores, negative_fill)
        peak = jnp.max(scores, -1, keepdims=True)
        if tile == 0:
            fresh_scores = lax.dot_general(
                query[...], fresh_ref[0], contract, preferred_element_type=jnp.float32
            )
            new_len = fresh_scores.shape[1]
            token = lax.rem(lax.broadcasted_iota(jnp.int32, fresh_scores.shape, 0), new_len)
            causal = lax.broadcasted_iota(jnp.int32, fresh_scores.shape, 1) <= token
            fresh_scores = jnp.where(causal, fresh_scores, negative_fill)
            peak = jnp.maximum(peak, jnp.max(fresh_scores, -1, keepdims=True))
        peak = jnp.maximum(peak * factor, peak_floor).astype(jnp.bfloat16).astype(jnp.float32)
        weights = jnp.exp2(scores * factor - peak)
        total = jnp.sum(weights, -1, keepdims=True)
        blended = jnp.dot(
            weights.astype(jnp.bfloat16), values, preferred_element_type=jnp.float32
        )
        if tile == 0:
            fresh_weights = jnp.exp2(fresh_scores * factor - peak)
            total = total + jnp.sum(fresh_weights, -1, keepdims=True)
            blended = blended + jnp.dot(
                fresh_weights.astype(jnp.bfloat16), fresh_ref[1], preferred_element_type=jnp.float32
            )
        pay[pl.ds(0, rows), :] = blended.astype(jnp.bfloat16)
        high = total.astype(jnp.bfloat16).astype(jnp.float32)
        low = total - high
        lane = lax.broadcasted_iota(jnp.int32, (rows, size), 1)
        stats = jnp.where(lane == 0, peak, jnp.where(lane == 1, high, jnp.where(lane == 2, low, 0.0)))
        halves = [stats[at : at + size].T[:8] for at in range(0, rows, size)]
        pay[pl.ds(rows, 8 * len(halves)), :] = jnp.concatenate(halves, 0).astype(jnp.bfloat16)


def attend(valid, queried, prior, fresh):
    rows, size = queried[0].shape
    pay = jax.ShapeDtypeStruct((rows + STAT_ROWS, size), jnp.bfloat16)
    return pl.pallas_call(
        attend_kernel,
        out_shape=[pay] * 4,
        in_specs=[SMEM] + [VMEM] * 6,
        out_specs=[VMEM] * 4,
        compiler_params=kernel_params(48),
    )(valid, *queried, prior, fresh)


def merge_kernel(p0, p1, p2, p3, out_ref):
    rows, size = out_ref.shape
    peaks, totals = [], []
    for pay in (p0, p1, p2, p3):
        stats = pay[pl.ds(rows, STAT_ROWS), :].astype(jnp.float32)
        columns = [
            jnp.concatenate([stats[8 * n : 8 * n + 8]] * (size // 8), 0).T
            for n in range(rows // size)
        ]
        columns = jnp.concatenate(columns, 0)
        peaks.append(columns[:, 0:1])
        totals.append(columns[:, 1:2] + columns[:, 2:3])
    top = functools.reduce(jnp.maximum, peaks)
    shares = [jnp.exp2(peak - top) for peak in peaks]
    total = sum(share * part for share, part in zip(shares, totals))
    blended = sum(
        share * pay[pl.ds(0, rows), :].astype(jnp.float32)
        for share, pay in zip(shares, (p0, p1, p2, p3))
    )
    out_ref[...] = (blended / total).astype(jnp.bfloat16)


def merge(pays):
    rows, size = pays[0].shape
    return pl.pallas_call(
        merge_kernel,
        out_shape=jax.ShapeDtypeStruct((rows - STAT_ROWS, size), jnp.bfloat16),
        in_specs=[VMEM] * 4,
        out_specs=VMEM,
        compiler_params=kernel_params(16),
    )(*pays)


def project_kernel(core_ref, *refs):
    attended, weights, out_ref = refs[:4], refs[4:12], refs[12]
    core = core_ref[0]
    tokens, wide = out_ref.shape[1], out_ref.shape[2]
    firsts = [ref[pl.ds(pl.multiple_of(core * tokens, tokens), tokens), :] for ref in attended]
    seconds = [ref[pl.ds(pl.multiple_of((1 - core) * tokens, tokens), tokens), :] for ref in attended]
    for dest in range(out_ref.shape[0]):
        at = pl.ds(dest * wide, wide)
        total = jnp.zeros((tokens, wide), jnp.float32)
        for n in range(4):
            total += jnp.dot(firsts[n], weights[2 * n][:, at], preferred_element_type=jnp.float32)
            total += jnp.dot(
                seconds[n], weights[2 * n + 1][:, at], preferred_element_type=jnp.float32
            )
        out_ref[dest] = total.astype(jnp.bfloat16)


def project(core, attended, weights, dests):
    rows, size = attended[0].shape
    columns = weights[0].shape[1]
    return pl.pallas_call(
        project_kernel,
        out_shape=jax.ShapeDtypeStruct((dests, rows // 2, columns // dests), jnp.bfloat16),
        in_specs=[SMEM] + [VMEM] * 12,
        out_specs=VMEM,
        compiler_params=kernel_params(32),
    )(core, *attended, *weights)


def shards(
    prior_cache,
    prefix_length,
    slot_trace,
    queries,
    new_token_cache,
    boundaries,
    output_weight,
    reward_weight,
):
    pool, seq, tp = lax.axis_index("pool"), lax.axis_index("seq"), lax.axis_index("tp")
    pools, seqs, tps = lax.axis_size("pool"), lax.axis_size("seq"), lax.axis_size("tp")
    slots, new_len, _, pair, size = queries.shape
    traces, block = prior_cache.shape[:2]
    core = lax.rem(seq, 2)
    core_arg = core.reshape(1).astype(jnp.int32)

    def from_pool(array, offset):
        return lax.ppermute(array, "pool", [((n + offset) % pools, n) for n in range(pools)])

    def swap_core(array):
        return lax.ppermute(array, "seq", [(n, n ^ 1) for n in range(seqs)])

    own_queries = jnp.transpose(queries[:, :, 0], (0, 2, 1, 3)).reshape(slots, pair * new_len, size)
    queried = [own_queries] + [from_pool(own_queries, o) for o in range(1, pools)]

    order = slot_trace.reshape(seqs, slots).T.reshape(-1)
    ordered = order_blocks(prior_cache.reshape(traces, 2 * block, size), order, slots)
    priors = [lax.all_to_all(part, "seq", split_axis=0, concat_axis=0, tiled=True) for part in ordered]

    rows_all = output_weight.reshape(pair * size, -1)
    columns = rows_all.shape[1] // pools

    def weight_block(half, column_block):
        return lax.dynamic_slice(rows_all, (half * size, column_block * columns), (size, columns))

    weights = [weight_block(core, pool), weight_block(1 - core, pool)]
    for o in range(1, pools):
        got = from_pool(weight_block(core, lax.rem(pool + pools - o, pools)), o)
        weights += [got, swap_core(got)]

    lengths = prefix_length[slot_trace]
    fresh = jnp.transpose(new_token_cache[:, :, 0], (0, 2, 1, 3))
    outs = []
    for slot in range(slots):
        length = lax.dynamic_slice(lengths, (seq * slots + slot,), (1,))
        valid = length - pool * seqs * block
        pays = attend(valid, [q[slot] for q in queried], priors[slot], fresh[slot])
        pays = [pays[0]] + [
            lax.ppermute(pays[o], "pool", [(n, (n + o) % pools) for n in range(pools)])
            for o in range(1, pools)
        ]
        attended = merge(pays)
        everyone = [attended] + [from_pool(attended, o) for o in range(1, pools)]
        partial = project(core_arg, everyone, weights, tps)
        arrived = lax.all_to_all(partial, "tp", split_axis=0, concat_axis=0, tiled=True)
        outs.append(jnp.sum(arrived.astype(jnp.float32), 0).astype(jnp.bfloat16))
    layer_out = jnp.stack(outs)
    picked = jnp.take_along_axis(layer_out, boundaries[:, :, None], axis=1)
    partial_rewards = jnp.sum(picked.astype(jnp.float32) * reward_weight, -1)
    spread = jnp.broadcast_to(partial_rewards, (pools * tps,) + partial_rewards.shape)
    rewards = jnp.sum(
        lax.all_to_all(spread, ("pool", "tp"), split_axis=0, concat_axis=0, tiled=True), 0
    )
    return (layer_out, rewards)


def solution(mesh):
    placed = (
        P(None, ("pool", "seq"), "tp", None, None),
        P(),
        P(),
        P("seq", None, "tp", "pool", None),
        P("seq", None, "tp", None, None),
        P("seq", None),
        P("tp", "pool", None, None),
        P(("pool", "tp")),
    )
    return jax.shard_map(
        shards,
        mesh=mesh,
        in_specs=placed,
        out_specs=(P("seq", None, ("pool", "tp")), P("seq", None)),
        check_vma=False,
    )
```

time: 480 us -> 155 us (0.32)
  waiting for transfers between devices: 316 us -> 46.4 us
  blocking collectives: 105 us -> 13 us
  starting transfers between devices: 0.08 us -> 52.1 us
  Pallas kernels: 0 us -> 20.5 us
  matrix products: 15 us -> 0 us
  between operations: 14.1 us -> 1.98 us
  other arithmetic: 11.9 us -> 1.99 us
    reduce_scatter x1 -> x0, waiting for transfers between devices: 230 us -> none  [shards(): lax.psum_scatter(lax.dot_general(weight_rows, token_rows, (((0,), (1,)),...]
    all_gather x1 -> x0, waiting for transfers between devices: 86 us -> none  [shards(): whole = lax.all_gather(moved, 'pool', axis=1, tiled=True)]
    psum x1 -> x0, blocking collectives: 73 us -> none  [shards(): rewards = lax.psum(partial_rewards, ('pool', 'tp'))]
    ppermute x0 -> x21, waiting for transfers between devices: none -> 27 us  [the longest x12 16.8 us: from_pool(): lax.ppermute(array, 'pool', [((n + offset) % pools, n) for n in range(poo...]
    all_to_all x0 -> x4, starting transfers between devices: none -> 26.2 us  [the longest x2 16.3 us: shards(): lax.all_to_all(partial, 'tp', split_axis=0, concat_axis=0, tiled=True)]
    ppermute x0 -> x21, starting transfers between devices: none -> 25.8 us  [the longest x12 16.6 us: from_pool(): lax.ppermute(array, 'pool', [((n + offset) % pools, n) for n in range(poo...]
    pallas_call x0 -> x7, Pallas kernels: none -> 20.5 us  [the longest x2 7.38 us: attend(): pl.pallas_call(attend_kernel, out_shape=[pay] * 4, in_specs=[SMEM] + [VME...]
    all_to_all x0 -> x4, waiting for transfers between devices: none -> 19.4 us  [the longest x2 12.1 us: shards(): lax.all_to_all(partial, 'tp', split_axis=0, concat_axis=0, tiled=True)]
  transfers between devices with their start and end apart: 2 -> 25, of which waited for: 2 -> 17; matrix products, arithmetic and copies ran while one was open for 0% -> 6% of each run, Pallas kernels for 0% -> 13%
where the time goes in v1:
time: 155 us; the launch traced here: 154 us
  starting transfers between devices  52.1 us (34%)
  waiting for transfers between devices  46.4 us (30%)
  Pallas kernels  20.5 us (13%)
  local copies, waits for them, and re-layouts  18.1 us (12%)
  blocking collectives  13 us (8%)
  other arithmetic  1.99 us (1%)
  between operations  1.98 us (1%)
    ppermute x12, waiting for transfers between devices, from_pool(): lax.ppermute(array, 'pool', [((n + offset) % pools, n) for n in range(poo...  16.8 us
    ppermute x12, starting transfers between devices, from_pool(): lax.ppermute(array, 'pool', [((n + offset) % pools, n) for n in range(poo...  16.6 us
    all_to_all x2, starting transfers between devices, shards(): lax.all_to_all(partial, 'tp', split_axis=0, concat_axis=0, tiled=True)  16.3 us
    all_to_all x1, blocking collectives, shards(): lax.all_to_all(spread, ('pool', 'tp'), split_axis=0, concat_axis=0, tiled...  13 us
    all_to_all x2, waiting for transfers between devices, shards(): lax.all_to_all(partial, 'tp', split_axis=0, concat_axis=0, tiled=True)  12.1 us
    ppermute x6, waiting for transfers between devices, shards(): lax.ppermute(pays[o], 'pool', [(n, (n + o) % pools) for n in range(pools)])  10.2 us
    all_to_all x2, starting transfers between devices, shards(): lax.all_to_all(part, 'seq', split_axis=0, concat_axis=0, tiled=True)  9.97 us
    ppermute x6, starting transfers between devices, shards(): lax.ppermute(pays[o], 'pool', [(n, (n + o) % pools) for n in range(pools)])  8.73 us
  transfers between devices with their start and end apart: 25, of which 17 were waited for; matrix products, arithmetic and copies ran while one was open for 6% of the time, Pallas kernels for 13%

profile of v1, /device:TPU:8, one launch (start us, length us, event | category | flops | bytes accessed | tf_op | source)
XLA Modules:
  0.0 154.1 jit_solution(7342887173439009107)
XLA Ops:
  0.6 1.6 %copy.26 = bf16[2,2,128,128]{3,2,1,0:T(8,128)(2,1)} copy(bf16[2,2,128,128]{3,1,2,0:T(2,128)(2,1)} %bitcast.43) | data formatting | bytes 262144 | tf_op jit(solution)/shard_map/transpose | solution.py:201
  2.2 1.5 collective-permute-start.2
  3.7 2.7 %collective-permute-start.1 = (bf16[2,256,128]{2,1,0:T(8,128)(2,1)}, bf16[2,256,128]{2,1,0:T(8,128)(2,1)}, u32[]{:S(2)}, u32[]{:S(2)}) collective-permute-start(bf16[2,256,128]{2,1,0:T(8,128)(2,1)} %bitcast.6), channel_id=1, source_target_pairs={{128,0},{192,64},{0,128},{64,192},{129,1},{193,65},{1,129},{65,193... | collective-permute-start | bytes 393224 | tf_op jit(solution)/shard_map/ppermute | solution.py:196
  7.4 1.6 %copy-done.7 = bf16[16,256,1,2,128]{4,3,2,1,0:T(2,128)(2,1)S(1)} copy-done((bf16[16,256,1,2,128]{4,3,2,1,0:T(2,128)(2,1)S(1)}, bf16[16,256,1,2,128]{4,3,2,1,0:T(2,128)(2,1)}, u32[]{:S(2)}) %copy-start.7) | copy-done | bytes 2097176
  8.9 4.9 %shard_map.95 = (bf16[8,2,256,128]{3,2,1,0:T(8,128)(2,1)}, bf16[8,2,256,128]{3,2,1,0:T(8,128)(2,1)S(1)}) custom-call(s32[16]{0:T(128)S(1)} %reshape.38.order_ref, bf16[16,512,128]{2,1,0:T(8,128)(2,1)S(1)} %bitcast.39), custom_call_target="tpu_custom_call" | custom-call | tf_op jit(solution)/shard_map/pallas_call | solution.py:43
  13.9 1.0 copy-done.8
  14.9 5.0 %all-to-all-start = ((bf16[8,2,256,128]{3,2,1,0:T(8,128)(2,1)}), bf16[8,2,256,128]{3,2,1,0:T(8,128)(2,1)S(1)}, u32[]{:S(2)}, u32[]{:S(2)}) async-start(bf16[8,2,256,128]{3,2,1,0:T(8,128)(2,1)} %get-tuple-element.12), calls=%async_computation | async-start | bytes 2097152 | tf_op jit(solution)/shard_map/all_to_all | solution.py:206
  19.9 2.9 %fusion = (bf16[128,2048]{1,0:T(8,128)(2,1)}, bf16[128,2048]{1,0:T(8,128)(2,1)}, bf16[128,2048]{1,0:T(8,128)(2,1)}, bf16[128,2048]{1,0:T(8,128)(2,1)S(1)}, bf16[128,2048]{1,0:T(8,128)(2,1)S(1)}) fusion(bf16[256,8192]{1,0:T(8,128)(2,1)} %bitcast.42, s32[]{:T(128)S(6)} %select_n.44, s32[]{:T(128)S(6)} %select_n.49, s32[]{:T(128)S(6)} %select_n.48, ...), kind=kLoop, calls=%fused_computation.18 | loop fusion | bytes 5242904 | tf_op jit(solution)/shard_map/dynamic_slice | solution.py:212
  23.4 2.3 %collective-permute-start.11 = (bf16[128,2048]{1,0:T(8,128)(2,1)}, bf16[128,2048]{1,0:T(8,128)(2,1)}, u32[]{:S(2)}, u32[]{:S(2)}) collective-permute-start(bf16[128,2048]{1,0:T(8,128)(2,1)} %get-tuple-element.23), channel_id=1, source_target_pairs={{128,0},{192,64},{0,128},{64,192},{129,1},{193,65},{1,129},{65,193... | collective-permute-start | bytes 1572872 | tf_op jit(solution)/shard_map/ppermute | solution.py:196
  27.1 7.4 %all-to-all-done.prior_ref = bf16[8,2,256,128]{3,2,1,0:T(8,128)(2,1)S(1)} async-done(((bf16[8,2,256,128]{3,2,1,0:T(8,128)(2,1)}), bf16[8,2,256,128]{3,2,1,0:T(8,128)(2,1)S(1)}, u32[]{:S(2)}, u32[]{:S(2)}) %all-to-all-start) | async-done | bytes 1048608 | tf_op jit(solution)/shard_map/all_to_all | solution.py:206
  34.4 4.9 %all-to-all-start.2 = ((bf16[8,2,256,128]{3,2,1,0:T(8,128)(2,1)}), bf16[8,2,256,128]{3,2,1,0:T(8,128)(2,1)S(1)}, u32[]{:S(2)}, u32[]{:S(2)}) async-start(bf16[8,2,256,128]{3,2,1,0:T(8,128)(2,1)} %copy-done.8), calls=%async_computation.2 | async-start | bytes 2097152 | tf_op jit(solution)/shard_map/all_to_all | solution.py:206
  41.2 1.5 collective-permute-start
  42.7 6.8 %collective-permute-done.13.refs_10_ = bf16[128,2048]{1,0:T(8,128)(2,1)} collective-permute-done((bf16[128,2048]{1,0:T(8,128)(2,1)}, bf16[128,2048]{1,0:T(8,128)(2,1)}, u32[]{:S(2)}, u32[]{:S(2)}) %collective-permute-start.13) | collective-permute-done | bytes 524320 | tf_op jit(solution)/shard_map/ppermute | solution.py:196
  50.1 1.2 collective-permute-done.9.refs_6_
  51.3 0.9 slice_bitcast_fusion.6
  52.9 3.7 %shard_map.96 = (bf16[272,128]{1,0:T(8,128)(2,1)S(1)}, bf16[272,128]{1,0:T(8,128)(2,1)S(1)}, bf16[272,128]{1,0:T(8,128)(2,1)S(1)}, bf16[272,128]{1,0:T(8,128)(2,1)S(1)}) custom-call(s32[1]{0:T(128)S(6)} %sub.23.info_ref, bf16[256,128]{1,0:T(8,128)(2,1)S(1)} %bitcast.40, bf16[256,128]{1,0:T(8,128)(2,1)S(1)} %get-tuple-element.33.q1, ...), custom_call_target="tpu_custom_call" | custom-call | tf_op jit(solution)/shard_map/pallas_call | solution.py:107
  56.9 3.6 %collective-permute-start.4 = (bf16[272,128]{1,0:T(8,128)(2,1)S(1)}, bf16[272,128]{1,0:T(8,128)(2,1)S(1)}, u32[]{:S(2)}, u32[]{:S(2)}) collective-permute-start(bf16[272,128]{1,0:T(8,128)(2,1)S(1)} %get-tuple-element.15), channel_id=1, source_target_pairs={{0,128},{64,192},{128,0},{192,64},{1,129},{65,193},{129,1},{193,65... | collective-permute-start | bytes 208904 | tf_op jit(solution)/shard_map/ppermute | solution.py:227
  60.5 2.4 %collective-permute-done.3.p1 = bf16[272,128]{1,0:T(8,128)(2,1)S(1)} collective-permute-done((bf16[272,128]{1,0:T(8,128)(2,1)S(1)}, bf16[272,128]{1,0:T(8,128)(2,1)S(1)}, u32[]{:S(2)}, u32[]{:S(2)}) %collective-permute-start.3) | collective-permute-done | bytes 69664 | tf_op jit(solution)/shard_map/ppermute | solution.py:227
  63.8 3.5 %collective-permute-done.5.p3 = bf16[272,128]{1,0:T(8,128)(2,1)S(1)} collective-permute-done((bf16[272,128]{1,0:T(8,128)(2,1)S(1)}, bf16[272,128]{1,0:T(8,128)(2,1)S(1)}, u32[]{:S(2)}, u32[]{:S(2)}) %collective-permute-start.5) | collective-permute-done | bytes 69664 | tf_op jit(solution)/shard_map/ppermute | solution.py:227
  68.0 3.3 %collective-permute-start.7 = (bf16[256,128]{1,0:T(8,128)(2,1)S(1)}, bf16[256,128]{1,0:T(8,128)(2,1)S(1)}, u32[]{:S(2)}, u32[]{:S(2)}) collective-permute-start(bf16[256,128]{1,0:T(8,128)(2,1)S(1)} %shard_map.97.refs_0_), channel_id=1, source_target_pairs={{128,0},{192,64},{0,128},{64,192},{129,1},{193,65},{1,129},{65,193... | collective-permute-start | bytes 196616 | tf_op jit(solution)/shard_map/ppermute | solution.py:196
  71.4 2.1 %collective-permute-done.8.refs_3_ = bf16[256,128]{1,0:T(8,128)(2,1)S(1)} collective-permute-done((bf16[256,128]{1,0:T(8,128)(2,1)S(1)}, bf16[256,128]{1,0:T(8,128)(2,1)S(1)}, u32[]{:S(2)}, u32[]{:S(2)}) %collective-permute-start.8) | collective-permute-done | bytes 65568 | tf_op jit(solution)/shard_map/ppermute | solution.py:196
  73.5 0.8 collective-permute-done.7.refs_2_
  74.3 1.3 collective-permute-done.6.refs_1_
  75.6 3.4 %shard_map.98 = bf16[8,128,256]{2,1,0:T(8,128)(2,1)} custom-call(s32[1]{0:T(128)} %bitcast.core_ref, bf16[256,128]{1,0:T(8,128)(2,1)S(1)} %shard_map.97.refs_0_, bf16[256,128]{1,0:T(8,128)(2,1)S(1)} %collective-permute-done.6.refs_1_, bf16[256,128]{1,0:T(8,128)(2,1)S(1)} %collective-permute-done.7.refs_2_, ...), custom_call_target="tpu_custom_call" | custom-call | tf_op jit(solution)/shard_map/pallas_call | solution.py:169
  79.0 0.8 copy-done.1
  79.9 0.8 copy-done.3
  80.7 0.8 copy-done.5
  81.5 8.4 %all-to-all-start.1 = ((bf16[8,128,256]{2,1,0:T(8,128)(2,1)}), bf16[8,128,256]{2,1,0:T(8,128)(2,1)}, u32[]{:S(2)}, u32[]{:S(2)}) async-start(bf16[8,128,256]{2,1,0:T(8,128)(2,1)} %shard_map.98), calls=%async_computation.1 | async-start | bytes 1048576 | tf_op jit(solution)/shard_map/all_to_all | solution.py:233
  90.4 0.9 copy.29
  91.3 3.7 %shard_map.99 = (bf16[272,128]{1,0:T(8,128)(2,1)S(1)}, bf16[272,128]{1,0:T(8,128)(2,1)S(1)}, bf16[272,128]{1,0:T(8,128)(2,1)S(1)}, bf16[272,128]{1,0:T(8,128)(2,1)S(1)}) custom-call(s32[1]{0:T(128)S(6)} %sub.28.info_ref, bf16[256,128]{1,0:T(8,128)(2,1)S(1)} %bitcast.41, bf16[256,128]{1,0:T(8,128)(2,1)S(1)} %get-tuple-element.34.q1, ...), custom_call_target="tpu_custom_call" | custom-call | tf_op jit(solution)/shard_map/pallas_call | solution.py:107
  95.0 0.9 collective-permute-start.15
  95.9 2.5 %collective-permute-start.16 = (bf16[272,128]{1,0:T(8,128)(2,1)S(1)}, bf16[272,128]{1,0:T(8,128)(2,1)S(1)}, u32[]{:S(2)}, u32[]{:S(2)}) collective-permute-start(bf16[272,128]{1,0:T(8,128)(2,1)S(1)} %get-tuple-element.20), channel_id=1, source_target_pairs={{0,128},{64,192},{128,0},{192,64},{1,129},{65,193},{129,1},{193,65... | collective-permute-start | bytes 208904 | tf_op jit(solution)/shard_map/ppermute | solution.py:227
  99.2 1.4 collective-permute-done.15.p1
  100.6 1.2 collective-permute-done.16.p2
  101.7 1.6 %collective-permute-done.17.p3 = bf16[272,128]{1,0:T(8,128)(2,1)S(1)} collective-permute-done((bf16[272,128]{1,0:T(8,128)(2,1)S(1)}, bf16[272,128]{1,0:T(8,128)(2,1)S(1)}, u32[]{:S(2)}, u32[]{:S(2)}) %collective-permute-start.17) | collective-permute-done | bytes 69664 | tf_op jit(solution)/shard_map/ppermute | solution.py:227
  104.0 1.2 collective-permute-start.20
  105.2 2.3 %collective-permute-start.19 = (bf16[256,128]{1,0:T(8,128)(2,1)S(1)}, bf16[256,128]{1,0:T(8,128)(2,1)S(1)}, u32[]{:S(2)}, u32[]{:S(2)}) collective-permute-start(bf16[256,128]{1,0:T(8,128)(2,1)S(1)} %shard_map.100.refs_0_), channel_id=1, source_target_pairs={{128,0},{192,64},{0,128},{64,192},{129,1},{193,65},{1,129},{65,193... | collective-permute-start | bytes 196616 | tf_op jit(solution)/shard_map/ppermute | solution.py:196
  108.0 1.6 %collective-permute-done.20.refs_3_ = bf16[256,128]{1,0:T(8,128)(2,1)S(1)} collective-permute-done((bf16[256,128]{1,0:T(8,128)(2,1)S(1)}, bf16[256,128]{1,0:T(8,128)(2,1)S(1)}, u32[]{:S(2)}, u32[]{:S(2)}) %collective-permute-start.20) | collective-permute-done | bytes 65568 | tf_op jit(solution)/shard_map/ppermute | solution.py:196
  109.6 1.4 collective-permute-done.19.refs_2_
  111.0 0.8 collective-permute-done.18.refs_1_
  111.8 1.0 copy-done.2
  112.8 1.0 copy-done.4
  113.9 1.0 copy-done.6
  114.9 3.4 %shard_map.101 = bf16[8,128,256]{2,1,0:T(8,128)(2,1)} custom-call(s32[1]{0:T(128)} %bitcast.core_ref, bf16[256,128]{1,0:T(8,128)(2,1)S(1)} %shard_map.100.refs_0_, bf16[256,128]{1,0:T(8,128)(2,1)S(1)} %collective-permute-done.18.refs_1_, bf16[256,128]{1,0:T(8,128)(2,1)S(1)} %collective-permute-done.19.refs_2_, ...), custom_call_target="tpu_custom_call" | custom-call | tf_op jit(solution)/shard_map/pallas_call | solution.py:169
  118.3 7.9 %all-to-all-start.3 = ((bf16[8,128,256]{2,1,0:T(8,128)(2,1)}), bf16[8,128,256]{2,1,0:T(8,128)(2,1)S(1)}, u32[]{:S(2)}, u32[]{:S(2)}) async-start(bf16[8,128,256]{2,1,0:T(8,128)(2,1)} %shard_map.101), calls=%async_computation.3 | async-start | bytes 1048576 | tf_op jit(solution)/shard_map/all_to_all | solution.py:233
  126.3 1.1 reduce_sum.42
  127.4 12.1 %all-to-all-done.3 = bf16[8,128,256]{2,1,0:T(8,128)(2,1)S(1)} async-done(((bf16[8,128,256]{2,1,0:T(8,128)(2,1)}), bf16[8,128,256]{2,1,0:T(8,128)(2,1)S(1)}, u32[]{:S(2)}, u32[]{:S(2)}) %all-to-all-start.3) | async-done | bytes 524320 | tf_op jit(solution)/shard_map/all_to_all | solution.py:233
  140.5 13.0 %all_to_all.25 = f32[32,2,16]{2,1,0:T(2,128)S(1)} all-to-all(f32[32,2,16]{2,1,0:T(2,128)S(1)} %broadcast_in_dim.19), channel_id=1, replica_groups=mesh['pool'=4,'seq'=8,'tp'=8] {'pool','tp'}, dimensions={0} | all-to-all | bytes 8192 | tf_op jit(solution)/shard_map/all_to_all | solution.py:240
  (67 shorter events, 11.0 us)
Async XLA Ops:
  0.6 38.7 %copy-start = (s32[16]{0:T(128)S(1)}, s32[16]{0:T(128)}, u32[]{:S(2)}) copy-start(s32[16]{0:T(128)} %param.9) | copy-start | bytes 196
  2.2 39.0 %collective-permute-start.2 = (bf16[2,256,128]{2,1,0:T(8,128)(2,1)}, bf16[2,256,128]{2,1,0:T(8,128)(2,1)S(1)}, u32[]{:S(2)}, u32[]{:S(2)}) collective-permute-start(bf16[2,256,128]{2,1,0:T(8,128)(2,1)} %bitcast.6), channel_id=1, source_target_pairs={{192,0},{0,64},{64,128},{128,192},{193,1},{1,65},{65,129},{129,193... | collective-permute-start | bytes 393224 | tf_op jit(solution)/shard_map/ppermute | solution.py:196
  3.7 47.5 %collective-permute-start.1 = (bf16[2,256,128]{2,1,0:T(8,128)(2,1)}, bf16[2,256,128]{2,1,0:T(8,128)(2,1)}, u32[]{:S(2)}, u32[]{:S(2)}) collective-permute-start(bf16[2,256,128]{2,1,0:T(8,128)(2,1)} %bitcast.6), channel_id=1, source_target_pairs={{128,0},{192,64},{0,128},{64,192},{129,1},{193,65},{1,129},{65,193... | collective-permute-start | bytes 393224 | tf_op jit(solution)/shard_map/ppermute | solution.py:196
  7.3 1.6 %copy-start.7 = (bf16[16,256,1,2,128]{4,3,2,1,0:T(2,128)(2,1)S(1)}, bf16[16,256,1,2,128]{4,3,2,1,0:T(2,128)(2,1)}, u32[]{:S(2)}) copy-start(bf16[16,256,1,2,128]{4,3,2,1,0:T(2,128)(2,1)} %param.8) | copy-start | bytes 6291460
  13.9 1.0 copy-start.8
  14.9 11.4 %copy-start.11 = (bf16[2,128,1,2,128]{4,3,2,1,0:T(2,128)(2,1)S(1)}, bf16[2,128,1,2,128]{4,3,2,1,0:T(2,128)(2,1)}, u32[]{:S(2)}) copy-start(bf16[2,128,1,2,128]{4,3,2,1,0:T(2,128)(2,1)} %param.12) | copy-start | bytes 393220
  14.9 11.4 %copy-start.10 = (bf16[2,128,1,2,128]{4,3,2,1,0:T(2,128)(2,1)S(1)}, bf16[2,128,1,2,128]{4,3,2,1,0:T(2,128)(2,1)}, u32[]{:S(2)}) copy-start(bf16[2,128,1,2,128]{4,3,2,1,0:T(2,128)(2,1)} %param.11) | copy-start | bytes 393220
  14.9 12.2 %copy-start.14 = (s32[16]{0:T(128)S(1)}, s32[16]{0:T(128)}, u32[]{:S(2)}) copy-start(s32[16]{0:T(128)} %param.10) | copy-start | bytes 196
  14.9 19.6 %all-to-all-start = ((bf16[8,2,256,128]{3,2,1,0:T(8,128)(2,1)}), bf16[8,2,256,128]{3,2,1,0:T(8,128)(2,1)S(1)}, u32[]{:S(2)}, u32[]{:S(2)}) async-start(bf16[8,2,256,128]{3,2,1,0:T(8,128)(2,1)} %get-tuple-element.12), calls=%async_computation | async-start | bytes 2097152 | tf_op jit(solution)/shard_map/all_to_all | solution.py:206
  22.8 26.7 %collective-permute-start.13 = (bf16[128,2048]{1,0:T(8,128)(2,1)}, bf16[128,2048]{1,0:T(8,128)(2,1)}, u32[]{:S(2)}, u32[]{:S(2)}) collective-permute-start(bf16[128,2048]{1,0:T(8,128)(2,1)} %get-tuple-element.22), channel_id=1, source_target_pairs={{192,0},{0,64},{64,128},{128,192},{193,1},{1,65},{65,129},{129,193... | collective-permute-start | bytes 1572872 | tf_op jit(solution)/shard_map/ppermute | solution.py:196
  23.4 26.1 %collective-permute-start.11 = (bf16[128,2048]{1,0:T(8,128)(2,1)}, bf16[128,2048]{1,0:T(8,128)(2,1)}, u32[]{:S(2)}, u32[]{:S(2)}) collective-permute-start(bf16[128,2048]{1,0:T(8,128)(2,1)} %get-tuple-element.23), channel_id=1, source_target_pairs={{128,0},{192,64},{0,128},{64,192},{129,1},{193,65},{1,129},{65,193... | collective-permute-start | bytes 1572872 | tf_op jit(solution)/shard_map/ppermute | solution.py:196
  25.7 25.5 %collective-permute-start.9 = (bf16[128,2048]{1,0:T(8,128)(2,1)}, bf16[128,2048]{1,0:T(8,128)(2,1)}, u32[]{:S(2)}, u32[]{:S(2)}) collective-permute-start(bf16[128,2048]{1,0:T(8,128)(2,1)} %get-tuple-element.24), channel_id=1, source_target_pairs={{64,0},{128,64},{192,128},{0,192},{65,1},{129,65},{193,129},{1,193... | collective-permute-start | bytes 1572872 | tf_op jit(solution)/shard_map/ppermute | solution.py:196
  34.4 47.1 %all-to-all-start.2 = ((bf16[8,2,256,128]{3,2,1,0:T(8,128)(2,1)}), bf16[8,2,256,128]{3,2,1,0:T(8,128)(2,1)S(1)}, u32[]{:S(2)}, u32[]{:S(2)}) async-start(bf16[8,2,256,128]{3,2,1,0:T(8,128)(2,1)} %copy-done.8), calls=%async_computation.2 | async-start | bytes 2097152 | tf_op jit(solution)/shard_map/all_to_all | solution.py:206
  41.2 11.7 %collective-permute-start = (bf16[2,256,128]{2,1,0:T(8,128)(2,1)}, bf16[2,256,128]{2,1,0:T(8,128)(2,1)S(1)}, u32[]{:S(2)}, u32[]{:S(2)}) collective-permute-start(bf16[2,256,128]{2,1,0:T(8,128)(2,1)} %bitcast.6), channel_id=1, source_target_pairs={{64,0},{128,64},{192,128},{0,192},{65,1},{129,65},{193,129},{1,193... | collective-permute-start | bytes 393224 | tf_op jit(solution)/shard_map/ppermute | solution.py:196
  49.6 21.8 %collective-permute-start.14 = (bf16[128,2048]{1,0:T(8,128)(2,1)}, bf16[128,2048]{1,0:T(8,128)(2,1)S(1)}, u32[]{:S(2)}, u32[]{:S(2)}) collective-permute-start(bf16[128,2048]{1,0:T(8,128)(2,1)} %collective-permute-done.13.refs_10_), channel_id=1, source_target_pairs={{0,8},{8,0},{16,24},{24,16},{32,40},{40,32},{48,56},{56,48},{1,9},... | collective-permute-start | bytes 1572872 | tf_op jit(solution)/shard_map/ppermute | solution.py:199
  49.6 21.8 %collective-permute-start.12 = (bf16[128,2048]{1,0:T(8,128)(2,1)}, bf16[128,2048]{1,0:T(8,128)(2,1)S(1)}, u32[]{:S(2)}, u32[]{:S(2)}) collective-permute-start(bf16[128,2048]{1,0:T(8,128)(2,1)} %collective-permute-done.11.refs_8_), channel_id=1, source_target_pairs={{0,8},{8,0},{16,24},{24,16},{32,40},{40,32},{48,56},{56,48},{1,9},... | collective-permute-start | bytes 1572872 | tf_op jit(solution)/shard_map/ppermute | solution.py:199
  51.2 20.1 %collective-permute-start.10 = (bf16[128,2048]{1,0:T(8,128)(2,1)}, bf16[128,2048]{1,0:T(8,128)(2,1)S(1)}, u32[]{:S(2)}, u32[]{:S(2)}) collective-permute-start(bf16[128,2048]{1,0:T(8,128)(2,1)} %collective-permute-done.9.refs_6_), channel_id=1, source_target_pairs={{0,8},{8,0},{16,24},{24,16},{32,40},{40,32},{48,56},{56,48},{1,9},... | collective-permute-start | bytes 1572872 | tf_op jit(solution)/shard_map/ppermute | solution.py:199
  56.6 6.3 %collective-permute-start.3 = (bf16[272,128]{1,0:T(8,128)(2,1)S(1)}, bf16[272,128]{1,0:T(8,128)(2,1)S(1)}, u32[]{:S(2)}, u32[]{:S(2)}) collective-permute-start(bf16[272,128]{1,0:T(8,128)(2,1)S(1)} %get-tuple-element.14), channel_id=1, source_target_pairs={{0,64},{64,128},{128,192},{192,0},{1,65},{65,129},{129,193},{193,1... | collective-permute-start | bytes 208904 | tf_op jit(solution)/shard_map/ppermute | solution.py:227
  56.9 6.8 %collective-permute-start.4 = (bf16[272,128]{1,0:T(8,128)(2,1)S(1)}, bf16[272,128]{1,0:T(8,128)(2,1)S(1)}, u32[]{:S(2)}, u32[]{:S(2)}) collective-permute-start(bf16[272,128]{1,0:T(8,128)(2,1)S(1)} %get-tuple-element.15), channel_id=1, source_target_pairs={{0,128},{64,192},{128,0},{192,64},{1,129},{65,193},{129,1},{193,65... | collective-permute-start | bytes 208904 | tf_op jit(solution)/shard_map/ppermute | solution.py:227
  62.9 4.3 %collective-permute-start.5 = (bf16[272,128]{1,0:T(8,128)(2,1)S(1)}, bf16[272,128]{1,0:T(8,128)(2,1)S(1)}, u32[]{:S(2)}, u32[]{:S(2)}) collective-permute-start(bf16[272,128]{1,0:T(8,128)(2,1)S(1)} %get-tuple-element.16), channel_id=1, source_target_pairs={{0,192},{64,0},{128,64},{192,128},{1,193},{65,1},{129,65},{193,129... | collective-permute-start | bytes 208904 | tf_op jit(solution)/shard_map/ppermute | solution.py:227
  67.9 5.6 %collective-permute-start.8 = (bf16[256,128]{1,0:T(8,128)(2,1)S(1)}, bf16[256,128]{1,0:T(8,128)(2,1)S(1)}, u32[]{:S(2)}, u32[]{:S(2)}) collective-permute-start(bf16[256,128]{1,0:T(8,128)(2,1)S(1)} %shard_map.97.refs_0_), channel_id=1, source_target_pairs={{192,0},{0,64},{64,128},{128,192},{193,1},{1,65},{65,129},{129,193... | collective-permute-start | bytes 196616 | tf_op jit(solution)/shard_map/ppermute | solution.py:196
  68.0 6.3 %collective-permute-start.7 = (bf16[256,128]{1,0:T(8,128)(2,1)S(1)}, bf16[256,128]{1,0:T(8,128)(2,1)S(1)}, u32[]{:S(2)}, u32[]{:S(2)}) collective-permute-start(bf16[256,128]{1,0:T(8,128)(2,1)S(1)} %shard_map.97.refs_0_), channel_id=1, source_target_pairs={{128,0},{192,64},{0,128},{64,192},{129,1},{193,65},{1,129},{65,193... | collective-permute-start | bytes 196616 | tf_op jit(solution)/shard_map/ppermute | solution.py:196
  71.4 4.3 %collective-permute-start.6 = (bf16[256,128]{1,0:T(8,128)(2,1)S(1)}, bf16[256,128]{1,0:T(8,128)(2,1)S(1)}, u32[]{:S(2)}, u32[]{:S(2)}) collective-permute-start(bf16[256,128]{1,0:T(8,128)(2,1)S(1)} %shard_map.97.refs_0_), channel_id=1, source_target_pairs={{64,0},{128,64},{192,128},{0,192},{65,1},{129,65},{193,129},{1,193... | collective-permute-start | bytes 196616 | tf_op jit(solution)/shard_map/ppermute | solution.py:196
  79.0 0.8 copy-start.1
  79.9 0.8 copy-start.3
  80.7 0.8 copy-start.5
  81.5 36.8 %all-to-all-start.1 = ((bf16[8,128,256]{2,1,0:T(8,128)(2,1)}), bf16[8,128,256]{2,1,0:T(8,128)(2,1)}, u32[]{:S(2)}, u32[]{:S(2)}) async-start(bf16[8,128,256]{2,1,0:T(8,128)(2,1)} %shard_map.98), calls=%async_computation.1 | async-start | bytes 1048576 | tf_op jit(solution)/shard_map/all_to_all | solution.py:233
  89.9 36.3 %copy-start.13 = (s32[2,16]{1,0:T(2,128)S(1)}, s32[2,16]{1,0:T(2,128)}, u32[]{:S(2)}) copy-start(s32[2,16]{1,0:T(2,128)} %param.13) | copy-start | bytes 388
  95.0 45.3 %copy-start.12 = (f32[256]{0:T(256)S(1)}, f32[256]{0:T(256)}, u32[]{:S(2)}) copy-start(f32[256]{0:T(256)} %param.15) | copy-start | bytes 3076
  95.0 5.6 %collective-permute-start.15 = (bf16[272,128]{1,0:T(8,128)(2,1)S(1)}, bf16[272,128]{1,0:T(8,128)(2,1)S(1)}, u32[]{:S(2)}, u32[]{:S(2)}) collective-permute-start(bf16[272,128]{1,0:T(8,128)(2,1)S(1)} %get-tuple-element.19), channel_id=1, source_target_pairs={{0,64},{64,128},{128,192},{192,0},{1,65},{65,129},{129,193},{193,1... | collective-permute-start | bytes 208904 | tf_op jit(solution)/shard_map/ppermute | solution.py:227
  95.9 5.9 %collective-permute-start.16 = (bf16[272,128]{1,0:T(8,128)(2,1)S(1)}, bf16[272,128]{1,0:T(8,128)(2,1)S(1)}, u32[]{:S(2)}, u32[]{:S(2)}) collective-permute-start(bf16[272,128]{1,0:T(8,128)(2,1)S(1)} %get-tuple-element.20), channel_id=1, source_target_pairs={{0,128},{64,192},{128,0},{192,64},{1,129},{65,193},{129,1},{193,65... | collective-permute-start | bytes 208904 | tf_op jit(solution)/shard_map/ppermute | solution.py:227
  98.4 4.9 %collective-permute-start.17 = (bf16[272,128]{1,0:T(8,128)(2,1)S(1)}, bf16[272,128]{1,0:T(8,128)(2,1)S(1)}, u32[]{:S(2)}, u32[]{:S(2)}) collective-permute-start(bf16[272,128]{1,0:T(8,128)(2,1)S(1)} %get-tuple-element.21), channel_id=1, source_target_pairs={{0,192},{64,0},{128,64},{192,128},{1,193},{65,1},{129,65},{193,129... | collective-permute-start | bytes 208904 | tf_op jit(solution)/shard_map/ppermute | solution.py:227
  104.0 5.6 %collective-permute-start.20 = (bf16[256,128]{1,0:T(8,128)(2,1)S(1)}, bf16[256,128]{1,0:T(8,128)(2,1)S(1)}, u32[]{:S(2)}, u32[]{:S(2)}) collective-permute-start(bf16[256,128]{1,0:T(8,128)(2,1)S(1)} %shard_map.100.refs_0_), channel_id=1, source_target_pairs={{192,0},{0,64},{64,128},{128,192},{193,1},{1,65},{65,129},{129,193... | collective-permute-start | bytes 196616 | tf_op jit(solution)/shard_map/ppermute | solution.py:196
  105.2 5.8 %collective-permute-start.19 = (bf16[256,128]{1,0:T(8,128)(2,1)S(1)}, bf16[256,128]{1,0:T(8,128)(2,1)S(1)}, u32[]{:S(2)}, u32[]{:S(2)}) collective-permute-start(bf16[256,128]{1,0:T(8,128)(2,1)S(1)} %shard_map.100.refs_0_), channel_id=1, source_target_pairs={{128,0},{192,64},{0,128},{64,192},{129,1},{193,65},{1,129},{65,193... | collective-permute-start | bytes 196616 | tf_op jit(solution)/shard_map/ppermute | solution.py:196
  107.5 4.3 %collective-permute-start.18 = (bf16[256,128]{1,0:T(8,128)(2,1)S(1)}, bf16[256,128]{1,0:T(8,128)(2,1)S(1)}, u32[]{:S(2)}, u32[]{:S(2)}) collective-permute-start(bf16[256,128]{1,0:T(8,128)(2,1)S(1)} %shard_map.100.refs_0_), channel_id=1, source_target_pairs={{64,0},{128,64},{192,128},{0,192},{65,1},{129,65},{193,129},{1,193... | collective-permute-start | bytes 196616 | tf_op jit(solution)/shard_map/ppermute | solution.py:196
  111.8 1.0 copy-start.2
  112.8 1.0 copy-start.4
  113.9 1.0 copy-start.6
  118.3 21.2 %all-to-all-start.3 = ((bf16[8,128,256]{2,1,0:T(8,128)(2,1)}), bf16[8,128,256]{2,1,0:T(8,128)(2,1)S(1)}, u32[]{:S(2)}, u32[]{:S(2)}) async-start(bf16[8,128,256]{2,1,0:T(8,128)(2,1)} %shard_map.101), calls=%async_computation.3 | async-start | bytes 1048576 | tf_op jit(solution)/shard_map/all_to_all | solution.py:233
  139.6 14.4 %copy-start.9 = (bf16[2,128,256]{2,1,0:T(8,128)(2,1)}, bf16[2,128,256]{2,1,0:T(8,128)(2,1)S(1)}, u32[]{:S(2)}) copy-start(bf16[2,128,256]{2,1,0:T(8,128)(2,1)S(1)} %pad_maximum_fusion) | copy-start | bytes 393220

commit v2 on v0

v2 whole, which is shorter than its diff:
```python
import functools

import jax
import jax.numpy as jnp
from jax import lax
from jax.experimental import pallas as pl
from jax.experimental.pallas import tpu as pltpu
from jax.sharding import PartitionSpec as P

negative_fill = -1e30
peak_floor = -1e25
log2_e = 1.4426950408889634
VMEM = pl.BlockSpec(memory_space=pltpu.VMEM)
SMEM = pl.BlockSpec(memory_space=pltpu.SMEM)
HBM = pl.BlockSpec(memory_space=pltpu.HBM)
EXTRA = 16
SLOT, POOL, CORE, TP = range(4)
LARGE = 60


def kernel_params(mib):
    return pltpu.CompilerParams(vmem_limit_bytes=mib * 1024 * 1024)


def cost(flops, moved, exps=0):
    return pl.CostEstimate(flops=flops, bytes_accessed=moved, transcendentals=exps)


def order_kernel(place_ref, trace_ref, cache_ref, out_ref, held, wide, ordered, sems, out_sems):
    traces, rows, size = held.shape
    groups = out_ref.shape[0]
    slots = traces // groups
    copies = [
        pltpu.make_async_copy(cache_ref.at[trace_ref[n]], held.at[n], sems.at[n])
        for n in range(traces)
    ]
    for copy in copies:
        copy.start()
    pending = []
    for n, copy in enumerate(copies):
        copy.wait()
        wide[n % 2] = held[n].astype(jnp.float32)
        for kind in range(2):
            part = wide[n % 2, pl.ds(kind, rows // 2, stride=2), :]
            at = n % slots * rows + kind * (rows // 2)
            ordered[n // slots, pl.ds(at, rows // 2), :] = part.astype(jnp.bfloat16)
        if n % slots == slots - 1:
            group = n // slots
            pending.append(
                pltpu.make_async_copy(ordered.at[group], out_ref.at[group], out_sems.at[group])
            )
            pending[-1].start()
    for copy in pending:
        copy.wait()


def order_blocks(place, slot_trace, prior_rows, groups):
    traces, rows, size = prior_rows.shape
    ordered = (groups, traces // groups * rows, size)
    return pl.pallas_call(
        order_kernel,
        out_shape=jax.ShapeDtypeStruct(ordered, jnp.bfloat16),
        in_specs=[SMEM, SMEM, HBM],
        out_specs=HBM,
        scratch_shapes=[
            pltpu.VMEM((traces, rows, size), jnp.bfloat16),
            pltpu.VMEM((2, rows, size), jnp.float32),
            pltpu.VMEM(ordered, jnp.bfloat16),
            pltpu.SemaphoreType.DMA((traces,)),
            pltpu.SemaphoreType.DMA((groups,)),
        ],
        compiler_params=kernel_params(LARGE),
        cost_estimate=cost(0, 4 * traces * rows * size),
    )(place, slot_trace, prior_rows)


def stage_kernel(
    place_ref, weight_ref, q0, q1, q2, q3, fresh_ref, packed_ref, new_ref, own_ref, *refs
):
    outs, (staged, kept, wide, in_sems, out_sems) = refs[:-5], refs[-5:]
    pools = len(outs) + 1
    size, columns = outs[0].shape
    arriving = []
    for o in range(1, pools):
        to = lax.rem(place_ref[POOL] + pools - o, pools)
        half = weight_ref.at[
            pl.ds(pl.multiple_of(place_ref[CORE] * size, size), size),
            pl.ds(pl.multiple_of(to * columns, columns), columns),
        ]
        arriving.append(pltpu.make_async_copy(half, staged.at[o - 1], in_sems.at[o]))
    own = weight_ref.at[:, pl.ds(pl.multiple_of(place_ref[POOL] * columns, columns), columns)]
    arriving.append(pltpu.make_async_copy(own, kept, in_sems.at[0]))
    for copy in arriving:
        copy.start()
    for n, ref in enumerate((q0, q1, q2, q3)):
        packed_ref[n] = ref[...]
    for slot in range(fresh_ref.shape[0]):
        wide[...] = fresh_ref[slot].astype(jnp.float32)
        for kind in range(2):
            part = wide[pl.ds(kind, wide.shape[0] // 2, stride=2), :]
            new_ref[slot, kind] = part.astype(jnp.bfloat16)
    leaving = [
        pltpu.make_async_copy(source, out, out_sems.at[n])
        for n, (source, out) in enumerate(
            [(staged.at[n], out) for n, out in enumerate(outs)] + [(kept, own_ref)]
        )
    ]
    for n, copy in enumerate(leaving):
        arriving[n].wait()
        copy.start()
    for copy in leaving:
        copy.wait()


def stage(place, weight, queried, fresh):
    pools = len(queried)
    slots, rows, size = fresh.shape
    block = (weight.shape[0] // 2, weight.shape[1] // pools)
    kept = (weight.shape[0], block[1])
    return pl.pallas_call(
        stage_kernel,
        out_shape=[
            jax.ShapeDtypeStruct((pools, *queried[0].shape), jnp.bfloat16),
            jax.ShapeDtypeStruct((slots, 2, rows // 2, size), jnp.bfloat16),
            jax.ShapeDtypeStruct(kept, jnp.bfloat16),
        ]
        + [jax.ShapeDtypeStruct(block, jnp.bfloat16)] * (pools - 1),
        in_specs=[SMEM, HBM] + [VMEM] * (pools + 1),
        out_specs=[VMEM] * 2 + [HBM] * pools,
        scratch_shapes=[
            pltpu.VMEM((pools - 1, *block), jnp.bfloat16),
            pltpu.VMEM(kept, jnp.bfloat16),
            pltpu.VMEM((rows, size), jnp.float32),
            pltpu.SemaphoreType.DMA((pools,)),
            pltpu.SemaphoreType.DMA((pools,)),
        ],
        compiler_params=kernel_params(LARGE),
        cost_estimate=cost(0, 8 * pools * block[0] * block[1]),
    )(place, weight, *queried, fresh)


def attend_kernel(
    place_ref, trace_ref, length_ref, query_ref, new_ref, prior_ref, pay_ref
):
    pools, slots, rows, size = query_ref.shape
    sources, block = prior_ref.shape[0], prior_ref.shape[1] // (2 * slots)
    width = sources * block
    factor = size**-0.5 * log2_e
    contract = (((1,), (1,)), ((), ()))
    position = lax.broadcasted_iota(jnp.int32, (1, width), 1)
    for slot in range(slots):
        valid = length_ref[trace_ref[place_ref[SLOT] + slot]] - place_ref[POOL] * width
        usable = position < valid
        at = 2 * slot * block
        keys = prior_ref[:, pl.ds(at, block), :].reshape(width, size)
        values = prior_ref[:, pl.ds(at + block, block), :].reshape(width, size)
        for tile in range(pools):
            pay = pay_ref.at[lax.rem(place_ref[POOL] + tile, pools)]
            query = query_ref[tile, slot]
            scores = lax.dot_general(query, keys, contract, preferred_element_type=jnp.float32)
            scores = jnp.where(usable, scores, negative_fill)
            peak = jnp.max(scores, -1, keepdims=True)
            if tile == 0:
                fresh_scores = lax.dot_general(
                    query, new_ref[slot, 0], contract, preferred_element_type=jnp.float32
                )
                heads = rows // fresh_scores.shape[1]
                token = lax.broadcasted_iota(jnp.int32, fresh_scores.shape, 0) // heads
                causal = lax.broadcasted_iota(jnp.int32, fresh_scores.shape, 1) <= token
                fresh_scores = jnp.where(causal, fresh_scores, negative_fill)
                peak = jnp.maximum(peak, jnp.max(fresh_scores, -1, keepdims=True))
            peak = jnp.maximum(peak * factor, peak_floor).astype(jnp.bfloat16).astype(jnp.float32)
            weights = jnp.exp2(scores * factor - peak)
            total = jnp.sum(weights, -1, keepdims=True)
            blended = jnp.dot(
                weights.astype(jnp.bfloat16), values, preferred_element_type=jnp.float32
            )
            if tile == 0:
                fresh_weights = jnp.exp2(fresh_scores * factor - peak)
                total = total + jnp.sum(fresh_weights, -1, keepdims=True)
                blended = blended + jnp.dot(
                    fresh_weights.astype(jnp.bfloat16),
                    new_ref[slot, 1],
                    preferred_element_type=jnp.float32,
                )
            pay[pl.ds(slot * rows, rows), :] = blended.astype(jnp.bfloat16)
            high = total.astype(jnp.bfloat16).astype(jnp.float32)
            columns = columns_of((rows, size), (peak, high, total - high))
            halves = [columns[n : n + size].T[:8] for n in range(0, rows, size)]
            pay[pl.ds(slots * rows + slot * EXTRA, EXTRA), :] = jnp.concatenate(halves, 0).astype(
                jnp.bfloat16
            )


def attend(place, slot_trace, prefix_length, queries, new, prior):
    pools, slots, rows, size = queries.shape
    width = prior.shape[0] * prior.shape[1] // (2 * slots)
    return pl.pallas_call(
        attend_kernel,
        out_shape=jax.ShapeDtypeStruct((pools, slots * (rows + EXTRA), size), jnp.bfloat16),
        in_specs=[SMEM] * 3 + [VMEM] * 3,
        out_specs=VMEM,
        compiler_params=kernel_params(24),
        cost_estimate=cost(32 * rows * width * size, 8 * width * size, 8 * rows * width),
    )(place, slot_trace, prefix_length, queries, new, prior)


def columns_of(shape, columns):
    lane = lax.broadcasted_iota(jnp.int32, shape, 1)
    laid = jnp.zeros(shape, jnp.float32)
    for n, column in enumerate(columns):
        laid = jnp.where(lane == n, column, laid)
    return laid


def rows_of(shape, rows):
    at = lax.broadcasted_iota(jnp.int32, shape, 0)
    laid = jnp.zeros(shape, jnp.float32)
    for n, row in enumerate(rows):
        laid = jnp.where(at == n, row, laid)
    return laid


def split_three(value):
    high = value.astype(jnp.bfloat16).astype(jnp.float32)
    middle = (value - high).astype(jnp.bfloat16).astype(jnp.float32)
    return high, middle, value - high - middle


def merge_kernel(pay_ref, out_ref, wide):
    rows, size = wide.shape
    heads = rows // size
    pools = out_ref.shape[0]
    slots = out_ref.shape[1] // rows
    for slot in range(slots):
        peaks, totals = [], []
        for n in range(pools):
            stats = pay_ref[n, pl.ds(slots * rows + slot * EXTRA, EXTRA), :].astype(jnp.float32)
            columns = jnp.concatenate(
                [
                    jnp.concatenate([stats[8 * half : 8 * half + 8]] * (size // 8), 0).T
                    for half in range(heads)
                ],
                0,
            )
            peaks.append(columns[:, 0:1])
            totals.append(columns[:, 1:2] + columns[:, 2:3])
        top = functools.reduce(jnp.maximum, peaks)
        shares = [jnp.exp2(peak - top) for peak in peaks]
        total = sum(share * part for share, part in zip(shares, totals))
        blended = sum(
            share * pay_ref[n, pl.ds(slot * rows, rows), :].astype(jnp.float32)
            for n, share in enumerate(shares)
        )
        wide[...] = blended / total
        for head in range(heads):
            part = wide[pl.ds(head, size, stride=heads), :].astype(jnp.bfloat16)
            for n in range(pools):
                out_ref[n, pl.ds(slot * rows + head * size, size), :] = part


def merge(pays, slots):
    pools, rows, size = pays.shape
    rows = rows // slots - EXTRA
    return pl.pallas_call(
        merge_kernel,
        out_shape=jax.ShapeDtypeStruct((pools, slots * rows, size), jnp.bfloat16),
        in_specs=[VMEM],
        out_specs=VMEM,
        scratch_shapes=[pltpu.VMEM((rows, size), jnp.float32)],
        compiler_params=kernel_params(8),
        cost_estimate=cost(0, 20 * rows * size),
    )(pays)


def project_kernel(place_ref, attended_ref, weight_ref, *refs):
    moved, (out_ref, weights, sems) = refs[:-3], refs[-3:]
    dests, wide = out_ref.shape[0], out_ref.shape[2]
    pools, tokens, size = attended_ref.shape[0], out_ref.shape[1], attended_ref.shape[2]
    slots = tokens // size
    columns = weights.shape[2]
    chunks = sems.shape[0]
    span = columns // chunks
    core = place_ref[CORE]
    copies = []
    for chunk in range(chunks):
        at = pl.ds(chunk * span, span)
        batch = [(weight_ref.at[:, at], weights.at[0, :, at])]
        for n, ref in enumerate(moved):
            half = core if n % 2 == 0 else 1 - core
            rows = pl.ds(pl.multiple_of(half * size, size), size)
            batch.append((ref.at[pl.ds(0, size), at], weights.at[1 + n // 2, rows, at]))
        copies.append([
            pltpu.make_async_copy(source, target, sems.at[chunk, n])
            for n, (source, target) in enumerate(batch)
        ])
        for copy in copies[-1]:
            copy.start()
    inputs = []
    for n in range(pools):
        ref = attended_ref.at[lax.rem(place_ref[POOL] + n, pools)]
        rows = [
            jnp.concatenate([ref[pl.ds(at, size), :], ref[pl.ds(at + size, size), :]], 1)
            for at in range(0, 2 * slots * size, 2 * size)
        ]
        inputs.append(jnp.concatenate(rows, 0))
    for chunk in range(chunks):
        for copy in copies[chunk]:
            copy.wait()
        for dest in range(chunk * dests // chunks, (chunk + 1) * dests // chunks):
            at = pl.ds(dest * wide, wide)
            total = jnp.dot(inputs[0], weights[0, :, at], preferred_element_type=jnp.float32)
            for n in range(1, pools):
                total += jnp.dot(inputs[n], weights[n, :, at], preferred_element_type=jnp.float32)
            out_ref[dest] = total.astype(jnp.bfloat16)


def project(place, attended, weight, moved, dests):
    pools, rows, size = attended.shape
    tokens = rows // 2
    columns = moved[0].shape[1]
    chunks = 4
    return pl.pallas_call(
        project_kernel,
        out_shape=jax.ShapeDtypeStruct((dests, tokens, columns // dests), jnp.bfloat16),
        in_specs=[SMEM, VMEM] + [HBM] * (1 + len(moved)),
        out_specs=VMEM,
        scratch_shapes=[
            pltpu.VMEM((pools, weight.shape[0], columns), jnp.bfloat16),
            pltpu.SemaphoreType.DMA((chunks, 1 + len(moved))),
        ],
        compiler_params=kernel_params(16),
        cost_estimate=cost(16 * tokens * size * columns, 16 * size * columns),
    )(place, attended, weight, *moved)


def finish_kernel(arrived_ref, bound_ref, reward_ref, out_ref, spread_ref):
    slots, tokens, wide = out_ref.shape
    steps = bound_ref.shape[1]
    for slot in range(slots):
        total = jnp.zeros((tokens, wide), jnp.float32)
        for n in range(arrived_ref.shape[0]):
            total += arrived_ref[n, pl.ds(slot * tokens, tokens), :].astype(jnp.float32)
        out_ref[slot] = total.astype(jnp.bfloat16)
        rounded = out_ref[slot].astype(jnp.float32)
        row = jnp.sum(rounded * reward_ref[...], -1, keepdims=True)
        lane = lax.broadcasted_iota(jnp.int32, (tokens, steps), 0)
        chosen = jnp.sum(jnp.where(lane == bound_ref[slot : slot + 1, :], row, 0.0), 0, keepdims=True)
        for n in range(spread_ref.shape[0]):
            spread_ref[n, slot : slot + 1, :] = chosen


def finish(arrived, boundaries, reward, spread):
    slots, steps = boundaries.shape
    _, rows, wide = arrived.shape
    return pl.pallas_call(
        finish_kernel,
        out_shape=[
            jax.ShapeDtypeStruct((slots, rows // slots, wide), jnp.bfloat16),
            jax.ShapeDtypeStruct((spread, slots, steps), jnp.float32),
        ],
        in_specs=[VMEM] * 3,
        out_specs=[VMEM] * 2,
        compiler_params=kernel_params(8),
    )(arrived, boundaries, reward)


def shards(
    prior_cache,
    prefix_length,
    slot_trace,
    queries,
    new_token_cache,
    boundaries,
    output_weight,
    reward_weight,
):
    pool, seq, tp = lax.axis_index("pool"), lax.axis_index("seq"), lax.axis_index("tp")
    pools, seqs, tps = lax.axis_size("pool"), lax.axis_size("seq"), lax.axis_size("tp")
    slots, new_len, _, pair, size = queries.shape
    traces, block = prior_cache.shape[:2]
    place = jnp.stack([seq * slots, pool, lax.rem(seq, 2), tp]).astype(jnp.int32)
    rows_all = output_weight.reshape(pair * size, -1)
    prior_rows = prior_cache.reshape(traces, 2 * block, size)
    own_queries = queries.reshape(slots, new_len * pair, size)

    def from_pool(array, offset):
        return lax.ppermute(array, "pool", [((n + offset) % pools, n) for n in range(pools)])

    def turn(array, axes):
        return lax.all_to_all(array, axes, split_axis=0, concat_axis=0, tiled=True)

    def swap_core(array):
        return lax.ppermute(array, "seq", [(n, n ^ 1) for n in range(seqs)])

    sent = order_blocks(place, slot_trace, prior_rows, seqs)
    sent, own_queries = lax.optimization_barrier((sent, own_queries))
    prior = turn(sent, "seq")

    queried = [own_queries] + [from_pool(own_queries, o) for o in range(1, pools)]
    fresh = new_token_cache.reshape(slots, 2 * new_len, size)
    packed, new, kept, *leaving = stage(place, rows_all, queried, fresh)
    came = [from_pool(part, o) for o, part in enumerate(leaving, 1)]
    pays = attend(place, slot_trace, prefix_length, packed, new, prior)
    pays, came = lax.optimization_barrier((turn(pays, "pool"), came))
    moved = [part for got in came for part in (got, swap_core(got))]
    gathered = turn(merge(pays, slots), "pool")
    partial = project(place, gathered, kept, moved, tps)
    arrived = turn(partial, "tp")
    layer_out, spread = finish(arrived, boundaries, reward_weight.reshape(1, -1), pools * tps)
    return (layer_out, jnp.sum(turn(spread, ("pool", "tp")), 0))


def solution(mesh):
    placed = (
        P(None, ("pool", "seq"), "tp", None, None),
        P(),
        P(),
        P("seq", None, "tp", "pool", None),
        P("seq", None, "tp", None, None),
        P("seq", None),
        P("tp", "pool", None, None),
        P(("pool", "tp")),
    )
    return jax.shard_map(
        shards,
        mesh=mesh,
        in_specs=placed,
        out_specs=(P("seq", None, ("pool", "tp")), P("seq", None)),
        check_vma=False,
    )
```

time: 480 us -> 130 us (0.27)
  waiting for transfers between devices: 316 us -> 22.4 us
  blocking collectives: 105 us -> 61.1 us
  Pallas kernels: 0 us -> 22.3 us
  starting transfers between devices: 0.08 us -> 18.6 us
  matrix products: 15 us -> 0 us
  local copies, waits for them, and re-layouts: 17.4 us -> 2.63 us
  between operations: 14.1 us -> 0.74 us
  other arithmetic: 11.9 us -> 1.22 us
    reduce_scatter x1 -> x0, waiting for transfers between devices: 230 us -> none  [shards(): lax.psum_scatter(lax.dot_general(weight_rows, token_rows, (((0,), (1,)),...]
    all_gather x1 -> x0, waiting for transfers between devices: 86 us -> none  [shards(): whole = lax.all_gather(moved, 'pool', axis=1, tiled=True)]
    psum x1 -> x0, blocking collectives: 73 us -> none  [shards(): rewards = lax.psum(partial_rewards, ('pool', 'tp'))]
    all_to_all x1 -> x3, blocking collectives: 31.7 us -> 61.1 us  [turn(): return lax.all_to_all(array, axes, split_axis=0, concat_axis=0, tiled=True)]
    pallas_call x0 -> x6, Pallas kernels: none -> 22.3 us  [the longest x1 8.51 us: attend(): pl.pallas_call(attend_kernel, out_shape=jax.ShapeDtypeStruct((pools, slot...]
    dot_general x10 -> x0, matrix products: 15 us -> none  [the longest x1 6.67 us: shards(): lax.dot_general(weight_rows, token_rows, (((0,), (1,)), ((), ())), prefer...]
    all_to_all x0 -> x2, waiting for transfers between devices: none -> 12.1 us  [turn(): return lax.all_to_all(array, axes, split_axis=0, concat_axis=0, tiled=True)]
    ppermute x0 -> x9, waiting for transfers between devices: none -> 10.2 us  [the longest x6 10.2 us: from_pool(): lax.ppermute(array, 'pool', [((n + offset) % pools, n) for n in range(poo...]
  transfers between devices with their start and end apart: 2 -> 11, of which waited for: 2 -> 7; matrix products, arithmetic and copies ran while one was open for 0% -> 0% of each run, Pallas kernels for 0% -> 11%
where the time goes in v2:
time: 130 us; the launch traced here: 129 us
  blocking collectives  61.1 us (47%)
  waiting for transfers between devices  22.4 us (17%)
  Pallas kernels  22.3 us (17%)
  starting transfers between devices  18.6 us (14%)
  local copies, waits for them, and re-layouts  2.63 us (2%)
    all_to_all x3, blocking collectives, turn(): return lax.all_to_all(array, axes, split_axis=0, concat_axis=0, tiled=True)  61.1 us
    all_to_all x2, waiting for transfers between devices, turn(): return lax.all_to_all(array, axes, split_axis=0, concat_axis=0, tiled=True)  12.1 us
    ppermute x6, waiting for transfers between devices, from_pool(): lax.ppermute(array, 'pool', [((n + offset) % pools, n) for n in range(poo...  10.2 us
    all_to_all x2, starting transfers between devices, turn(): return lax.all_to_all(array, axes, split_axis=0, concat_axis=0, tiled=True)  9.46 us
    ppermute x6, starting transfers between devices, from_pool(): lax.ppermute(array, 'pool', [((n + offset) % pools, n) for n in range(poo...  8.66 us
    pallas_call x1, Pallas kernels, attend(): pl.pallas_call(attend_kernel, out_shape=jax.ShapeDtypeStruct((pools, slot...  8.51 us
    pallas_call x1, Pallas kernels, stage(): pl.pallas_call(stage_kernel, out_shape=[jax.ShapeDtypeStruct((pools, *que...  4.84 us
    pallas_call x1, Pallas kernels, project(): pl.pallas_call(project_kernel, out_shape=jax.ShapeDtypeStruct((dests, tok...  3.6 us
  transfers between devices with their start and end apart: 11, of which 7 were waited for; matrix products, arithmetic and copies ran while one was open for 0% of the time, Pallas kernels for 11%

profile of v2, /device:TPU:8, one launch (start us, length us, event | category | flops | bytes accessed | tf_op | source)
XLA Modules:
  0.0 129.0 jit_solution(16273247632449545588)
XLA Ops:
  0.6 0.6 pad_add_fusion.place_ref
  1.3 3.3 %shard_map.95 = bf16[8,1024,128]{2,1,0:T(8,128)(2,1)} custom-call(s32[4]{0:T(128)} %pad_add_fusion.place_ref, s32[16]{0:T(128)} %trace_ref.3, bf16[16,512,128]{2,1,0:T(8,128)(2,1)} %bitcast.11), custom_call_target="tpu_custom_call" | custom-call | bytes 4194304 | tf_op jit(solution)/shard_map/pallas_call | solution.py:60
  4.6 0.0 copy-start.8
  4.6 5.8 %all-to-all-start = ((bf16[8,1024,128]{2,1,0:T(8,128)(2,1)}), bf16[8,1024,128]{2,1,0:T(8,128)(2,1)S(1)}, u32[]{:S(2)}, u32[]{:S(2)}) async-start(bf16[8,1024,128]{2,1,0:T(8,128)(2,1)} %shard_map.95), calls=%async_computation | async-start | bytes 4194304 | tf_op jit(solution)/shard_map/all_to_all | solution.py:391
  10.4 0.0 copy-done.8
  10.4 0.7 collective-permute-start.2
  11.1 2.7 %collective-permute-start.1 = (bf16[2,256,128]{2,1,0:T(8,128)(2,1)S(1)}, bf16[2,256,128]{2,1,0:T(8,128)(2,1)S(1)}, u32[]{:S(2)}, u32[]{:S(2)}) collective-permute-start(bf16[2,256,128]{2,1,0:T(8,128)(2,1)S(1)} %bitcast.14), channel_id=1, source_target_pairs={{128,0},{192,64},{0,128},{64,192},{129,1},{193,65},{1,129},{65,193... | collective-permute-start | bytes 393224 | tf_op jit(solution)/shard_map/ppermute | solution.py:388
  13.9 1.4 %collective-permute-start = (bf16[2,256,128]{2,1,0:T(8,128)(2,1)S(1)}, bf16[2,256,128]{2,1,0:T(8,128)(2,1)S(1)}, u32[]{:S(2)}, u32[]{:S(2)}) collective-permute-start(bf16[2,256,128]{2,1,0:T(8,128)(2,1)S(1)} %bitcast.15), channel_id=1, source_target_pairs={{64,0},{128,64},{192,128},{0,192},{65,1},{129,65},{193,129},{1,193... | collective-permute-start | bytes 393224 | tf_op jit(solution)/shard_map/ppermute | solution.py:388
  15.3 2.5 %collective-permute-done.2.q3 = bf16[2,256,128]{2,1,0:T(8,128)(2,1)S(1)} collective-permute-done((bf16[2,256,128]{2,1,0:T(8,128)(2,1)S(1)}, bf16[2,256,128]{2,1,0:T(8,128)(2,1)S(1)}, u32[]{:S(2)}, u32[]{:S(2)}) %collective-permute-start.2) | collective-permute-done | bytes 131104 | tf_op jit(solution)/shard_map/ppermute | solution.py:388
  17.8 2.4 %collective-permute-done.1.q2 = bf16[2,256,128]{2,1,0:T(8,128)(2,1)S(1)} collective-permute-done((bf16[2,256,128]{2,1,0:T(8,128)(2,1)S(1)}, bf16[2,256,128]{2,1,0:T(8,128)(2,1)S(1)}, u32[]{:S(2)}, u32[]{:S(2)}) %collective-permute-start.1) | collective-permute-done | bytes 131104 | tf_op jit(solution)/shard_map/ppermute | solution.py:388
  20.2 0.4 collective-permute-done.q1
  20.6 0.0 copy-done.9
  20.6 0.3 copy-done.10
  20.9 0.4 copy-done.11
  21.2 4.8 %shard_map.96 = (bf16[4,2,256,128]{3,2,1,0:T(8,128)(2,1)}, bf16[2,2,128,128]{3,2,1,0:T(8,128)(2,1)}, bf16[256,2048]{1,0:T(8,128)(2,1)}, bf16[128,2048]{1,0:T(8,1...) custom-call(s32[4]{0:T(128)} %pad_add_fusion.place_ref, bf16[256,8192]{1,0:T(8,128)(2,1)} %bitcast.10, ...), custom_call_target="tpu_custom_call" | custom-call | bytes 8388608 | tf_op jit(solution)/shard_map/pallas_call | solution.py:120
  26.1 2.8 %collective-permute-start.3 = (bf16[128,2048]{1,0:T(8,128)(2,1)}, bf16[128,2048]{1,0:T(8,128)(2,1)S(1)}, u32[]{:S(2)}, u32[]{:S(2)}) collective-permute-start(bf16[128,2048]{1,0:T(8,128)(2,1)} %get-tuple-element.20), channel_id=1, source_target_pairs={{64,0},{128,64},{192,128},{0,192},{65,1},{129,65},{193,129},{1,193... | collective-permute-start | bytes 1572872 | tf_op jit(solution)/shard_map/ppermute | solution.py:388
  28.8 1.0 collective-permute-start.4
  29.9 0.0 collective-permute-start.5
  29.9 6.3 %all-to-all-done.prior_ref = bf16[8,1024,128]{2,1,0:T(8,128)(2,1)S(1)} async-done(((bf16[8,1024,128]{2,1,0:T(8,128)(2,1)}), bf16[8,1024,128]{2,1,0:T(8,128)(2,1)S(1)}, u32[]{:S(2)}, u32[]{:S(2)}) %all-to-all-start) | async-done | bytes 2097184 | tf_op jit(solution)/shard_map/all_to_all | solution.py:391
  36.2 0.0 copy-done.1
  36.2 0.0 copy-done.4
  36.2 0.0 copy-done.7
  36.2 0.0 copy-start.5
  36.2 1.0 copy-done.5
  37.2 0.9 copy-done.6
  38.1 8.5 %shard_map.97 = bf16[4,544,128]{2,1,0:T(8,128)(2,1)} custom-call(s32[4]{0:T(128)S(1)} %copy-done.1, s32[16]{0:T(128)S(1)} %copy-done.4, s32[16]{0:T(128)S(1)} %copy-done.7, bf16[4,2,256,128]{3,2,1,0:T(8,128)(2,1)S(1)} %copy-done.5, bf16[2,2,128,128]{3,2,1,0:T(8,128)(2,1)S(1)} %copy-done.6, bf16[8,1024,128]{2,1,0:T(8,128)(2,1)S(1)} %all-to-all-done.prior_ref), custom_call_target="tpu_custom_call" | custom-call | flops 2147483648 | bytes 2097152 | tf_op jit(solution)/shard_map/pallas_call | solution.py:198
  46.7 3.6 %all-to-all-start.1 = ((bf16[4,544,128]{2,1,0:T(8,128)(2,1)}), bf16[4,544,128]{2,1,0:T(8,128)(2,1)S(1)}, u32[]{:S(2)}, u32[]{:S(2)}) async-start(bf16[4,544,128]{2,1,0:T(8,128)(2,1)} %shard_map.97), calls=%async_computation.1 | async-start | bytes 1114112 | tf_op jit(solution)/shard_map/all_to_all | solution.py:391
  50.3 1.9 %collective-permute-done.3.refs_0_ = bf16[128,2048]{1,0:T(8,128)(2,1)S(1)} collective-permute-done((bf16[128,2048]{1,0:T(8,128)(2,1)}, bf16[128,2048]{1,0:T(8,128)(2,1)S(1)}, u32[]{:S(2)}, u32[]{:S(2)}) %collective-permute-start.3) | collective-permute-done | bytes 524320 | tf_op jit(solution)/shard_map/ppermute | solution.py:388
  52.2 0.0 collective-permute-done.4.refs_2_
  52.2 3.0 %collective-permute-done.5.refs_4_ = bf16[128,2048]{1,0:T(8,128)(2,1)} collective-permute-done((bf16[128,2048]{1,0:T(8,128)(2,1)}, bf16[128,2048]{1,0:T(8,128)(2,1)}, u32[]{:S(2)}, u32[]{:S(2)}) %collective-permute-start.5) | collective-permute-done | bytes 524320 | tf_op jit(solution)/shard_map/ppermute | solution.py:388
  55.2 5.8 %all-to-all-done.1.pay_ref = bf16[4,544,128]{2,1,0:T(8,128)(2,1)S(1)} async-done(((bf16[4,544,128]{2,1,0:T(8,128)(2,1)}), bf16[4,544,128]{2,1,0:T(8,128)(2,1)S(1)}, u32[]{:S(2)}, u32[]{:S(2)}) %all-to-all-start.1) | async-done | bytes 557088 | tf_op jit(solution)/shard_map/all_to_all | solution.py:391
  61.0 0.0 collective-permute-start.6
  61.0 0.5 collective-permute-start.7
  61.5 0.0 collective-permute-start.8
  61.5 1.2 shard_map.98
  62.8 12.8 %all_to_all.25.attended_ref = bf16[4,512,128]{2,1,0:T(8,128)(2,1)S(1)} all-to-all(bf16[4,512,128]{2,1,0:T(8,128)(2,1)S(1)} %shard_map.98), channel_id=1, replica_groups=mesh['pool'=4,'seq'=8,'tp'=8] {'pool'}, dimensions={0} | all-to-all | bytes 1048576 | tf_op jit(solution)/shard_map/all_to_all | solution.py:391
  75.6 0.0 collective-permute-done.6.refs_1_
  75.6 0.0 collective-permute-done.7.refs_3_
  75.6 0.0 collective-permute-done.8.refs_5_
  75.6 0.0 copy-done
  75.6 3.6 %shard_map.99 = bf16[8,256,256]{2,1,0:T(8,128)(2,1)S(1)} custom-call(s32[4]{0:T(128)S(1)} %copy-done.1, bf16[4,512,128]{2,1,0:T(8,128)(2,1)S(1)} %all_to_all.25.attended_ref, bf16[256,2048]{1,0:T(8,128)(2,1)S(1)} %copy-done, bf16[128,2048]{1,0:T(8,128)(2,1)S(1)} %collective-permute-done.3.refs_0_, bf16[128,2048]{1,0:T(8,128)(2,1)S(1)} %collective-permute-done.6.refs_1_, ...), custom_call_target="tpu_custom_call" | custom-call | flops 1073741824 | bytes 4194304 | tf_op jit(solution)/shard_map/pallas_call | solution.py:323
  79.2 0.0 copy-start.2
  79.3 0.0 copy-start.3
  79.3 35.5 %all_to_all.26.arrived_ref = bf16[8,256,256]{2,1,0:T(8,128)(2,1)S(1)} all-to-all(bf16[8,256,256]{2,1,0:T(8,128)(2,1)S(1)} %shard_map.99), channel_id=1, replica_groups=mesh['pool'=4,'seq'=8,'tp'=8] {'tp'}, dimensions={0} | all-to-all | bytes 2097152 | tf_op jit(solution)/shard_map/all_to_all | solution.py:391
  114.8 0.0 copy-done.3
  114.8 0.8 shard_map.100
  115.6 12.8 %all_to_all.27 = f32[32,2,16]{2,1,0:T(2,128)S(1)} all-to-all(f32[32,2,16]{2,1,0:T(2,128)S(1)} %get-tuple-element.29), channel_id=1, replica_groups=mesh['pool'=4,'seq'=8,'tp'=8] {'pool','tp'}, dimensions={0} | all-to-all | bytes 8192 | tf_op jit(solution)/shard_map/all_to_all | solution.py:391
  128.4 0.6 reduce_sum.9
  (9 shorter events, 0.0 us)
Async XLA Ops:
  4.6 5.9 %copy-start.8 = (bf16[2,128,1,2,128]{4,3,2,1,0:T(2,128)(2,1)S(1)}, bf16[2,128,1,2,128]{4,3,2,1,0:T(2,128)(2,1)}, u32[]{:S(2)}) copy-start(bf16[2,128,1,2,128]{4,3,2,1,0:T(2,128)(2,1)} %param.11) | copy-start | bytes 393220
  4.6 31.6 %all-to-all-start = ((bf16[8,1024,128]{2,1,0:T(8,128)(2,1)}), bf16[8,1024,128]{2,1,0:T(8,128)(2,1)S(1)}, u32[]{:S(2)}, u32[]{:S(2)}) async-start(bf16[8,1024,128]{2,1,0:T(8,128)(2,1)} %shard_map.95), calls=%async_computation | async-start | bytes 4194304 | tf_op jit(solution)/shard_map/all_to_all | solution.py:391
  10.4 7.3 %collective-permute-start.2 = (bf16[2,256,128]{2,1,0:T(8,128)(2,1)S(1)}, bf16[2,256,128]{2,1,0:T(8,128)(2,1)S(1)}, u32[]{:S(2)}, u32[]{:S(2)}) collective-permute-start(bf16[2,256,128]{2,1,0:T(8,128)(2,1)S(1)} %bitcast.13), channel_id=1, source_target_pairs={{192,0},{0,64},{64,128},{128,192},{193,1},{1,65},{65,129},{129,193... | collective-permute-start | bytes 393224 | tf_op jit(solution)/shard_map/ppermute | solution.py:388
  11.1 9.1 %collective-permute-start.1 = (bf16[2,256,128]{2,1,0:T(8,128)(2,1)S(1)}, bf16[2,256,128]{2,1,0:T(8,128)(2,1)S(1)}, u32[]{:S(2)}, u32[]{:S(2)}) collective-permute-start(bf16[2,256,128]{2,1,0:T(8,128)(2,1)S(1)} %bitcast.14), channel_id=1, source_target_pairs={{128,0},{192,64},{0,128},{64,192},{129,1},{193,65},{1,129},{65,193... | collective-permute-start | bytes 393224 | tf_op jit(solution)/shard_map/ppermute | solution.py:388
  13.9 6.7 %collective-permute-start = (bf16[2,256,128]{2,1,0:T(8,128)(2,1)S(1)}, bf16[2,256,128]{2,1,0:T(8,128)(2,1)S(1)}, u32[]{:S(2)}, u32[]{:S(2)}) collective-permute-start(bf16[2,256,128]{2,1,0:T(8,128)(2,1)S(1)} %bitcast.15), channel_id=1, source_target_pairs={{64,0},{128,64},{192,128},{0,192},{65,1},{129,65},{193,129},{1,193... | collective-permute-start | bytes 393224 | tf_op jit(solution)/shard_map/ppermute | solution.py:388
  17.8 2.8 %copy-start.9 = (bf16[2,256,128]{2,1,0:T(8,128)(2,1)}, bf16[2,256,128]{2,1,0:T(8,128)(2,1)S(1)}, u32[]{:S(2)}) copy-start(bf16[2,256,128]{2,1,0:T(8,128)(2,1)S(1)} %collective-permute-done.2.q3) | copy-start | bytes 393220
  20.2 0.7 copy-start.10
  20.6 0.7 copy-start.11
  21.2 15.0 %copy-start.1 = (s32[4]{0:T(128)S(1)}, s32[4]{0:T(128)}, u32[]{:S(2)}) copy-start(s32[4]{0:T(128)} %pad_add_fusion.place_ref) | copy-start | bytes 52
  21.2 15.0 %copy-start.4 = (s32[16]{0:T(128)S(1)}, s32[16]{0:T(128)}, u32[]{:S(2)}) copy-start(s32[16]{0:T(128)} %trace_ref.3) | copy-start | bytes 196
  21.2 15.0 %copy-start.7 = (s32[16]{0:T(128)S(1)}, s32[16]{0:T(128)}, u32[]{:S(2)}) copy-start(s32[16]{0:T(128)} %length_ref.1) | copy-start | bytes 196
  26.1 26.1 %collective-permute-start.3 = (bf16[128,2048]{1,0:T(8,128)(2,1)}, bf16[128,2048]{1,0:T(8,128)(2,1)S(1)}, u32[]{:S(2)}, u32[]{:S(2)}) collective-permute-start(bf16[128,2048]{1,0:T(8,128)(2,1)} %get-tuple-element.20), channel_id=1, source_target_pairs={{64,0},{128,64},{192,128},{0,192},{65,1},{129,65},{193,129},{1,193... | collective-permute-start | bytes 1572872 | tf_op jit(solution)/shard_map/ppermute | solution.py:388
  28.8 23.4 %collective-permute-start.4 = (bf16[128,2048]{1,0:T(8,128)(2,1)}, bf16[128,2048]{1,0:T(8,128)(2,1)S(1)}, u32[]{:S(2)}, u32[]{:S(2)}) collective-permute-start(bf16[128,2048]{1,0:T(8,128)(2,1)} %get-tuple-element.21), channel_id=1, source_target_pairs={{128,0},{192,64},{0,128},{64,192},{129,1},{193,65},{1,129},{65,193... | collective-permute-start | bytes 1572872 | tf_op jit(solution)/shard_map/ppermute | solution.py:388
  29.9 25.4 %collective-permute-start.5 = (bf16[128,2048]{1,0:T(8,128)(2,1)}, bf16[128,2048]{1,0:T(8,128)(2,1)}, u32[]{:S(2)}, u32[]{:S(2)}) collective-permute-start(bf16[128,2048]{1,0:T(8,128)(2,1)} %get-tuple-element.22), channel_id=1, source_target_pairs={{192,0},{0,64},{64,128},{128,192},{193,1},{1,65},{65,129},{129,193... | collective-permute-start | bytes 1572872 | tf_op jit(solution)/shard_map/ppermute | solution.py:388
  36.2 1.0 copy-start.5
  37.2 0.9 copy-start.6
  46.7 29.0 %copy-start = (bf16[256,2048]{1,0:T(8,128)(2,1)S(1)}, bf16[256,2048]{1,0:T(8,128)(2,1)}, u32[]{:S(2)}) copy-start(bf16[256,2048]{1,0:T(8,128)(2,1)} %get-tuple-element.24.weight_ref) | copy-start | bytes 3145732
  46.7 14.4 %all-to-all-start.1 = ((bf16[4,544,128]{2,1,0:T(8,128)(2,1)}), bf16[4,544,128]{2,1,0:T(8,128)(2,1)S(1)}, u32[]{:S(2)}, u32[]{:S(2)}) async-start(bf16[4,544,128]{2,1,0:T(8,128)(2,1)} %shard_map.97), calls=%async_computation.1 | async-start | bytes 1114112 | tf_op jit(solution)/shard_map/all_to_all | solution.py:391
  61.0 14.6 %collective-permute-start.6 = (bf16[128,2048]{1,0:T(8,128)(2,1)S(1)}, bf16[128,2048]{1,0:T(8,128)(2,1)S(1)}, u32[]{:S(2)}, u32[]{:S(2)}) collective-permute-start(bf16[128,2048]{1,0:T(8,128)(2,1)S(1)} %collective-permute-done.3.refs_0_), channel_id=1, source_target_pairs={{0,8},{8,0},{16,24},{24,16},{32,40},{40,32},{48,56},{56,48},{1,9},... | collective-permute-start | bytes 1572872 | tf_op jit(solution)/shard_map/ppermute | solution.py:394
  61.0 14.6 %collective-permute-start.7 = (bf16[128,2048]{1,0:T(8,128)(2,1)S(1)}, bf16[128,2048]{1,0:T(8,128)(2,1)S(1)}, u32[]{:S(2)}, u32[]{:S(2)}) collective-permute-start(bf16[128,2048]{1,0:T(8,128)(2,1)S(1)} %collective-permute-done.4.refs_2_), channel_id=1, source_target_pairs={{0,8},{8,0},{16,24},{24,16},{32,40},{40,32},{48,56},{56,48},{1,9},... | collective-permute-start | bytes 1572872 | tf_op jit(solution)/shard_map/ppermute | solution.py:394
  61.5 14.1 %collective-permute-start.8 = (bf16[128,2048]{1,0:T(8,128)(2,1)}, bf16[128,2048]{1,0:T(8,128)(2,1)S(1)}, u32[]{:S(2)}, u32[]{:S(2)}) collective-permute-start(bf16[128,2048]{1,0:T(8,128)(2,1)} %collective-permute-done.5.refs_4_), channel_id=1, source_target_pairs={{0,8},{8,0},{16,24},{24,16},{32,40},{40,32},{48,56},{56,48},{1,9},... | collective-permute-start | bytes 1572872 | tf_op jit(solution)/shard_map/ppermute | solution.py:394
  79.2 35.5 %copy-start.2 = (s32[2,16]{1,0:T(2,128)S(1)}, s32[2,16]{1,0:T(2,128)}, u32[]{:S(2)}) copy-start(s32[2,16]{1,0:T(2,128)} %bound_ref.1) | copy-start | bytes 388
  79.3 35.5 %copy-start.3 = (f32[256]{0:T(256)S(1)}, f32[256]{0:T(256)}, u32[]{:S(2)}) copy-start(f32[256]{0:T(256)} %param.15) | copy-start | bytes 3076

commit v3 on v2

--- a/solution.py
+++ b/solution.py
@@ -26,7 +26,10 @@
     return pl.CostEstimate(flops=flops, bytes_accessed=moved, transcendentals=exps)
 
 
-def order_kernel(place_ref, trace_ref, cache_ref, out_ref, held, wide, ordered, sems, out_sems):
+def order_kernel(
+    place_ref, trace_ref, cache_ref, query_ref, reward_ref, out_ref, leaving_ref,
+    held, wide, ordered, laid, sems, out_sems, own_sems,
+):
     traces, rows, size = held.shape
     groups = out_ref.shape[0]
     slots = traces // groups
@@ -36,6 +39,12 @@
     ]
     for copy in copies:
         copy.start()
+    query_rows = query_ref.shape[0]
+    query_copy = pltpu.make_async_copy(query_ref, laid.at[pl.ds(0, query_rows), :], own_sems.at[0])
+    query_copy.start()
+    pieces = split_three(reward_ref[...])
+    pieces = [piece[half : half + 1, :] for half in range(2) for piece in pieces]
+    laid[pl.ds(query_rows, EXTRA), :] = rows_of((EXTRA, size), pieces).astype(jnp.bfloat16)
     pending = []
     for n, copy in enumerate(copies):
         copy.wait()
@@ -50,35 +59,43 @@
                 pltpu.make_async_copy(ordered.at[group], out_ref.at[group], out_sems.at[group])
             )
             pending[-1].start()
+        if n == traces // 2:
+            query_copy.wait()
+            pending.append(pltpu.make_async_copy(laid, leaving_ref, own_sems.at[1]))
+            pending[-1].start()
     for copy in pending:
         copy.wait()
 
 
-def order_blocks(place, slot_trace, prior_rows, groups):
+def order_blocks(place, slot_trace, prior_rows, queries, reward, groups):
     traces, rows, size = prior_rows.shape
     ordered = (groups, traces // groups * rows, size)
+    laid = (queries.shape[0] + EXTRA, size)
     return pl.pallas_call(
         order_kernel,
-        out_shape=jax.ShapeDtypeStruct(ordered, jnp.bfloat16),
-        in_specs=[SMEM, SMEM, HBM],
-        out_specs=HBM,
+        out_shape=[
+            jax.ShapeDtypeStruct(ordered, jnp.bfloat16),
+            jax.ShapeDtypeStruct(laid, jnp.bfloat16),
+        ],
+        in_specs=[SMEM, SMEM, HBM, HBM, VMEM],
+        out_specs=[HBM, HBM],
         scratch_shapes=[
             pltpu.VMEM((traces, rows, size), jnp.bfloat16),
             pltpu.VMEM((2, rows, size), jnp.float32),
             pltpu.VMEM(ordered, jnp.bfloat16),
+            pltpu.VMEM(laid, jnp.bfloat16),
             pltpu.SemaphoreType.DMA((traces,)),
             pltpu.SemaphoreType.DMA((groups,)),
+            pltpu.SemaphoreType.DMA((2,)),
         ],
         compiler_params=kernel_params(LARGE),
         cost_estimate=cost(0, 4 * traces * rows * size),
-    )(place, slot_trace, prior_rows)
-
-
-def stage_kernel(
-    place_ref, weight_ref, q0, q1, q2, q3, fresh_ref, packed_ref, new_ref, own_ref, *refs
-):
-    outs, (staged, kept, wide, in_sems, out_sems) = refs[:-5], refs[-5:]
-    pools = len(outs) + 1
+    )(place, slot_trace, prior_rows, queries, reward)
+
+
+def stage_kernel(place_ref, weight_ref, *refs):
+    outs, (staged, kept, in_sems, out_sems) = refs[-8:-4], refs[-4:]
+    pools = len(outs)
     size, columns = outs[0].shape
     arriving = []
     for o in range(1, pools):
@@ -92,18 +109,10 @@
     arriving.append(pltpu.make_async_copy(own, kept, in_sems.at[0]))
     for copy in arriving:
         copy.start()
-    for n, ref in enumerate((q0, q1, q2, q3)):
-        packed_ref[n] = ref[...]
-    for slot in range(fresh_ref.shape[0]):
-        wide[...] = fresh_ref[slot].astype(jnp.float32)
-        for kind in range(2):
-            part = wide[pl.ds(kind, wide.shape[0] // 2, stride=2), :]
-            new_ref[slot, kind] = part.astype(jnp.bfloat16)
+    sources = [staged.at[n] for n in range(pools - 1)] + [kept]
     leaving = [
         pltpu.make_async_copy(source, out, out_sems.at[n])
-        for n, (source, out) in enumerate(
-            [(staged.at[n], out) for n, out in enumerate(outs)] + [(kept, own_ref)]
-        )
+        for n, (source, out) in enumerate(zip(sources, outs))
     ]
     for n, copy in enumerate(leaving):
         arriving[n].wait()
@@ -112,35 +121,108 @@
         copy.wait()
 
 
-def stage(place, weight, queried, fresh):
-    pools = len(queried)
-    slots, rows, size = fresh.shape
+def stage(place, weight, pools, behind):
     block = (weight.shape[0] // 2, weight.shape[1] // pools)
     kept = (weight.shape[0], block[1])
     return pl.pallas_call(
         stage_kernel,
-        out_shape=[
-            jax.ShapeDtypeStruct((pools, *queried[0].shape), jnp.bfloat16),
-            jax.ShapeDtypeStruct((slots, 2, rows // 2, size), jnp.bfloat16),
-            jax.ShapeDtypeStruct(kept, jnp.bfloat16),
-        ]
-        + [jax.ShapeDtypeStruct(block, jnp.bfloat16)] * (pools - 1),
-        in_specs=[SMEM, HBM] + [VMEM] * (pools + 1),
-        out_specs=[VMEM] * 2 + [HBM] * pools,
+        out_shape=[jax.ShapeDtypeStruct(block, jnp.bfloat16)] * (pools - 1)
+        + [jax.ShapeDtypeStruct(kept, jnp.bfloat16)],
+        in_specs=[SMEM, HBM, HBM],
+        out_specs=[HBM] * pools,
         scratch_shapes=[
             pltpu.VMEM((pools - 1, *block), jnp.bfloat16),
             pltpu.VMEM(kept, jnp.bfloat16),
-            pltpu.VMEM((rows, size), jnp.float32),
             pltpu.SemaphoreType.DMA((pools,)),
             pltpu.SemaphoreType.DMA((pools,)),
         ],
         compiler_params=kernel_params(LARGE),
         cost_estimate=cost(0, 8 * pools * block[0] * block[1]),
-    )(place, weight, *queried, fresh)
+    )(place, weight, behind)
+
+
+def pack_kernel(
+    place_ref, q0, q1, q2, q3, fresh_ref, behind_ref, packed_ref, new_ref, head_ref, wide
+):
+    slots, rows = packed_ref.shape[1:3]
+    head_ref[...] = jnp.zeros_like(head_ref)
+    found = []
+    for n, ref in enumerate((q0, q1, q2, q3)):
+        for slot in range(slots):
+            packed_ref[n, slot] = ref[pl.ds(slot * rows, rows), :]
+        pieces = ref[pl.ds(slots * rows, EXTRA), :].astype(jnp.float32)
+        found += [three_rows(pieces, half) for half in range(2)]
+    count = len(found)
+    at = pl.ds(pl.multiple_of(place_ref[TP] * count, count), count)
+    head_ref[at, :] = rows_of((count, wide.shape[1]), found)
+    for slot in range(slots):
+        wide[...] = fresh_ref[slot].astype(jnp.float32)
+        for kind in range(2):
+            part = wide[pl.ds(kind, wide.shape[0] // 2, stride=2), :]
+            new_ref[slot, kind] = part.astype(jnp.bfloat16)
+
+
+def pack(place, queried, fresh, behind, tps):
+    pools = len(queried)
+    slots, rows, size = fresh.shape
+    per_slot = (queried[0].shape[0] - EXTRA) // slots
+    return pl.pallas_call(
+        pack_kernel,
+        out_shape=[
+            jax.ShapeDtypeStruct((pools, slots, per_slot, size), jnp.bfloat16),
+            jax.ShapeDtypeStruct((slots, 2, rows // 2, size), jnp.bfloat16),
+            jax.ShapeDtypeStruct((tps * pools * 2, size), jnp.float32),
+        ],
+        in_specs=[SMEM] + [VMEM] * (pools + 1) + [HBM],
+        out_specs=[VMEM] * 3,
+        scratch_shapes=[pltpu.VMEM((rows, size), jnp.float32)],
+        compiler_params=kernel_params(8),
+        cost_estimate=cost(0, 4 * pools * slots * per_slot * size),
+    )(place, *queried, fresh, behind)
+
+
+def reward_rows_kernel(place_ref, weight_ref, head_ref, out_ref, weights, sems):
+    pools, rows, columns = weights.shape
+    size = out_ref.shape[1]
+    copies = []
+    for n in range(pools):
+        start = pl.multiple_of(lax.rem(place_ref[POOL] + n, pools) * columns, columns)
+        copies.append(
+            pltpu.make_async_copy(weight_ref.at[:, pl.ds(start, columns)], weights.at[n], sems.at[n])
+        )
+        copies[-1].start()
+    total = jnp.zeros((rows, size), jnp.float32)
+    for n, copy in enumerate(copies):
+        copy.wait()
+        for m in range(columns // size):
+            at = 2 * (m // 2 * pools + n) + m % 2
+            part = weights[n, :, pl.ds(m * size, size)].astype(jnp.float32)
+            total += part * head_ref[at : at + 1, :]
+    column = jnp.sum(total, -1, keepdims=True)
+    for n in range(rows // size):
+        row = jnp.broadcast_to(column[n * size : (n + 1) * size], (size, size)).T
+        out_ref[pl.ds(4 * n, 4), :] = row[:4]
+
+
+def reward_rows(place, weight_rows, head, pools):
+    rows, columns = weight_rows.shape
+    size = head.shape[1]
+    return pl.pallas_call(
+        reward_rows_kernel,
+        out_shape=jax.ShapeDtypeStruct((4 * rows // size, size), jnp.float32),
+        in_specs=[SMEM, HBM, VMEM],
+        out_specs=VMEM,
+        scratch_shapes=[
+            pltpu.VMEM((pools, rows, columns // pools), jnp.bfloat16),
+            pltpu.SemaphoreType.DMA((pools,)),
+        ],
+        compiler_params=kernel_params(LARGE),
+        cost_estimate=cost(16 * rows * columns, 2 * rows * columns),
+    )(place, weight_rows, head)
 
 
 def attend_kernel(
-    place_ref, trace_ref, length_ref, query_ref, new_ref, prior_ref, pay_ref
+    place_ref, trace_ref, length_ref, query_ref, new_ref, behind_ref, prior_ref, pay_ref
 ):
     pools, slots, rows, size = query_ref.shape
     sources, block = prior_ref.shape[0], prior_ref.shape[1] // (2 * slots)
@@ -148,16 +230,28 @@
     factor = size**-0.5 * log2_e
     contract = (((1,), (1,)), ((), ()))
     position = lax.broadcasted_iota(jnp.int32, (1, width), 1)
+
+    def keys_of(slot):
+        return prior_ref[:, pl.ds(2 * slot * block, block), :].reshape(width, size)
+
+    def scores_of(slot, tile):
+        return lax.dot_general(
+            query_ref[tile, slot], keys_of(slot), contract, preferred_element_type=jnp.float32
+        )
+
+    ahead = scores_of(0, 0)
     for slot in range(slots):
         valid = length_ref[trace_ref[place_ref[SLOT] + slot]] - place_ref[POOL] * width
         usable = position < valid
-        at = 2 * slot * block
-        keys = prior_ref[:, pl.ds(at, block), :].reshape(width, size)
-        values = prior_ref[:, pl.ds(at + block, block), :].reshape(width, size)
+        values = prior_ref[:, pl.ds((2 * slot + 1) * block, block), :].reshape(width, size)
         for tile in range(pools):
             pay = pay_ref.at[lax.rem(place_ref[POOL] + tile, pools)]
             query = query_ref[tile, slot]
-            scores = lax.dot_general(query, keys, contract, preferred_element_type=jnp.float32)
+            scores = ahead
+            if tile < pools - 1:
+                ahead = scores_of(slot, tile + 1)
+            elif slot < slots - 1:
+                ahead = scores_of(slot + 1, 0)
             scores = jnp.where(usable, scores, negative_fill)
             peak = jnp.max(scores, -1, keepdims=True)
             if tile == 0:
@@ -192,17 +286,17 @@
             )
 
 
-def attend(place, slot_trace, prefix_length, queries, new, prior):
+def attend(place, slot_trace, prefix_length, queries, new, behind, prior):
     pools, slots, rows, size = queries.shape
     width = prior.shape[0] * prior.shape[1] // (2 * slots)
     return pl.pallas_call(
         attend_kernel,
         out_shape=jax.ShapeDtypeStruct((pools, slots * (rows + EXTRA), size), jnp.bfloat16),
-        in_specs=[SMEM] * 3 + [VMEM] * 3,
+        in_specs=[SMEM] * 3 + [VMEM] * 4,
         out_specs=VMEM,
         compiler_params=kernel_params(24),
         cost_estimate=cost(32 * rows * width * size, 8 * width * size, 8 * rows * width),
-    )(place, slot_trace, prefix_length, queries, new, prior)
+    )(place, slot_trace, prefix_length, queries, new, behind, prior)
 
 
 def columns_of(shape, columns):
@@ -227,7 +321,7 @@
     return high, middle, value - high - middle
 
 
-def merge_kernel(pay_ref, out_ref, wide):
+def merge_kernel(pay_ref, seen_ref, out_ref, wide):
     rows, size = wide.shape
     heads = rows // size
     pools = out_ref.shape[0]
@@ -236,15 +330,15 @@
         peaks, totals = [], []
         for n in range(pools):
             stats = pay_ref[n, pl.ds(slots * rows + slot * EXTRA, EXTRA), :].astype(jnp.float32)
-            columns = jnp.concatenate(
+            laid = jnp.concatenate(
                 [
                     jnp.concatenate([stats[8 * half : 8 * half + 8]] * (size // 8), 0).T
                     for half in range(heads)
                 ],
                 0,
             )
-            peaks.append(columns[:, 0:1])
-            totals.append(columns[:, 1:2] + columns[:, 2:3])
+            peaks.append(laid[:, 0:1])
+            totals.append(laid[:, 1:2] + laid[:, 2:3])
         top = functools.reduce(jnp.maximum, peaks)
         shares = [jnp.exp2(peak - top) for peak in peaks]
         total = sum(share * part for share, part in zip(shares, totals))
@@ -257,26 +351,36 @@
             part = wide[pl.ds(head, size, stride=heads), :].astype(jnp.bfloat16)
             for n in range(pools):
                 out_ref[n, pl.ds(slot * rows + head * size, size), :] = part
-
-
-def merge(pays, slots):
+    rewards = []
+    for slot in range(slots):
+        reward = jnp.zeros((size, 1), jnp.float32)
+        for head in range(heads):
+            part = out_ref[0, pl.ds(slot * rows + head * size, size), :].astype(jnp.float32)
+            reward += jnp.sum(part * seen_ref[4 * head : 4 * head + 1, :], -1, keepdims=True)
+        rewards += split_three(reward)
+    laid = columns_of((size, size), rewards).T[:EXTRA].astype(jnp.bfloat16)
+    for n in range(pools):
+        out_ref[n, pl.ds(slots * rows, EXTRA), :] = laid
+
+
+def merge(pays, seen, slots):
     pools, rows, size = pays.shape
     rows = rows // slots - EXTRA
     return pl.pallas_call(
         merge_kernel,
-        out_shape=jax.ShapeDtypeStruct((pools, slots * rows, size), jnp.bfloat16),
-        in_specs=[VMEM],
+        out_shape=jax.ShapeDtypeStruct((pools, slots * rows + EXTRA, size), jnp.bfloat16),
+        in_specs=[VMEM] * 2,
         out_specs=VMEM,
         scratch_shapes=[pltpu.VMEM((rows, size), jnp.float32)],
         compiler_params=kernel_params(8),
         cost_estimate=cost(0, 20 * rows * size),
-    )(pays)
+    )(pays, seen)
 
 
 def project_kernel(place_ref, attended_ref, weight_ref, *refs):
-    moved, (out_ref, weights, sems) = refs[:-3], refs[-3:]
-    dests, wide = out_ref.shape[0], out_ref.shape[2]
-    pools, tokens, size = attended_ref.shape[0], out_ref.shape[1], attended_ref.shape[2]
+    outs, (weights, sems) = refs[-10:-2], refs[-2:]
+    moved, dests, wide = refs[:-10], len(outs), outs[0].shape[1]
+    pools, tokens, size = attended_ref.shape[0], outs[0].shape[0] - EXTRA, attended_ref.shape[2]
     slots = tokens // size
     columns = weights.shape[2]
     chunks = sems.shape[0]
@@ -304,27 +408,38 @@
             for at in range(0, 2 * slots * size, 2 * size)
         ]
         inputs.append(jnp.concatenate(rows, 0))
+    rewards = jnp.zeros((EXTRA, size), jnp.float32)
+    for n in range(pools):
+        rewards += attended_ref[n, pl.ds(2 * tokens, EXTRA), :].astype(jnp.float32)
+    pieces = []
+    for slot in range(slots):
+        pieces += split_three(three_rows(rewards, slot))
+    laid = rows_of((EXTRA, size), pieces)
+    laid = jnp.concatenate([laid, jnp.zeros_like(laid)], 1).astype(jnp.bfloat16)
+    for out in outs:
+        out[pl.ds(tokens, EXTRA), :] = laid
     for chunk in range(chunks):
         for copy in copies[chunk]:
             copy.wait()
-        for dest in range(chunk * dests // chunks, (chunk + 1) * dests // chunks):
-            at = pl.ds(dest * wide, wide)
-            total = jnp.dot(inputs[0], weights[0, :, at], preferred_element_type=jnp.float32)
-            for n in range(1, pools):
-                total += jnp.dot(inputs[n], weights[n, :, at], preferred_element_type=jnp.float32)
-            out_ref[dest] = total.astype(jnp.bfloat16)
+    for o, out in enumerate(outs):
+        dest = lax.rem(place_ref[TP] + o, dests)
+        at = pl.ds(pl.multiple_of(dest * wide, wide), wide)
+        total = jnp.dot(inputs[0], weights[0, :, at], preferred_element_type=jnp.float32)
+        for n in range(1, pools):
+            total += jnp.dot(inputs[n], weights[n, :, at], preferred_element_type=jnp.float32)
+        out[pl.ds(0, tokens), :] = total.astype(jnp.bfloat16)
 
 
 def project(place, attended, weight, moved, dests):
     pools, rows, size = attended.shape
-    tokens = rows // 2
+    tokens = (rows - EXTRA) // 2
     columns = moved[0].shape[1]
-    chunks = 4
+    chunks = 1
     return pl.pallas_call(
         project_kernel,
-        out_shape=jax.ShapeDtypeStruct((dests, tokens, columns // dests), jnp.bfloat16),
+        out_shape=[jax.ShapeDtypeStruct((tokens + EXTRA, columns // dests), jnp.bfloat16)] * dests,
         in_specs=[SMEM, VMEM] + [HBM] * (1 + len(moved)),
-        out_specs=VMEM,
+        out_specs=[VMEM] * dests,
         scratch_shapes=[
             pltpu.VMEM((pools, weight.shape[0], columns), jnp.bfloat16),
             pltpu.SemaphoreType.DMA((chunks, 1 + len(moved))),
@@ -334,35 +449,41 @@
     )(place, attended, weight, *moved)
 
 
-def finish_kernel(arrived_ref, bound_ref, reward_ref, out_ref, spread_ref):
+def three_rows(array, slot):
+    return sum(array[3 * slot + n : 3 * slot + n + 1] for n in range(3))
+
+
+def finish_kernel(*refs):
+    arrived, (bound_ref, out_ref, reward_ref) = refs[:-3], refs[-3:]
     slots, tokens, wide = out_ref.shape
     steps = bound_ref.shape[1]
+    rewards = jnp.zeros((EXTRA, wide), jnp.float32)
+    for ref in arrived:
+        rewards += ref[pl.ds(slots * tokens, EXTRA), :].astype(jnp.float32)
     for slot in range(slots):
         total = jnp.zeros((tokens, wide), jnp.float32)
-        for n in range(arrived_ref.shape[0]):
-            total += arrived_ref[n, pl.ds(slot * tokens, tokens), :].astype(jnp.float32)
+        for ref in arrived:
+            total += ref[pl.ds(slot * tokens, tokens), :].astype(jnp.float32)
         out_ref[slot] = total.astype(jnp.bfloat16)
-        rounded = out_ref[slot].astype(jnp.float32)
-        row = jnp.sum(rounded * reward_ref[...], -1, keepdims=True)
+        row = jnp.broadcast_to(three_rows(rewards, slot)[:, :tokens], (tokens, tokens)).T[:, :steps]
         lane = lax.broadcasted_iota(jnp.int32, (tokens, steps), 0)
-        chosen = jnp.sum(jnp.where(lane == bound_ref[slot : slot + 1, :], row, 0.0), 0, keepdims=True)
-        for n in range(spread_ref.shape[0]):
-            spread_ref[n, slot : slot + 1, :] = chosen
-
-
-def finish(arrived, boundaries, reward, spread):
+        chosen = jnp.where(lane == bound_ref[slot : slot + 1, :], row, 0.0)
+        reward_ref[slot : slot + 1, :] = jnp.sum(chosen, 0, keepdims=True)
+
+
+def finish(arrived, boundaries):
     slots, steps = boundaries.shape
-    _, rows, wide = arrived.shape
+    rows, wide = arrived[0].shape
     return pl.pallas_call(
         finish_kernel,
         out_shape=[
-            jax.ShapeDtypeStruct((slots, rows // slots, wide), jnp.bfloat16),
-            jax.ShapeDtypeStruct((spread, slots, steps), jnp.float32),
-        ],
-        in_specs=[VMEM] * 3,
+            jax.ShapeDtypeStruct((slots, (rows - EXTRA) // slots, wide), jnp.bfloat16),
+            jax.ShapeDtypeStruct((slots, steps), jnp.float32),
+        ],
+        in_specs=[VMEM] * (1 + len(arrived)),
         out_specs=[VMEM] * 2,
         compiler_params=kernel_params(8),
-    )(arrived, boundaries, reward)
+    )(*arrived, boundaries)
 
 
 def shards(
@@ -382,7 +503,7 @@
     place = jnp.stack([seq * slots, pool, lax.rem(seq, 2), tp]).astype(jnp.int32)
     rows_all = output_weight.reshape(pair * size, -1)
     prior_rows = prior_cache.reshape(traces, 2 * block, size)
-    own_queries = queries.reshape(slots, new_len * pair, size)
+    own_queries = queries.reshape(slots * new_len * pair, size)
 
     def from_pool(array, offset):
         return lax.ppermute(array, "pool", [((n + offset) % pools, n) for n in range(pools)])
@@ -393,22 +514,33 @@
     def swap_core(array):
         return lax.ppermute(array, "seq", [(n, n ^ 1) for n in range(seqs)])
 
-    sent = order_blocks(place, slot_trace, prior_rows, seqs)
-    sent, own_queries = lax.optimization_barrier((sent, own_queries))
+    sent, own = order_blocks(
+        place, slot_trace, prior_rows, own_queries, reward_weight.reshape(-1, size), seqs
+    )
     prior = turn(sent, "seq")
 
-    queried = [own_queries] + [from_pool(own_queries, o) for o in range(1, pools)]
+    queried = [own] + [from_pool(own, o) for o in range(1, pools)]
+    *leaving, kept = stage(place, rows_all, pools, own)
+    came = [from_pool(part, o) for o, part in enumerate(leaving, 1)]
     fresh = new_token_cache.reshape(slots, 2 * new_len, size)
-    packed, new, kept, *leaving = stage(place, rows_all, queried, fresh)
-    came = [from_pool(part, o) for o, part in enumerate(leaving, 1)]
-    pays = attend(place, slot_trace, prefix_length, packed, new, prior)
+    packed, new, head = pack(place, queried, fresh, kept, tps)
+
+    step = 1
+    while step < tps:
+        head = head + lax.ppermute(head, "tp", [(n, n ^ step) for n in range(tps)])
+        step *= 2
+    seen = reward_rows(place, rows_all, head, pools)
+
+    pays = attend(place, slot_trace, prefix_length, packed, new, seen, prior)
     pays, came = lax.optimization_barrier((turn(pays, "pool"), came))
     moved = [part for got in came for part in (got, swap_core(got))]
-    gathered = turn(merge(pays, slots), "pool")
+    gathered = turn(merge(pays, seen, slots), "pool")
     partial = project(place, gathered, kept, moved, tps)
-    arrived = turn(partial, "tp")
-    layer_out, spread = finish(arrived, boundaries, reward_weight.reshape(1, -1), pools * tps)
-    return (layer_out, jnp.sum(turn(spread, ("pool", "tp")), 0))
+    arrived = [partial[0]] + [
+        lax.ppermute(partial[o], "tp", [(n, (n + o) % tps) for n in range(tps)])
+        for o in (4, 3, 5, 2, 6, 1, 7)
+    ]
+    return tuple(finish(arrived, boundaries))
 
 
 def solution(mesh):

time: 130 us -> 121 us (0.931)
  blocking collectives: 61.1 us -> 13 us
  starting transfers between devices: 18.6 us -> 42.6 us
  waiting for transfers between devices: 22.4 us -> 33.2 us
  Pallas kernels: 22.3 us -> 24.8 us
    all_to_all x3 -> x1, blocking collectives: 61.1 us -> 13 us  [turn(): return lax.all_to_all(array, axes, split_axis=0, concat_axis=0, tiled=True)]
    ppermute x0 -> x10, starting transfers between devices: none -> 23.3 us  [the longest x7 12 us: shards(): lax.ppermute(partial[o], 'tp', [(n, (n + o) % tps) for n in range(tps)])]
    ppermute x0 -> x10, waiting for transfers between devices: none -> 21.6 us  [the longest x7 17.4 us: shards(): lax.ppermute(partial[o], 'tp', [(n, (n + o) % tps) for n in range(tps)])]
    all_to_all x2, waiting for transfers between devices: 12.1 us -> 5.32 us  [turn(): return lax.all_to_all(array, axes, split_axis=0, concat_axis=0, tiled=True)]
    ppermute x6, waiting for transfers between devices: 10.2 us -> 6.22 us  [from_pool(): lax.ppermute(array, 'pool', [((n + offset) % pools, n) for n in range(poo...]
    pallas_call x4 -> x6, Pallas kernels: 12.6 us -> 15.7 us  [the longest x1 4.03 us: reward_rows(): pl.pallas_call(reward_rows_kernel, out_shape=jax.ShapeDtypeStruct((4 * ro...]
    unnamed x24 -> x28, local copies, waits for them, and re-layouts: 2.63 us -> 3.74 us
  transfers between devices with their start and end apart: 11 -> 21, of which waited for: 7 -> 12; matrix products, arithmetic and copies ran while one was open for 0% -> 1% of each run, Pallas kernels for 11% -> 14%
where the time goes in v3:
time: 121 us; the launch traced here: 119 us
  starting transfers between devices  42.6 us (35%)
  waiting for transfers between devices  33.2 us (27%)
  Pallas kernels  24.8 us (20%)
  blocking collectives  13 us (11%)
  local copies, waits for them, and re-layouts  3.74 us (3%)
  other arithmetic  1.24 us (1%)
    ppermute x7, waiting for transfers between devices, shards(): lax.ppermute(partial[o], 'tp', [(n, (n + o) % tps) for n in range(tps)])  17.4 us
    all_to_all x1, blocking collectives, turn(): return lax.all_to_all(array, axes, split_axis=0, concat_axis=0, tiled=True)  13 us
    ppermute x7, starting transfers between devices, shards(): lax.ppermute(partial[o], 'tp', [(n, (n + o) % tps) for n in range(tps)])  12 us
    ppermute x3, starting transfers between devices, shards(): head = head + lax.ppermute(head, 'tp', [(n, n ^ step) for n in range(tps)])  11.3 us
    all_to_all x2, starting transfers between devices, turn(): return lax.all_to_all(array, axes, split_axis=0, concat_axis=0, tiled=True)  9.8 us
    ppermute x6, starting transfers between devices, from_pool(): lax.ppermute(array, 'pool', [((n + offset) % pools, n) for n in range(poo...  8.95 us
    pallas_call x1, Pallas kernels, attend(): pl.pallas_call(attend_kernel, out_shape=jax.ShapeDtypeStruct((pools, slot...  7.72 us
    ppermute x6, waiting for transfers between devices, from_pool(): lax.ppermute(array, 'pool', [((n + offset) % pools, n) for n in range(poo...  6.22 us
  transfers between devices with their start and end apart: 21, of which 12 were waited for; matrix products, arithmetic and copies ran while one was open for 1% of the time, Pallas kernels for 14%

profile of v3, /device:TPU:8, one launch (start us, length us, event | category | flops | bytes accessed | tf_op | source)
XLA Modules:
  0.0 119.3 jit_solution(16239762594367240112)
XLA Ops:
  0.6 0.6 pad_add_fusion.place_ref
  1.2 3.5 %shard_map.95 = (bf16[8,1024,128]{2,1,0:T(8,128)(2,1)}, bf16[528,128]{1,0:T(8,128)(2,1)}) custom-call(s32[4]{0:T(128)} %pad_add_fusion.place_ref, s32[16]{0:T(128)} %trace_ref.3, bf16[16,512,128]{2,1,0:T(8,128)(2,1)} %bitcast.12, bf16[512,128]{1,0:T(8,128)(2,1)} %bitcast.13, f32[2,128]{1,0:T(2,128)} %bitcast.14), custom_call_target="tpu_custom_call" | custom-call | bytes 4194304 | tf_op jit(solution)/shard_map/pallas_call | solution.py:74
  4.8 5.8 %all-to-all-start = ((bf16[8,1024,128]{2,1,0:T(8,128)(2,1)}), bf16[8,1024,128]{2,1,0:T(8,128)(2,1)S(1)}, u32[]{:S(2)}, u32[]{:S(2)}) async-start(bf16[8,1024,128]{2,1,0:T(8,128)(2,1)} %get-tuple-element.28), calls=%async_computation | async-start | bytes 4194304 | tf_op jit(solution)/shard_map/all_to_all | solution.py:512
  10.6 0.7 collective-permute-start.2
  11.3 2.7 %collective-permute-start.1 = (bf16[528,128]{1,0:T(8,128)(2,1)S(1)}, bf16[528,128]{1,0:T(8,128)(2,1)S(1)}, u32[]{:S(2)}, u32[]{:S(2)}) collective-permute-start(bf16[528,128]{1,0:T(8,128)(2,1)S(1)} %copy-done.2), channel_id=1, source_target_pairs={{128,0},{192,64},{0,128},{64,192},{129,1},{193,65},{1,129},{65,193... | collective-permute-start | bytes 405512 | tf_op jit(solution)/shard_map/ppermute | solution.py:509
  14.0 1.4 %collective-permute-start = (bf16[528,128]{1,0:T(8,128)(2,1)S(1)}, bf16[528,128]{1,0:T(8,128)(2,1)S(1)}, u32[]{:S(2)}, u32[]{:S(2)}) collective-permute-start(bf16[528,128]{1,0:T(8,128)(2,1)S(1)} %copy-done.2), channel_id=1, source_target_pairs={{64,0},{128,64},{192,128},{0,192},{65,1},{129,65},{193,129},{1,193... | collective-permute-start | bytes 405512 | tf_op jit(solution)/shard_map/ppermute | solution.py:509
  15.5 3.6 %shard_map.96 = (bf16[128,2048]{1,0:T(8,128)(2,1)}, bf16[128,2048]{1,0:T(8,128)(2,1)}, bf16[128,2048]{1,0:T(8,128)(2,1)}, bf16[256,2048]{1,0:T(8,128)(2,1)}) custom-call(s32[4]{0:T(128)} %pad_add_fusion.place_ref, bf16[256,8192]{1,0:T(8,128)(2,1)} %bitcast.10, bf16[528,128]{1,0:T(8,128)(2,1)} %get-tuple-element.23.refs_0_.q0), custom_call_target="tpu_custom_call" | custom-call | bytes 8388608 | tf_op jit(solution)/shard_map/pallas_call | solution.py:127
  19.1 1.5 %collective-permute-done.1.q2 = bf16[528,128]{1,0:T(8,128)(2,1)S(1)} collective-permute-done((bf16[528,128]{1,0:T(8,128)(2,1)S(1)}, bf16[528,128]{1,0:T(8,128)(2,1)S(1)}, u32[]{:S(2)}, u32[]{:S(2)}) %collective-permute-start.1) | collective-permute-done | bytes 135200 | tf_op jit(solution)/shard_map/ppermute | solution.py:509
  20.5 0.4 collective-permute-done.q1
  20.9 1.2 %copy-done = bf16[256,2048]{1,0:T(8,128)(2,1)S(1)} copy-done((bf16[256,2048]{1,0:T(8,128)(2,1)S(1)}, bf16[256,2048]{1,0:T(8,128)(2,1)}, u32[]{:S(2)}) %copy-start) | copy-done | bytes 1048600
  22.2 0.6 shard_map.97
  22.8 0.8 copy-done.11
  23.6 1.6 %collective-permute-start.3 = (f32[64,128]{1,0:T(8,128)S(1)}, f32[64,128]{1,0:T(8,128)S(1)}, u32[]{:S(2)}, u32[]{:S(2)}) collective-permute-start(f32[64,128]{1,0:T(8,128)S(1)} %get-tuple-element.27), channel_id=1, source_target_pairs={{0,1},{1,0},{2,3},{3,2},{4,5},{5,4},{6,7},{7,6},{8,9},{9,8},{10,11... | collective-permute-start | bytes 98312 | tf_op jit(solution)/shard_map/ppermute | solution.py:530
  25.1 2.4 %collective-permute-done.3 = f32[64,128]{1,0:T(8,128)S(1)} collective-permute-done((f32[64,128]{1,0:T(8,128)S(1)}, f32[64,128]{1,0:T(8,128)S(1)}, u32[]{:S(2)}, u32[]{:S(2)}) %collective-permute-start.3) | collective-permute-done | bytes 32800 | tf_op jit(solution)/shard_map/ppermute | solution.py:530
  27.5 2.9 %collective-permute-start.4 = (f32[64,128]{1,0:T(8,128)S(1)}, f32[64,128]{1,0:T(8,128)S(1)}, u32[]{:S(2)}, u32[]{:S(2)}) collective-permute-start(f32[64,128]{1,0:T(8,128)S(1)} %add.9), channel_id=1, source_target_pairs={{0,2},{1,3},{2,0},{3,1},{4,6},{5,7},{6,4},{7,5},{8,10},{9,11},{10,... | collective-permute-start | bytes 98312 | tf_op jit(solution)/shard_map/ppermute | solution.py:530
  30.4 1.9 %collective-permute-done.4 = f32[64,128]{1,0:T(8,128)S(1)} collective-permute-done((f32[64,128]{1,0:T(8,128)S(1)}, f32[64,128]{1,0:T(8,128)S(1)}, u32[]{:S(2)}, u32[]{:S(2)}) %collective-permute-start.4) | collective-permute-done | bytes 32800 | tf_op jit(solution)/shard_map/ppermute | solution.py:530
  32.3 6.8 %collective-permute-start.5 = (f32[64,128]{1,0:T(8,128)S(1)}, f32[64,128]{1,0:T(8,128)S(1)}, u32[]{:S(2)}, u32[]{:S(2)}) collective-permute-start(f32[64,128]{1,0:T(8,128)S(1)} %add.10), channel_id=1, source_target_pairs={{0,4},{1,5},{2,6},{3,7},{4,0},{5,1},{6,2},{7,3},{8,12},{9,13},{10,... | collective-permute-start | bytes 98312 | tf_op jit(solution)/shard_map/ppermute | solution.py:530
  39.1 2.3 %collective-permute-start.6 = (bf16[128,2048]{1,0:T(8,128)(2,1)}, bf16[128,2048]{1,0:T(8,128)(2,1)S(1)}, u32[]{:S(2)}, u32[]{:S(2)}) collective-permute-start(bf16[128,2048]{1,0:T(8,128)(2,1)} %get-tuple-element.29), channel_id=1, source_target_pairs={{64,0},{128,64},{192,128},{0,192},{65,1},{129,65},{193,129},{1,193... | collective-permute-start | bytes 1572872 | tf_op jit(solution)/shard_map/ppermute | solution.py:509
  41.4 1.1 collective-permute-start.7
  42.5 0.7 collective-permute-start.8
  43.2 0.0 collective-permute-done.5
  43.2 0.6 add.11.head_ref
  43.8 4.0 %shard_map.98.behind_ref.seen_ref = f32[8,128]{1,0:T(8,128)} custom-call(s32[4]{0:T(128)} %pad_add_fusion.place_ref, bf16[256,8192]{1,0:T(8,128)(2,1)} %bitcast.11, f32[64,128]{1,0:T(8,128)} %add.11.head_ref), custom_call_target="tpu_custom_call" | custom-call | flops 33554432 | bytes 4194304 | tf_op jit(solution)/shard_map/pallas_call | solution.py:210
  47.9 0.0 all-to-all-done.prior_ref
  47.9 0.7 copy-done.7
  48.6 1.0 copy-done.12
  49.6 7.7 %shard_map.99 = bf16[4,544,128]{2,1,0:T(8,128)(2,1)} custom-call(s32[4]{0:T(128)S(1)} %copy-done.6, s32[16]{0:T(128)S(1)} %copy-done.10, s32[16]{0:T(128)S(1)} %copy-done.13, bf16[4,2,256,128]{3,2,1,0:T(8,128)(2,1)S(1)} %copy-done.12, bf16[2,2,128,128]{3,2,1,0:T(8,128)(2,1)S(1)} %get-tuple-element.26.new_ref, f32[8,128]{1,0:T(8,128)S(1)} %copy-done.7, ...), custom_call_target="tpu_custom_call" | custom-call | flops 2147483648 | bytes 2097152 | tf_op jit(solution)/shard_map/pallas_call | solution.py:292
  57.4 4.0 %all-to-all-start.1 = ((bf16[4,544,128]{2,1,0:T(8,128)(2,1)}), bf16[4,544,128]{2,1,0:T(8,128)(2,1)S(1)}, u32[]{:S(2)}, u32[]{:S(2)}) async-start(bf16[4,544,128]{2,1,0:T(8,128)(2,1)} %shard_map.99), calls=%async_computation.1 | async-start | bytes 1114112 | tf_op jit(solution)/shard_map/all_to_all | solution.py:512
  61.3 0.3 collective-permute-done.6.refs_0_
  61.6 4.1 %collective-permute-done.8.refs_4_ = bf16[128,2048]{1,0:T(8,128)(2,1)} collective-permute-done((bf16[128,2048]{1,0:T(8,128)(2,1)}, bf16[128,2048]{1,0:T(8,128)(2,1)}, u32[]{:S(2)}, u32[]{:S(2)}) %collective-permute-start.8) | collective-permute-done | bytes 524320 | tf_op jit(solution)/shard_map/ppermute | solution.py:509
  65.7 5.3 %all-to-all-done.1.pay_ref = bf16[4,544,128]{2,1,0:T(8,128)(2,1)S(1)} async-done(((bf16[4,544,128]{2,1,0:T(8,128)(2,1)}), bf16[4,544,128]{2,1,0:T(8,128)(2,1)S(1)}, u32[]{:S(2)}, u32[]{:S(2)}) %all-to-all-start.1) | async-done | bytes 557088 | tf_op jit(solution)/shard_map/all_to_all | solution.py:512
  71.0 0.5 collective-permute-start.10
  71.5 0.0 collective-permute-start.11
  71.5 1.4 %shard_map.100 = bf16[4,528,128]{2,1,0:T(8,128)(2,1)S(1)} custom-call(bf16[4,544,128]{2,1,0:T(8,128)(2,1)S(1)} %all-to-all-done.1.pay_ref, f32[8,128]{1,0:T(8,128)S(1)} %copy-done.8), custom_call_target="tpu_custom_call" | custom-call | bytes 655360 | tf_op jit(solution)/shard_map/pallas_call | solution.py:369
  72.8 13.0 %all_to_all.15.attended_ref = bf16[4,528,128]{2,1,0:T(8,128)(2,1)S(1)} all-to-all(bf16[4,528,128]{2,1,0:T(8,128)(2,1)S(1)} %shard_map.100), channel_id=1, replica_groups=mesh['pool'=4,'seq'=8,'tp'=8] {'pool'}, dimensions={0} | all-to-all | bytes 1081344 | tf_op jit(solution)/shard_map/all_to_all | solution.py:512
  85.9 3.2 %shard_map.101 = (bf16[272,256]{1,0:T(8,128)(2,1)S(1)}, bf16[272,256]{1,0:T(8,128)(2,1)S(1)}, bf16[272,256]{1,0:T(8,128)(2,1)S(1)}, bf16[272,256]{1,0:T(8,128)(2...) custom-call(s32[4]{0:T(128)S(1)} %copy-done.6, ...), custom_call_target="tpu_custom_call" | custom-call | flops 1073741824 | bytes 4194304 | tf_op jit(solution)/shard_map/pallas_call | solution.py:438
  89.0 2.5 %collective-permute-start.12 = (bf16[272,256]{1,0:T(8,128)(2,1)S(1)}, bf16[272,256]{1,0:T(8,128)(2,1)S(1)}, u32[]{:S(2)}, u32[]{:S(2)}) collective-permute-start(bf16[272,256]{1,0:T(8,128)(2,1)S(1)} %get-tuple-element.37), channel_id=1, source_target_pairs={{0,4},{1,5},{2,6},{3,7},{4,0},{5,1},{6,2},{7,3},{8,12},{9,13},{10,... | collective-permute-start | bytes 417800 | tf_op jit(solution)/shard_map/ppermute | solution.py:540
  91.5 2.6 %collective-permute-start.13 = (bf16[272,256]{1,0:T(8,128)(2,1)S(1)}, bf16[272,256]{1,0:T(8,128)(2,1)S(1)}, u32[]{:S(2)}, u32[]{:S(2)}) collective-permute-start(bf16[272,256]{1,0:T(8,128)(2,1)S(1)} %get-tuple-element.38), channel_id=1, source_target_pairs={{0,3},{1,4},{2,5},{3,6},{4,7},{5,0},{6,1},{7,2},{8,11},{9,12},{10,... | collective-permute-start | bytes 417800 | tf_op jit(solution)/shard_map/ppermute | solution.py:540
  94.2 2.4 %collective-permute-start.14 = (bf16[272,256]{1,0:T(8,128)(2,1)S(1)}, bf16[272,256]{1,0:T(8,128)(2,1)S(1)}, u32[]{:S(2)}, u32[]{:S(2)}) collective-permute-start(bf16[272,256]{1,0:T(8,128)(2,1)S(1)} %get-tuple-element.39), channel_id=1, source_target_pairs={{0,5},{1,6},{2,7},{3,0},{4,1},{5,2},{6,3},{7,4},{8,13},{9,14},{10,... | collective-permute-start | bytes 417800 | tf_op jit(solution)/shard_map/ppermute | solution.py:540
  96.6 1.6 %collective-permute-start.15 = (bf16[272,256]{1,0:T(8,128)(2,1)S(1)}, bf16[272,256]{1,0:T(8,128)(2,1)S(1)}, u32[]{:S(2)}, u32[]{:S(2)}) collective-permute-start(bf16[272,256]{1,0:T(8,128)(2,1)S(1)} %get-tuple-element.40), channel_id=1, source_target_pairs={{0,2},{1,3},{2,4},{3,5},{4,6},{5,7},{6,0},{7,1},{8,10},{9,11},{10,... | collective-permute-start | bytes 417800 | tf_op jit(solution)/shard_map/ppermute | solution.py:540
  98.2 2.5 %collective-permute-start.16 = (bf16[272,256]{1,0:T(8,128)(2,1)S(1)}, bf16[272,256]{1,0:T(8,128)(2,1)S(1)}, u32[]{:S(2)}, u32[]{:S(2)}) collective-permute-start(bf16[272,256]{1,0:T(8,128)(2,1)S(1)} %get-tuple-element.41), channel_id=1, source_target_pairs={{0,6},{1,7},{2,0},{3,1},{4,2},{5,3},{6,4},{7,5},{8,14},{9,15},{10,... | collective-permute-start | bytes 417800 | tf_op jit(solution)/shard_map/ppermute | solution.py:540
  100.7 4.3 %collective-permute-done.12.refs_1_ = bf16[272,256]{1,0:T(8,128)(2,1)S(1)} collective-permute-done((bf16[272,256]{1,0:T(8,128)(2,1)S(1)}, bf16[272,256]{1,0:T(8,128)(2,1)S(1)}, u32[]{:S(2)}, u32[]{:S(2)}) %collective-permute-start.12) | collective-permute-done | bytes 139296 | tf_op jit(solution)/shard_map/ppermute | solution.py:540
  105.0 6.8 %collective-permute-done.13.refs_2_ = bf16[272,256]{1,0:T(8,128)(2,1)S(1)} collective-permute-done((bf16[272,256]{1,0:T(8,128)(2,1)S(1)}, bf16[272,256]{1,0:T(8,128)(2,1)S(1)}, u32[]{:S(2)}, u32[]{:S(2)}) %collective-permute-start.13) | collective-permute-done | bytes 139296 | tf_op jit(solution)/shard_map/ppermute | solution.py:540
  111.8 0.3 collective-permute-start.18
  112.1 4.3 %collective-permute-done.15.refs_4_ = bf16[272,256]{1,0:T(8,128)(2,1)S(1)} collective-permute-done((bf16[272,256]{1,0:T(8,128)(2,1)S(1)}, bf16[272,256]{1,0:T(8,128)(2,1)S(1)}, u32[]{:S(2)}, u32[]{:S(2)}) %collective-permute-start.15) | collective-permute-done | bytes 139296 | tf_op jit(solution)/shard_map/ppermute | solution.py:540
  116.4 1.9 %collective-permute-done.17.refs_6_ = bf16[272,256]{1,0:T(8,128)(2,1)S(1)} collective-permute-done((bf16[272,256]{1,0:T(8,128)(2,1)S(1)}, bf16[272,256]{1,0:T(8,128)(2,1)S(1)}, u32[]{:S(2)}, u32[]{:S(2)}) %collective-permute-start.17) | collective-permute-done | bytes 139296 | tf_op jit(solution)/shard_map/ppermute | solution.py:540
  118.3 0.1 collective-permute-done.18.refs_7_
  118.4 0.9 shard_map.102
  (35 shorter events, 0.1 us)
Async XLA Ops:
  4.7 5.9 %copy-start.2 = (bf16[528,128]{1,0:T(8,128)(2,1)S(1)}, bf16[528,128]{1,0:T(8,128)(2,1)}, u32[]{:S(2)}) copy-start(bf16[528,128]{1,0:T(8,128)(2,1)} %get-tuple-element.23.refs_0_.q0) | copy-start | bytes 405508
  4.8 43.1 %all-to-all-start = ((bf16[8,1024,128]{2,1,0:T(8,128)(2,1)}), bf16[8,1024,128]{2,1,0:T(8,128)(2,1)S(1)}, u32[]{:S(2)}, u32[]{:S(2)}) async-start(bf16[8,1024,128]{2,1,0:T(8,128)(2,1)} %get-tuple-element.28), calls=%async_computation | async-start | bytes 4194304 | tf_op jit(solution)/shard_map/all_to_all | solution.py:512
  10.6 8.4 %collective-permute-start.2 = (bf16[528,128]{1,0:T(8,128)(2,1)S(1)}, bf16[528,128]{1,0:T(8,128)(2,1)S(1)}, u32[]{:S(2)}, u32[]{:S(2)}) collective-permute-start(bf16[528,128]{1,0:T(8,128)(2,1)S(1)} %copy-done.2), channel_id=1, source_target_pairs={{192,0},{0,64},{64,128},{128,192},{193,1},{1,65},{65,129},{129,193... | collective-permute-start | bytes 405512 | tf_op jit(solution)/shard_map/ppermute | solution.py:509
  11.3 9.2 %collective-permute-start.1 = (bf16[528,128]{1,0:T(8,128)(2,1)S(1)}, bf16[528,128]{1,0:T(8,128)(2,1)S(1)}, u32[]{:S(2)}, u32[]{:S(2)}) collective-permute-start(bf16[528,128]{1,0:T(8,128)(2,1)S(1)} %copy-done.2), channel_id=1, source_target_pairs={{128,0},{192,64},{0,128},{64,192},{129,1},{193,65},{1,129},{65,193... | collective-permute-start | bytes 405512 | tf_op jit(solution)/shard_map/ppermute | solution.py:509
  14.0 6.9 %collective-permute-start = (bf16[528,128]{1,0:T(8,128)(2,1)S(1)}, bf16[528,128]{1,0:T(8,128)(2,1)S(1)}, u32[]{:S(2)}, u32[]{:S(2)}) collective-permute-start(bf16[528,128]{1,0:T(8,128)(2,1)S(1)} %copy-done.2), channel_id=1, source_target_pairs={{64,0},{128,64},{192,128},{0,192},{65,1},{129,65},{193,129},{1,193... | collective-permute-start | bytes 405512 | tf_op jit(solution)/shard_map/ppermute | solution.py:509
  15.5 5.5 %copy-start.3 = (bf16[528,128]{1,0:T(8,128)(2,1)S(1)}, bf16[528,128]{1,0:T(8,128)(2,1)}, u32[]{:S(2)}) copy-start(bf16[528,128]{1,0:T(8,128)(2,1)} %get-tuple-element.23.refs_0_.q0) | copy-start | bytes 405508
  15.5 5.5 %copy-start.4 = (bf16[2,128,1,2,128]{4,3,2,1,0:T(2,128)(2,1)S(1)}, bf16[2,128,1,2,128]{4,3,2,1,0:T(2,128)(2,1)}, u32[]{:S(2)}) copy-start(bf16[2,128,1,2,128]{4,3,2,1,0:T(2,128)(2,1)} %param.12) | copy-start | bytes 393220
  15.5 5.5 %copy-start.5 = (s32[4]{0:T(128)S(1)}, s32[4]{0:T(128)}, u32[]{:S(2)}) copy-start(s32[4]{0:T(128)} %pad_add_fusion.place_ref) | copy-start | bytes 52
  20.9 1.2 %copy-start = (bf16[256,2048]{1,0:T(8,128)(2,1)S(1)}, bf16[256,2048]{1,0:T(8,128)(2,1)}, u32[]{:S(2)}) copy-start(bf16[256,2048]{1,0:T(8,128)(2,1)} %get-tuple-element.24.behind_ref.weight_ref) | copy-start | bytes 3145732
  22.8 0.8 copy-start.11
  23.6 3.9 %collective-permute-start.3 = (f32[64,128]{1,0:T(8,128)S(1)}, f32[64,128]{1,0:T(8,128)S(1)}, u32[]{:S(2)}, u32[]{:S(2)}) collective-permute-start(f32[64,128]{1,0:T(8,128)S(1)} %get-tuple-element.27), channel_id=1, source_target_pairs={{0,1},{1,0},{2,3},{3,2},{4,5},{5,4},{6,7},{7,6},{8,9},{9,8},{10,11... | collective-permute-start | bytes 98312 | tf_op jit(solution)/shard_map/ppermute | solution.py:530
  27.5 4.8 %collective-permute-start.4 = (f32[64,128]{1,0:T(8,128)S(1)}, f32[64,128]{1,0:T(8,128)S(1)}, u32[]{:S(2)}, u32[]{:S(2)}) collective-permute-start(f32[64,128]{1,0:T(8,128)S(1)} %add.9), channel_id=1, source_target_pairs={{0,2},{1,3},{2,0},{3,1},{4,6},{5,7},{6,4},{7,5},{8,10},{9,11},{10,... | collective-permute-start | bytes 98312 | tf_op jit(solution)/shard_map/ppermute | solution.py:530
  32.3 10.9 %collective-permute-start.5 = (f32[64,128]{1,0:T(8,128)S(1)}, f32[64,128]{1,0:T(8,128)S(1)}, u32[]{:S(2)}, u32[]{:S(2)}) collective-permute-start(f32[64,128]{1,0:T(8,128)S(1)} %add.10), channel_id=1, source_target_pairs={{0,4},{1,5},{2,6},{3,7},{4,0},{5,1},{6,2},{7,3},{8,12},{9,13},{10,... | collective-permute-start | bytes 98312 | tf_op jit(solution)/shard_map/ppermute | solution.py:530
  39.1 22.5 %collective-permute-start.6 = (bf16[128,2048]{1,0:T(8,128)(2,1)}, bf16[128,2048]{1,0:T(8,128)(2,1)S(1)}, u32[]{:S(2)}, u32[]{:S(2)}) collective-permute-start(bf16[128,2048]{1,0:T(8,128)(2,1)} %get-tuple-element.29), channel_id=1, source_target_pairs={{64,0},{128,64},{192,128},{0,192},{65,1},{129,65},{193,129},{1,193... | collective-permute-start | bytes 1572872 | tf_op jit(solution)/shard_map/ppermute | solution.py:509
  41.4 20.2 %collective-permute-start.7 = (bf16[128,2048]{1,0:T(8,128)(2,1)}, bf16[128,2048]{1,0:T(8,128)(2,1)S(1)}, u32[]{:S(2)}, u32[]{:S(2)}) collective-permute-start(bf16[128,2048]{1,0:T(8,128)(2,1)} %get-tuple-element.30), channel_id=1, source_target_pairs={{128,0},{192,64},{0,128},{64,192},{129,1},{193,65},{1,129},{65,193... | collective-permute-start | bytes 1572872 | tf_op jit(solution)/shard_map/ppermute | solution.py:509
  42.5 23.1 %collective-permute-start.8 = (bf16[128,2048]{1,0:T(8,128)(2,1)}, bf16[128,2048]{1,0:T(8,128)(2,1)}, u32[]{:S(2)}, u32[]{:S(2)}) collective-permute-start(bf16[128,2048]{1,0:T(8,128)(2,1)} %get-tuple-element.31), channel_id=1, source_target_pairs={{192,0},{0,64},{64,128},{128,192},{193,1},{1,65},{65,129},{129,193... | collective-permute-start | bytes 1572872 | tf_op jit(solution)/shard_map/ppermute | solution.py:509
  43.8 4.1 %copy-start.6 = (s32[4]{0:T(128)S(1)}, s32[4]{0:T(128)}, u32[]{:S(2)}) copy-start(s32[4]{0:T(128)} %pad_add_fusion.place_ref) | copy-start | bytes 52
  43.8 4.1 %copy-start.10 = (s32[16]{0:T(128)S(1)}, s32[16]{0:T(128)}, u32[]{:S(2)}) copy-start(s32[16]{0:T(128)} %trace_ref.3) | copy-start | bytes 196
  43.8 4.1 %copy-start.13 = (s32[16]{0:T(128)S(1)}, s32[16]{0:T(128)}, u32[]{:S(2)}) copy-start(s32[16]{0:T(128)} %length_ref.1) | copy-start | bytes 196
  47.9 0.7 copy-start.7
  48.6 1.0 copy-start.12
  49.6 21.9 %copy-start.8 = (f32[8,128]{1,0:T(8,128)S(1)}, f32[8,128]{1,0:T(8,128)}, u32[]{:S(2)}) copy-start(f32[8,128]{1,0:T(8,128)} %shard_map.98.behind_ref.seen_ref) | copy-start | bytes 12292
  57.4 28.5 %copy-start.1 = (bf16[256,2048]{1,0:T(8,128)(2,1)S(1)}, bf16[256,2048]{1,0:T(8,128)(2,1)}, u32[]{:S(2)}) copy-start(bf16[256,2048]{1,0:T(8,128)(2,1)} %get-tuple-element.24.behind_ref.weight_ref) | copy-start | bytes 3145732
  57.4 13.6 %all-to-all-start.1 = ((bf16[4,544,128]{2,1,0:T(8,128)(2,1)}), bf16[4,544,128]{2,1,0:T(8,128)(2,1)S(1)}, u32[]{:S(2)}, u32[]{:S(2)}) async-start(bf16[4,544,128]{2,1,0:T(8,128)(2,1)} %shard_map.99), calls=%async_computation.1 | async-start | bytes 1114112 | tf_op jit(solution)/shard_map/all_to_all | solution.py:512
  71.0 14.8 %collective-permute-start.9 = (bf16[128,2048]{1,0:T(8,128)(2,1)S(1)}, bf16[128,2048]{1,0:T(8,128)(2,1)S(1)}, u32[]{:S(2)}, u32[]{:S(2)}) collective-permute-start(bf16[128,2048]{1,0:T(8,128)(2,1)S(1)} %collective-permute-done.6.refs_0_), channel_id=1, source_target_pairs={{0,8},{8,0},{16,24},{24,16},{32,40},{40,32},{48,56},{56,48},{1,9},... | collective-permute-start | bytes 1572872 | tf_op jit(solution)/shard_map/ppermute | solution.py:515
  71.0 14.8 %collective-permute-start.10 = (bf16[128,2048]{1,0:T(8,128)(2,1)S(1)}, bf16[128,2048]{1,0:T(8,128)(2,1)S(1)}, u32[]{:S(2)}, u32[]{:S(2)}) collective-permute-start(bf16[128,2048]{1,0:T(8,128)(2,1)S(1)} %collective-permute-done.7.refs_2_), channel_id=1, source_target_pairs={{0,8},{8,0},{16,24},{24,16},{32,40},{40,32},{48,56},{56,48},{1,9},... | collective-permute-start | bytes 1572872 | tf_op jit(solution)/shard_map/ppermute | solution.py:515
  71.5 14.3 %collective-permute-start.11 = (bf16[128,2048]{1,0:T(8,128)(2,1)}, bf16[128,2048]{1,0:T(8,128)(2,1)S(1)}, u32[]{:S(2)}, u32[]{:S(2)}) collective-permute-start(bf16[128,2048]{1,0:T(8,128)(2,1)} %collective-permute-done.8.refs_4_), channel_id=1, source_target_pairs={{0,8},{8,0},{16,24},{24,16},{32,40},{40,32},{48,56},{56,48},{1,9},... | collective-permute-start | bytes 1572872 | tf_op jit(solution)/shard_map/ppermute | solution.py:515
  85.8 32.6 %copy-start.9 = (s32[2,16]{1,0:T(2,128)S(1)}, s32[2,16]{1,0:T(2,128)}, u32[]{:S(2)}) copy-start(s32[2,16]{1,0:T(2,128)} %refs_8_.1) | copy-start | bytes 388
  89.0 16.0 %collective-permute-start.12 = (bf16[272,256]{1,0:T(8,128)(2,1)S(1)}, bf16[272,256]{1,0:T(8,128)(2,1)S(1)}, u32[]{:S(2)}, u32[]{:S(2)}) collective-permute-start(bf16[272,256]{1,0:T(8,128)(2,1)S(1)} %get-tuple-element.37), channel_id=1, source_target_pairs={{0,4},{1,5},{2,6},{3,7},{4,0},{5,1},{6,2},{7,3},{8,12},{9,13},{10,... | collective-permute-start | bytes 417800 | tf_op jit(solution)/shard_map/ppermute | solution.py:540
  91.5 20.2 %collective-permute-start.13 = (bf16[272,256]{1,0:T(8,128)(2,1)S(1)}, bf16[272,256]{1,0:T(8,128)(2,1)S(1)}, u32[]{:S(2)}, u32[]{:S(2)}) collective-permute-start(bf16[272,256]{1,0:T(8,128)(2,1)S(1)} %get-tuple-element.38), channel_id=1, source_target_pairs={{0,3},{1,4},{2,5},{3,6},{4,7},{5,0},{6,1},{7,2},{8,11},{9,12},{10,... | collective-permute-start | bytes 417800 | tf_op jit(solution)/shard_map/ppermute | solution.py:540
  94.2 17.9 %collective-permute-start.14 = (bf16[272,256]{1,0:T(8,128)(2,1)S(1)}, bf16[272,256]{1,0:T(8,128)(2,1)S(1)}, u32[]{:S(2)}, u32[]{:S(2)}) collective-permute-start(bf16[272,256]{1,0:T(8,128)(2,1)S(1)} %get-tuple-element.39), channel_id=1, source_target_pairs={{0,5},{1,6},{2,7},{3,0},{4,1},{5,2},{6,3},{7,4},{8,13},{9,14},{10,... | collective-permute-start | bytes 417800 | tf_op jit(solution)/shard_map/ppermute | solution.py:540
  96.6 19.8 %collective-permute-start.15 = (bf16[272,256]{1,0:T(8,128)(2,1)S(1)}, bf16[272,256]{1,0:T(8,128)(2,1)S(1)}, u32[]{:S(2)}, u32[]{:S(2)}) collective-permute-start(bf16[272,256]{1,0:T(8,128)(2,1)S(1)} %get-tuple-element.40), channel_id=1, source_target_pairs={{0,2},{1,3},{2,4},{3,5},{4,6},{5,7},{6,0},{7,1},{8,10},{9,11},{10,... | collective-permute-start | bytes 417800 | tf_op jit(solution)/shard_map/ppermute | solution.py:540
  98.2 18.2 %collective-permute-start.16 = (bf16[272,256]{1,0:T(8,128)(2,1)S(1)}, bf16[272,256]{1,0:T(8,128)(2,1)S(1)}, u32[]{:S(2)}, u32[]{:S(2)}) collective-permute-start(bf16[272,256]{1,0:T(8,128)(2,1)S(1)} %get-tuple-element.41), channel_id=1, source_target_pairs={{0,6},{1,7},{2,0},{3,1},{4,2},{5,3},{6,4},{7,5},{8,14},{9,15},{10,... | collective-permute-start | bytes 417800 | tf_op jit(solution)/shard_map/ppermute | solution.py:540
  105.0 13.3 %collective-permute-start.17 = (bf16[272,256]{1,0:T(8,128)(2,1)S(1)}, bf16[272,256]{1,0:T(8,128)(2,1)S(1)}, u32[]{:S(2)}, u32[]{:S(2)}) collective-permute-start(bf16[272,256]{1,0:T(8,128)(2,1)S(1)} %get-tuple-element.42), channel_id=1, source_target_pairs={{0,1},{1,2},{2,3},{3,4},{4,5},{5,6},{6,7},{7,0},{8,9},{9,10},{10,1... | collective-permute-start | bytes 417800 | tf_op jit(solution)/shard_map/ppermute | solution.py:540
  111.8 6.6 %collective-permute-start.18 = (bf16[272,256]{1,0:T(8,128)(2,1)S(1)}, bf16[272,256]{1,0:T(8,128)(2,1)S(1)}, u32[]{:S(2)}, u32[]{:S(2)}) collective-permute-start(bf16[272,256]{1,0:T(8,128)(2,1)S(1)} %get-tuple-element.43), channel_id=1, source_target_pairs={{0,7},{1,0},{2,1},{3,2},{4,3},{5,4},{6,5},{7,6},{8,15},{9,8},{10,9... | collective-permute-start | bytes 417800 | tf_op jit(solution)/shard_map/ppermute | solution.py:540

commit v4 on v3

--- a/solution.py
+++ b/solution.py
@@ -181,49 +181,18 @@
     )(place, *queried, fresh, behind)
 
 
-def reward_rows_kernel(place_ref, weight_ref, head_ref, out_ref, weights, sems):
-    pools, rows, columns = weights.shape
-    size = out_ref.shape[1]
+def attend_kernel(
+    place_ref, trace_ref, length_ref, query_ref, new_ref, prior_ref, weight_ref, head_ref,
+    pay_ref, seen_ref, held, sems,
+):
+    span = held.shape[2]
     copies = []
-    for n in range(pools):
-        start = pl.multiple_of(lax.rem(place_ref[POOL] + n, pools) * columns, columns)
+    for n in range(held.shape[0]):
+        start = pl.multiple_of(lax.rem(place_ref[POOL] + n, held.shape[0]) * span, span)
         copies.append(
-            pltpu.make_async_copy(weight_ref.at[:, pl.ds(start, columns)], weights.at[n], sems.at[n])
+            pltpu.make_async_copy(weight_ref.at[:, pl.ds(start, span)], held.at[n], sems.at[n])
         )
         copies[-1].start()
-    total = jnp.zeros((rows, size), jnp.float32)
-    for n, copy in enumerate(copies):
-        copy.wait()
-        for m in range(columns // size):
-            at = 2 * (m // 2 * pools + n) + m % 2
-            part = weights[n, :, pl.ds(m * size, size)].astype(jnp.float32)
-            total += part * head_ref[at : at + 1, :]
-    column = jnp.sum(total, -1, keepdims=True)
-    for n in range(rows // size):
-        row = jnp.broadcast_to(column[n * size : (n + 1) * size], (size, size)).T
-        out_ref[pl.ds(4 * n, 4), :] = row[:4]
-
-
-def reward_rows(place, weight_rows, head, pools):
-    rows, columns = weight_rows.shape
-    size = head.shape[1]
-    return pl.pallas_call(
-        reward_rows_kernel,
-        out_shape=jax.ShapeDtypeStruct((4 * rows // size, size), jnp.float32),
-        in_specs=[SMEM, HBM, VMEM],
-        out_specs=VMEM,
-        scratch_shapes=[
-            pltpu.VMEM((pools, rows, columns // pools), jnp.bfloat16),
-            pltpu.SemaphoreType.DMA((pools,)),
-        ],
-        compiler_params=kernel_params(LARGE),
-        cost_estimate=cost(16 * rows * columns, 2 * rows * columns),
-    )(place, weight_rows, head)
-
-
-def attend_kernel(
-    place_ref, trace_ref, length_ref, query_ref, new_ref, behind_ref, prior_ref, pay_ref
-):
     pools, slots, rows, size = query_ref.shape
     sources, block = prior_ref.shape[0], prior_ref.shape[1] // (2 * slots)
     width = sources * block
@@ -286,17 +255,37 @@
             )
 
 
-def attend(place, slot_trace, prefix_length, queries, new, behind, prior):
+    seen = jnp.zeros((held.shape[1], size), jnp.float32)
+    for n, copy in enumerate(copies):
+        copy.wait()
+        for m in range(span // size):
+            at = 2 * (m // 2 * pools + n) + m % 2
+            part = held[n, :, pl.ds(m * size, size)].astype(jnp.float32)
+            seen += part * head_ref[at : at + 1, :]
+    column = jnp.sum(seen, -1, keepdims=True)
+    for n in range(held.shape[1] // size):
+        row = jnp.broadcast_to(column[n * size : (n + 1) * size], (size, size)).T
+        seen_ref[pl.ds(4 * n, 4), :] = row[:4]
+
+
+def attend(place, slot_trace, prefix_length, queries, new, prior, weight, head):
     pools, slots, rows, size = queries.shape
     width = prior.shape[0] * prior.shape[1] // (2 * slots)
     return pl.pallas_call(
         attend_kernel,
-        out_shape=jax.ShapeDtypeStruct((pools, slots * (rows + EXTRA), size), jnp.bfloat16),
-        in_specs=[SMEM] * 3 + [VMEM] * 4,
-        out_specs=VMEM,
-        compiler_params=kernel_params(24),
+        out_shape=[
+            jax.ShapeDtypeStruct((pools, slots * (rows + EXTRA), size), jnp.bfloat16),
+            jax.ShapeDtypeStruct((4 * weight.shape[0] // size, size), jnp.float32),
+        ],
+        in_specs=[SMEM] * 3 + [VMEM] * 3 + [HBM, VMEM],
+        out_specs=[VMEM] * 2,
+        scratch_shapes=[
+            pltpu.VMEM((pools, weight.shape[0], weight.shape[1] // pools), jnp.bfloat16),
+            pltpu.SemaphoreType.DMA((pools,)),
+        ],
+        compiler_params=kernel_params(28),
         cost_estimate=cost(32 * rows * width * size, 8 * width * size, 8 * rows * width),
-    )(place, slot_trace, prefix_length, queries, new, behind, prior)
+    )(place, slot_trace, prefix_length, queries, new, prior, weight, head)
 
 
 def columns_of(shape, columns):
@@ -377,25 +366,25 @@
     )(pays, seen)
 
 
-def project_kernel(place_ref, attended_ref, weight_ref, *refs):
-    outs, (weights, sems) = refs[-10:-2], refs[-2:]
-    moved, dests, wide = refs[:-10], len(outs), outs[0].shape[1]
+def project_kernel(offsets, place_ref, attended_ref, weight_ref, *refs):
+    outs, (weights, sems) = refs[-2 - len(offsets) : -2], refs[-2:]
+    moved, wide = refs[: -2 - len(offsets)], outs[0].shape[1]
+    dests = weight_ref.shape[1] // wide
     pools, tokens, size = attended_ref.shape[0], outs[0].shape[0] - EXTRA, attended_ref.shape[2]
     slots = tokens // size
-    columns = weights.shape[2]
-    chunks = sems.shape[0]
-    span = columns // chunks
     core = place_ref[CORE]
     copies = []
-    for chunk in range(chunks):
-        at = pl.ds(chunk * span, span)
-        batch = [(weight_ref.at[:, at], weights.at[0, :, at])]
+    for i, o in enumerate(offsets):
+        dest = lax.rem(place_ref[TP] + o, dests)
+        start = pl.ds(pl.multiple_of(dest * wide, wide), wide)
+        at = pl.ds(i * wide, wide)
+        batch = [(weight_ref.at[:, start], weights.at[0, :, at])]
         for n, ref in enumerate(moved):
             half = core if n % 2 == 0 else 1 - core
             rows = pl.ds(pl.multiple_of(half * size, size), size)
-            batch.append((ref.at[pl.ds(0, size), at], weights.at[1 + n // 2, rows, at]))
+            batch.append((ref.at[pl.ds(0, size), start], weights.at[1 + n // 2, rows, at]))
         copies.append([
-            pltpu.make_async_copy(source, target, sems.at[chunk, n])
+            pltpu.make_async_copy(source, target, sems.at[i, n])
             for n, (source, target) in enumerate(batch)
         ])
         for copy in copies[-1]:
@@ -416,36 +405,33 @@
         pieces += split_three(three_rows(rewards, slot))
     laid = rows_of((EXTRA, size), pieces)
     laid = jnp.concatenate([laid, jnp.zeros_like(laid)], 1).astype(jnp.bfloat16)
-    for out in outs:
+    for i, out in enumerate(outs):
         out[pl.ds(tokens, EXTRA), :] = laid
-    for chunk in range(chunks):
-        for copy in copies[chunk]:
+        for copy in copies[i]:
             copy.wait()
-    for o, out in enumerate(outs):
-        dest = lax.rem(place_ref[TP] + o, dests)
-        at = pl.ds(pl.multiple_of(dest * wide, wide), wide)
+        at = pl.ds(i * wide, wide)
         total = jnp.dot(inputs[0], weights[0, :, at], preferred_element_type=jnp.float32)
         for n in range(1, pools):
             total += jnp.dot(inputs[n], weights[n, :, at], preferred_element_type=jnp.float32)
         out[pl.ds(0, tokens), :] = total.astype(jnp.bfloat16)
 
 
-def project(place, attended, weight, moved, dests):
+def project(place, attended, weight, moved, dests, offsets):
     pools, rows, size = attended.shape
     tokens = (rows - EXTRA) // 2
-    columns = moved[0].shape[1]
-    chunks = 1
-    return pl.pallas_call(
-        project_kernel,
-        out_shape=[jax.ShapeDtypeStruct((tokens + EXTRA, columns // dests), jnp.bfloat16)] * dests,
+    wide = weight.shape[1] // dests
+    count = len(offsets)
+    return pl.pallas_call(
+        functools.partial(project_kernel, offsets),
+        out_shape=[jax.ShapeDtypeStruct((tokens + EXTRA, wide), jnp.bfloat16)] * count,
         in_specs=[SMEM, VMEM] + [HBM] * (1 + len(moved)),
-        out_specs=[VMEM] * dests,
+        out_specs=[VMEM] * count,
         scratch_shapes=[
-            pltpu.VMEM((pools, weight.shape[0], columns), jnp.bfloat16),
-            pltpu.SemaphoreType.DMA((chunks, 1 + len(moved))),
+            pltpu.VMEM((pools, weight.shape[0], count * wide), jnp.bfloat16),
+            pltpu.SemaphoreType.DMA((count, 1 + len(moved))),
         ],
         compiler_params=kernel_params(16),
-        cost_estimate=cost(16 * tokens * size * columns, 16 * size * columns),
+        cost_estimate=cost(16 * tokens * size * count * wide, 16 * size * count * wide),
     )(place, attended, weight, *moved)
 
 
@@ -525,21 +511,22 @@
     fresh = new_token_cache.reshape(slots, 2 * new_len, size)
     packed, new, head = pack(place, queried, fresh, kept, tps)
 
-    step = 1
-    while step < tps:
-        head = head + lax.ppermute(head, "tp", [(n, n ^ step) for n in range(tps)])
-        step *= 2
-    seen = reward_rows(place, rows_all, head, pools)
-
-    pays = attend(place, slot_trace, prefix_length, packed, new, seen, prior)
-    pays, came = lax.optimization_barrier((turn(pays, "pool"), came))
+    near = [lax.ppermute(head, "tp", [(n, n ^ o) for n in range(tps)]) for o in (1, 2, 3)]
+    head = head + near[0] + near[1] + near[2]
+    head = head + lax.ppermute(head, "tp", [(n, n ^ 4) for n in range(tps)])
+
+    pays, seen = attend(
+        place, slot_trace, prefix_length, packed, new, prior, rows_all, head
+    )
+    pays, came = lax.optimization_barrier((pays, came))
     moved = [part for got in came for part in (got, swap_core(got))]
-    gathered = turn(merge(pays, seen, slots), "pool")
-    partial = project(place, gathered, kept, moved, tps)
-    arrived = [partial[0]] + [
-        lax.ppermute(partial[o], "tp", [(n, (n + o) % tps) for n in range(tps)])
-        for o in (4, 3, 5, 2, 6, 1, 7)
-    ]
+    gathered = turn(merge(turn(pays, "pool"), seen, slots), "pool")
+    arrived = []
+    for offsets in ((4, 3, 5), (2, 6, 1, 7, 0)):
+        for o, part in zip(offsets, project(place, gathered, kept, moved, tps, offsets)):
+            arrived.append(
+                lax.ppermute(part, "tp", [(n, (n + o) % tps) for n in range(tps)]) if o else part
+            )
     return tuple(finish(arrived, boundaries))
 
 

time: 121 us -> 114 us (0.942)
  blocking collectives: 13 us -> 0 us
  starting transfers between devices: 42.6 us -> 47.8 us
  Pallas kernels: 24.8 us -> 27.3 us
    all_to_all x1 -> x0, blocking collectives: 13 us -> none  [turn(): return lax.all_to_all(array, axes, split_axis=0, concat_axis=0, tiled=True)]
    all_to_all x2 -> x3, waiting for transfers between devices: 5.32 us -> 15.9 us  [turn(): return lax.all_to_all(array, axes, split_axis=0, concat_axis=0, tiled=True)]
    ppermute x10 -> x11, waiting for transfers between devices: 21.6 us -> 14.1 us  [the longest x7 6.63 us: shards(): lax.ppermute(part, 'tp', [(n, (n + o) % tps) for n in range(tps)])]
    all_to_all x2 -> x3, starting transfers between devices: 9.8 us -> 14.2 us  [turn(): return lax.all_to_all(array, axes, split_axis=0, concat_axis=0, tiled=True)]
    ppermute x6, waiting for transfers between devices: 6.22 us -> 2.54 us  [from_pool(): lax.ppermute(array, 'pool', [((n + offset) % pools, n) for n in range(poo...]
    pallas_call x3, Pallas kernels: 14.9 us -> 16.5 us  [the longest x1 9.87 us: attend(): pl.pallas_call(attend_kernel, out_shape=[jax.ShapeDtypeStruct((pools, slo...]
    ppermute x10 -> x11, starting transfers between devices: 23.3 us -> 24.9 us  [the longest x7 15.8 us: shards(): lax.ppermute(part, 'tp', [(n, (n + o) % tps) for n in range(tps)])]
    unnamed x28 -> x22, local copies, waits for them, and re-layouts: 3.74 us -> 4.24 us
  transfers between devices with their start and end apart: 21 -> 23, of which waited for: 12 -> 10; matrix products, arithmetic and copies ran while one was open for 1% -> 0% of each run, Pallas kernels for 14% -> 18%
where the time goes in v4:
time: 114 us; the launch traced here: 113 us
  starting transfers between devices  47.8 us (42%)
  waiting for transfers between devices  32.5 us (29%)
  Pallas kernels  27.3 us (24%)
  local copies, waits for them, and re-layouts  4.24 us (4%)
    all_to_all x3, waiting for transfers between devices, turn(): return lax.all_to_all(array, axes, split_axis=0, concat_axis=0, tiled=True)  15.9 us
    ppermute x7, starting transfers between devices, shards(): lax.ppermute(part, 'tp', [(n, (n + o) % tps) for n in range(tps)])  15.8 us
    all_to_all x3, starting transfers between devices, turn(): return lax.all_to_all(array, axes, split_axis=0, concat_axis=0, tiled=True)  14.2 us
    pallas_call x1, Pallas kernels, attend(): pl.pallas_call(attend_kernel, out_shape=[jax.ShapeDtypeStruct((pools, slo...  9.87 us
    ppermute x6, starting transfers between devices, from_pool(): lax.ppermute(array, 'pool', [((n + offset) % pools, n) for n in range(poo...  8.24 us
    pallas_call x2, Pallas kernels, project(): pl.pallas_call(functools.partial(project_kernel, offsets), out_shape=[jax...  6.67 us
    ppermute x7, waiting for transfers between devices, shards(): lax.ppermute(part, 'tp', [(n, (n + o) % tps) for n in range(tps)])  6.63 us
    ppermute x1, starting transfers between devices, shards(): head = head + lax.ppermute(head, 'tp', [(n, n ^ 4) for n in range(tps)])  4.79 us
  transfers between devices with their start and end apart: 23, of which 10 were waited for; matrix products, arithmetic and copies ran while one was open for 0% of the time, Pallas kernels for 18%

profile of v4, /device:TPU:8, one launch (start us, length us, event | category | flops | bytes accessed | tf_op | source)
XLA Modules:
  0.0 113.4 jit_solution(2984533751320068566)
XLA Ops:
  0.6 0.6 pad_add_fusion.place_ref
  1.3 3.5 %shard_map.95 = (bf16[8,1024,128]{2,1,0:T(8,128)(2,1)}, bf16[528,128]{1,0:T(8,128)(2,1)}) custom-call(s32[4]{0:T(128)} %pad_add_fusion.place_ref, s32[16]{0:T(128)} %trace_ref.3, bf16[16,512,128]{2,1,0:T(8,128)(2,1)} %bitcast.12, bf16[512,128]{1,0:T(8,128)(2,1)} %bitcast.13, f32[2,128]{1,0:T(2,128)} %bitcast.14), custom_call_target="tpu_custom_call" | custom-call | bytes 4194304 | tf_op jit(solution)/shard_map/pallas_call | solution.py:74
  4.8 6.5 %all-to-all-start = ((bf16[8,1024,128]{2,1,0:T(8,128)(2,1)}), bf16[8,1024,128]{2,1,0:T(8,128)(2,1)}, u32[]{:S(2)}, u32[]{:S(2)}) async-start(bf16[8,1024,128]{2,1,0:T(8,128)(2,1)} %get-tuple-element.29), calls=%async_computation | async-start | bytes 4194304 | tf_op jit(solution)/shard_map/all_to_all | solution.py:498
  11.4 2.7 %collective-permute-start.1 = (bf16[528,128]{1,0:T(8,128)(2,1)S(1)}, bf16[528,128]{1,0:T(8,128)(2,1)S(1)}, u32[]{:S(2)}, u32[]{:S(2)}) collective-permute-start(bf16[528,128]{1,0:T(8,128)(2,1)S(1)} %copy-done.4), channel_id=1, source_target_pairs={{128,0},{192,64},{0,128},{64,192},{129,1},{193,65},{1,129},{65,193... | collective-permute-start | bytes 405512 | tf_op jit(solution)/shard_map/ppermute | solution.py:495
  14.1 1.4 %collective-permute-start = (bf16[528,128]{1,0:T(8,128)(2,1)S(1)}, bf16[528,128]{1,0:T(8,128)(2,1)S(1)}, u32[]{:S(2)}, u32[]{:S(2)}) collective-permute-start(bf16[528,128]{1,0:T(8,128)(2,1)S(1)} %copy-done.4), channel_id=1, source_target_pairs={{64,0},{128,64},{192,128},{0,192},{65,1},{129,65},{193,129},{1,193... | collective-permute-start | bytes 405512 | tf_op jit(solution)/shard_map/ppermute | solution.py:495
  15.5 0.0 copy-start.10
  15.6 3.6 %shard_map.96 = (bf16[128,2048]{1,0:T(8,128)(2,1)}, bf16[128,2048]{1,0:T(8,128)(2,1)}, bf16[128,2048]{1,0:T(8,128)(2,1)}, bf16[256,2048]{1,0:T(8,128)(2,1)}) custom-call(s32[4]{0:T(128)} %pad_add_fusion.place_ref, bf16[256,8192]{1,0:T(8,128)(2,1)} %bitcast.9, bf16[528,128]{1,0:T(8,128)(2,1)} %get-tuple-element.25.refs_0_.q0), custom_call_target="tpu_custom_call" | custom-call | bytes 8388608 | tf_op jit(solution)/shard_map/pallas_call | solution.py:127
  19.2 2.0 %collective-permute-done.2.q3 = bf16[528,128]{1,0:T(8,128)(2,1)S(1)} collective-permute-done((bf16[528,128]{1,0:T(8,128)(2,1)S(1)}, bf16[528,128]{1,0:T(8,128)(2,1)S(1)}, u32[]{:S(2)}, u32[]{:S(2)}) %collective-permute-start.2) | collective-permute-done | bytes 135200 | tf_op jit(solution)/shard_map/ppermute | solution.py:495
  21.1 0.0 collective-permute-done.1.q2
  21.1 0.6 collective-permute-done.q1
  21.7 1.2 %copy-done = bf16[256,2048]{1,0:T(8,128)(2,1)S(1)} copy-done((bf16[256,2048]{1,0:T(8,128)(2,1)S(1)}, bf16[256,2048]{1,0:T(8,128)(2,1)}, u32[]{:S(2)}) %copy-start) | copy-done | bytes 1048600
  22.9 0.6 shard_map.97
  23.5 3.6 %collective-permute-start.5 = (f32[64,128]{1,0:T(8,128)S(1)}, f32[64,128]{1,0:T(8,128)S(1)}, u32[]{:S(2)}, u32[]{:S(2)}) collective-permute-start(f32[64,128]{1,0:T(8,128)S(1)} %get-tuple-element.30), channel_id=1, source_target_pairs={{0,3},{1,2},{2,1},{3,0},{4,7},{5,6},{6,5},{7,4},{8,11},{9,10},{10,... | collective-permute-start | bytes 98312 | tf_op jit(solution)/shard_map/ppermute | solution.py:514
  27.2 2.3 %collective-permute-start.7 = (bf16[128,2048]{1,0:T(8,128)(2,1)}, bf16[128,2048]{1,0:T(8,128)(2,1)S(1)}, u32[]{:S(2)}, u32[]{:S(2)}) collective-permute-start(bf16[128,2048]{1,0:T(8,128)(2,1)} %get-tuple-element.32), channel_id=1, source_target_pairs={{64,0},{128,64},{192,128},{0,192},{65,1},{129,65},{193,129},{1,193... | collective-permute-start | bytes 1572872 | tf_op jit(solution)/shard_map/ppermute | solution.py:495
  29.4 1.1 %collective-permute-start.8 = (bf16[128,2048]{1,0:T(8,128)(2,1)}, bf16[128,2048]{1,0:T(8,128)(2,1)S(1)}, u32[]{:S(2)}, u32[]{:S(2)}) collective-permute-start(bf16[128,2048]{1,0:T(8,128)(2,1)} %get-tuple-element.33), channel_id=1, source_target_pairs={{128,0},{192,64},{0,128},{64,192},{129,1},{193,65},{1,129},{65,193... | collective-permute-start | bytes 1572872 | tf_op jit(solution)/shard_map/ppermute | solution.py:495
  30.6 0.7 collective-permute-start.9
  31.3 0.0 collective-permute-start.4
  31.3 0.0 collective-permute-done.5
  31.3 0.7 collective-permute-start.3
  31.9 4.2 %collective-permute-done.4 = f32[64,128]{1,0:T(8,128)S(1)} collective-permute-done((f32[64,128]{1,0:T(8,128)S(1)}, f32[64,128]{1,0:T(8,128)S(1)}, u32[]{:S(2)}, u32[]{:S(2)}) %collective-permute-start.4) | collective-permute-done | bytes 32800 | tf_op jit(solution)/shard_map/ppermute | solution.py:514
  36.1 4.8 %collective-permute-start.6 = (f32[64,128]{1,0:T(8,128)S(1)}, f32[64,128]{1,0:T(8,128)S(1)}, u32[]{:S(2)}, u32[]{:S(2)}) collective-permute-start(f32[64,128]{1,0:T(8,128)S(1)} %add_add_fusion), channel_id=1, source_target_pairs={{0,4},{1,5},{2,6},{3,7},{4,0},{5,1},{6,2},{7,3},{8,12},{9,13},{10,... | collective-permute-start | bytes 98312 | tf_op jit(solution)/shard_map/ppermute | solution.py:516
  40.9 3.3 %collective-permute-done.6 = f32[64,128]{1,0:T(8,128)S(1)} collective-permute-done((f32[64,128]{1,0:T(8,128)S(1)}, f32[64,128]{1,0:T(8,128)S(1)}, u32[]{:S(2)}, u32[]{:S(2)}) %collective-permute-start.6) | collective-permute-done | bytes 32800 | tf_op jit(solution)/shard_map/ppermute | solution.py:516
  44.2 0.0 all-to-all-done.prior_ref
  44.2 0.0 copy-start.2
  44.2 2.2 %copy-done.2 = bf16[1,2,128,8192]{3,2,1,0:T(8,128)(2,1)S(1)} copy-done((bf16[1,2,128,8192]{3,2,1,0:T(8,128)(2,1)S(1)}, bf16[1,2,128,8192]{3,2,1,0:T(8,128)(2,1)}, u32[]{:S(2)}) %copy-start.2) | copy-done | bytes 4194328
  46.4 9.9 %shard_map.98 = (bf16[4,544,128]{2,1,0:T(8,128)(2,1)S(1)}, f32[8,128]{1,0:T(8,128)S(1)}) custom-call(s32[4]{0:T(128)S(1)} %copy-done.7, s32[16]{0:T(128)S(1)} %copy-done.9, s32[16]{0:T(128)S(1)} %copy-done.10, bf16[4,2,256,128]{3,2,1,0:T(8,128)(2,1)S(1)} %get-tuple-element.27.query_ref, bf16[2,2,128,128]{3,2,1,0:T(8,128)(2,1)S(1)} %get-tuple-element.28.new_ref, ...), custom_call_target="tpu_custom_call" | custom-call | flops 2147483648 | bytes 2097152 | tf_op jit(solution)/shard_map/pallas_call | solution.py:274
  56.3 0.8 copy-done.3
  57.1 0.0 collective-permute-done.9.refs_4_
  57.1 4.2 %all-to-all-start.1 = ((bf16[4,544,128]{2,1,0:T(8,128)(2,1)}), bf16[4,544,128]{2,1,0:T(8,128)(2,1)S(1)}, u32[]{:S(2)}, u32[]{:S(2)}) async-start(bf16[4,544,128]{2,1,0:T(8,128)(2,1)} %copy-done.3), calls=%async_computation.1 | async-start | bytes 1114112 | tf_op jit(solution)/shard_map/all_to_all | solution.py:498
  61.3 0.5 collective-permute-start.11
  61.8 7.7 %all-to-all-done.1.pay_ref = bf16[4,544,128]{2,1,0:T(8,128)(2,1)S(1)} async-done(((bf16[4,544,128]{2,1,0:T(8,128)(2,1)}), bf16[4,544,128]{2,1,0:T(8,128)(2,1)S(1)}, u32[]{:S(2)}, u32[]{:S(2)}) %all-to-all-start.1) | async-done | bytes 557088 | tf_op jit(solution)/shard_map/all_to_all | solution.py:498
  69.6 2.2 %shard_map.99 = bf16[4,528,128]{2,1,0:T(8,128)(2,1)} custom-call(bf16[4,544,128]{2,1,0:T(8,128)(2,1)S(1)} %all-to-all-done.1.pay_ref, f32[8,128]{1,0:T(8,128)S(1)} %get-tuple-element.36.seen_ref), custom_call_target="tpu_custom_call" | custom-call | bytes 655360 | tf_op jit(solution)/shard_map/pallas_call | solution.py:358
  71.7 3.5 %all-to-all-start.2 = ((bf16[4,528,128]{2,1,0:T(8,128)(2,1)}), bf16[4,528,128]{2,1,0:T(8,128)(2,1)S(1)}, u32[]{:S(2)}, u32[]{:S(2)}) async-start(bf16[4,528,128]{2,1,0:T(8,128)(2,1)} %shard_map.99), calls=%async_computation.2 | async-start | bytes 1081344 | tf_op jit(solution)/shard_map/all_to_all | solution.py:498
  75.3 8.1 %all-to-all-done.2.attended_ref = bf16[4,528,128]{2,1,0:T(8,128)(2,1)S(1)} async-done(((bf16[4,528,128]{2,1,0:T(8,128)(2,1)}), bf16[4,528,128]{2,1,0:T(8,128)(2,1)S(1)}, u32[]{:S(2)}, u32[]{:S(2)}) %all-to-all-start.2) | async-done | bytes 540704 | tf_op jit(solution)/shard_map/all_to_all | solution.py:498
  83.4 2.8 %shard_map.100 = (bf16[272,256]{1,0:T(8,128)(2,1)S(1)}, bf16[272,256]{1,0:T(8,128)(2,1)S(1)}, bf16[272,256]{1,0:T(8,128)(2,1)S(1)}) custom-call(s32[4]{0:T(128)S(1)} %copy-done.7, bf16[4,528,128]{2,1,0:T(8,128)(2,1)S(1)} %all-to-all-done.2.attended_ref, bf16[256,2048]{1,0:T(8,128)(2,1)S(1)} %copy-done.1, ...), custom_call_target="tpu_custom_call" | custom-call | flops 402653184 | bytes 1572864 | tf_op jit(solution)/shard_map/pallas_call | solution.py:424
  86.2 4.7 %collective-permute-start.13 = (bf16[272,256]{1,0:T(8,128)(2,1)S(1)}, bf16[272,256]{1,0:T(8,128)(2,1)S(1)}, u32[]{:S(2)}, u32[]{:S(2)}) collective-permute-start(bf16[272,256]{1,0:T(8,128)(2,1)S(1)} %get-tuple-element.40), channel_id=1, source_target_pairs={{0,4},{1,5},{2,6},{3,7},{4,0},{5,1},{6,2},{7,3},{8,12},{9,13},{10,... | collective-permute-start | bytes 417800 | tf_op jit(solution)/shard_map/ppermute | solution.py:528
  90.9 1.8 %collective-permute-start.14 = (bf16[272,256]{1,0:T(8,128)(2,1)S(1)}, bf16[272,256]{1,0:T(8,128)(2,1)S(1)}, u32[]{:S(2)}, u32[]{:S(2)}) collective-permute-start(bf16[272,256]{1,0:T(8,128)(2,1)S(1)} %get-tuple-element.41), channel_id=1, source_target_pairs={{0,3},{1,4},{2,5},{3,6},{4,7},{5,0},{6,1},{7,2},{8,11},{9,12},{10,... | collective-permute-start | bytes 417800 | tf_op jit(solution)/shard_map/ppermute | solution.py:528
  92.7 3.2 %collective-permute-start.15 = (bf16[272,256]{1,0:T(8,128)(2,1)S(1)}, bf16[272,256]{1,0:T(8,128)(2,1)S(1)}, u32[]{:S(2)}, u32[]{:S(2)}) collective-permute-start(bf16[272,256]{1,0:T(8,128)(2,1)S(1)} %get-tuple-element.42), channel_id=1, source_target_pairs={{0,5},{1,6},{2,7},{3,0},{4,1},{5,2},{6,3},{7,4},{8,13},{9,14},{10,... | collective-permute-start | bytes 417800 | tf_op jit(solution)/shard_map/ppermute | solution.py:528
  95.9 3.8 %shard_map.101 = (bf16[272,256]{1,0:T(8,128)(2,1)S(1)}, bf16[272,256]{1,0:T(8,128)(2,1)S(1)}, bf16[272,256]{1,0:T(8,128)(2,1)S(1)}, bf16[272,256]{1,0:T(8,128)(2,1)S(1)}, bf16[272,256]{1,0:T(8,128)(2,1)S(1)}) custom-call(s32[4]{0:T(128)S(1)} %copy-done.7, bf16[4,528,128]{2,1,0:T(8,128)(2,1)S(1)} %all-to-all-done.2.attended_ref, ...), custom_call_target="tpu_custom_call" | custom-call | flops 671088640 | bytes 2621440 | tf_op jit(solution)/shard_map/pallas_call | solution.py:424
  99.8 2.6 %collective-permute-start.16 = (bf16[272,256]{1,0:T(8,128)(2,1)S(1)}, bf16[272,256]{1,0:T(8,128)(2,1)S(1)}, u32[]{:S(2)}, u32[]{:S(2)}) collective-permute-start(bf16[272,256]{1,0:T(8,128)(2,1)S(1)} %get-tuple-element.43), channel_id=1, source_target_pairs={{0,2},{1,3},{2,4},{3,5},{4,6},{5,7},{6,0},{7,1},{8,10},{9,11},{10,... | collective-permute-start | bytes 417800 | tf_op jit(solution)/shard_map/ppermute | solution.py:528
  102.4 1.6 %collective-permute-start.17 = (bf16[272,256]{1,0:T(8,128)(2,1)S(1)}, bf16[272,256]{1,0:T(8,128)(2,1)S(1)}, u32[]{:S(2)}, u32[]{:S(2)}) collective-permute-start(bf16[272,256]{1,0:T(8,128)(2,1)S(1)} %get-tuple-element.44), channel_id=1, source_target_pairs={{0,6},{1,7},{2,0},{3,1},{4,2},{5,3},{6,4},{7,5},{8,14},{9,15},{10,... | collective-permute-start | bytes 417800 | tf_op jit(solution)/shard_map/ppermute | solution.py:528
  104.0 1.4 %collective-permute-start.18 = (bf16[272,256]{1,0:T(8,128)(2,1)S(1)}, bf16[272,256]{1,0:T(8,128)(2,1)S(1)}, u32[]{:S(2)}, u32[]{:S(2)}) collective-permute-start(bf16[272,256]{1,0:T(8,128)(2,1)S(1)} %get-tuple-element.45), channel_id=1, source_target_pairs={{0,1},{1,2},{2,3},{3,4},{4,5},{5,6},{6,7},{7,0},{8,9},{9,10},{10,1... | collective-permute-start | bytes 417800 | tf_op jit(solution)/shard_map/ppermute | solution.py:528
  105.4 1.4 %collective-permute-done.14.refs_1_ = bf16[272,256]{1,0:T(8,128)(2,1)S(1)} collective-permute-done((bf16[272,256]{1,0:T(8,128)(2,1)S(1)}, bf16[272,256]{1,0:T(8,128)(2,1)S(1)}, u32[]{:S(2)}, u32[]{:S(2)}) %collective-permute-start.14) | collective-permute-done | bytes 139296 | tf_op jit(solution)/shard_map/ppermute | solution.py:528
  106.8 0.4 collective-permute-start.19
  107.2 1.1 collective-permute-done.16.refs_3_
  108.3 2.8 %collective-permute-done.17.refs_4_ = bf16[272,256]{1,0:T(8,128)(2,1)S(1)} collective-permute-done((bf16[272,256]{1,0:T(8,128)(2,1)S(1)}, bf16[272,256]{1,0:T(8,128)(2,1)S(1)}, u32[]{:S(2)}, u32[]{:S(2)}) %collective-permute-start.17) | collective-permute-done | bytes 139296 | tf_op jit(solution)/shard_map/ppermute | solution.py:528
  111.1 1.4 %collective-permute-done.19.refs_6_ = bf16[272,256]{1,0:T(8,128)(2,1)S(1)} collective-permute-done((bf16[272,256]{1,0:T(8,128)(2,1)S(1)}, bf16[272,256]{1,0:T(8,128)(2,1)S(1)}, u32[]{:S(2)}, u32[]{:S(2)}) %collective-permute-start.19) | collective-permute-done | bytes 139296 | tf_op jit(solution)/shard_map/ppermute | solution.py:528
  112.5 0.9 shard_map.102
  (31 shorter events, 0.1 us)
Async XLA Ops:
  4.8 6.6 %copy-start.4 = (bf16[528,128]{1,0:T(8,128)(2,1)S(1)}, bf16[528,128]{1,0:T(8,128)(2,1)}, u32[]{:S(2)}) copy-start(bf16[528,128]{1,0:T(8,128)(2,1)} %get-tuple-element.25.refs_0_.q0) | copy-start | bytes 405508
  4.8 39.4 %all-to-all-start = ((bf16[8,1024,128]{2,1,0:T(8,128)(2,1)}), bf16[8,1024,128]{2,1,0:T(8,128)(2,1)}, u32[]{:S(2)}, u32[]{:S(2)}) async-start(bf16[8,1024,128]{2,1,0:T(8,128)(2,1)} %get-tuple-element.29), calls=%async_computation | async-start | bytes 4194304 | tf_op jit(solution)/shard_map/all_to_all | solution.py:498
  11.4 9.7 %collective-permute-start.2 = (bf16[528,128]{1,0:T(8,128)(2,1)S(1)}, bf16[528,128]{1,0:T(8,128)(2,1)S(1)}, u32[]{:S(2)}, u32[]{:S(2)}) collective-permute-start(bf16[528,128]{1,0:T(8,128)(2,1)S(1)} %copy-done.4), channel_id=1, source_target_pairs={{192,0},{0,64},{64,128},{128,192},{193,1},{1,65},{65,129},{129,193... | collective-permute-start | bytes 405512 | tf_op jit(solution)/shard_map/ppermute | solution.py:495
  11.4 9.7 %collective-permute-start.1 = (bf16[528,128]{1,0:T(8,128)(2,1)S(1)}, bf16[528,128]{1,0:T(8,128)(2,1)S(1)}, u32[]{:S(2)}, u32[]{:S(2)}) collective-permute-start(bf16[528,128]{1,0:T(8,128)(2,1)S(1)} %copy-done.4), channel_id=1, source_target_pairs={{128,0},{192,64},{0,128},{64,192},{129,1},{193,65},{1,129},{65,193... | collective-permute-start | bytes 405512 | tf_op jit(solution)/shard_map/ppermute | solution.py:495
  14.1 7.6 %collective-permute-start = (bf16[528,128]{1,0:T(8,128)(2,1)S(1)}, bf16[528,128]{1,0:T(8,128)(2,1)S(1)}, u32[]{:S(2)}, u32[]{:S(2)}) collective-permute-start(bf16[528,128]{1,0:T(8,128)(2,1)S(1)} %copy-done.4), channel_id=1, source_target_pairs={{64,0},{128,64},{192,128},{0,192},{65,1},{129,65},{193,129},{1,193... | collective-permute-start | bytes 405512 | tf_op jit(solution)/shard_map/ppermute | solution.py:495
  15.5 6.2 %copy-start.5 = (bf16[528,128]{1,0:T(8,128)(2,1)S(1)}, bf16[528,128]{1,0:T(8,128)(2,1)}, u32[]{:S(2)}) copy-start(bf16[528,128]{1,0:T(8,128)(2,1)} %get-tuple-element.25.refs_0_.q0) | copy-start | bytes 405508
  15.5 6.2 %copy-start.6 = (bf16[2,128,1,2,128]{4,3,2,1,0:T(2,128)(2,1)S(1)}, bf16[2,128,1,2,128]{4,3,2,1,0:T(2,128)(2,1)}, u32[]{:S(2)}) copy-start(bf16[2,128,1,2,128]{4,3,2,1,0:T(2,128)(2,1)} %param.12) | copy-start | bytes 393220
  15.5 6.2 %copy-start.7 = (s32[4]{0:T(128)S(1)}, s32[4]{0:T(128)}, u32[]{:S(2)}) copy-start(s32[4]{0:T(128)} %pad_add_fusion.place_ref) | copy-start | bytes 52
  15.5 28.7 %copy-start.9 = (s32[16]{0:T(128)S(1)}, s32[16]{0:T(128)}, u32[]{:S(2)}) copy-start(s32[16]{0:T(128)} %trace_ref.3) | copy-start | bytes 196
  15.5 28.7 %copy-start.10 = (s32[16]{0:T(128)S(1)}, s32[16]{0:T(128)}, u32[]{:S(2)}) copy-start(s32[16]{0:T(128)} %length_ref.1) | copy-start | bytes 196
  21.7 1.2 %copy-start = (bf16[256,2048]{1,0:T(8,128)(2,1)S(1)}, bf16[256,2048]{1,0:T(8,128)(2,1)}, u32[]{:S(2)}) copy-start(bf16[256,2048]{1,0:T(8,128)(2,1)} %get-tuple-element.26.behind_ref.weight_ref) | copy-start | bytes 3145732
  23.5 7.7 %collective-permute-start.5 = (f32[64,128]{1,0:T(8,128)S(1)}, f32[64,128]{1,0:T(8,128)S(1)}, u32[]{:S(2)}, u32[]{:S(2)}) collective-permute-start(f32[64,128]{1,0:T(8,128)S(1)} %get-tuple-element.30), channel_id=1, source_target_pairs={{0,3},{1,2},{2,1},{3,0},{4,7},{5,6},{6,5},{7,4},{8,11},{9,10},{10,... | collective-permute-start | bytes 98312 | tf_op jit(solution)/shard_map/ppermute | solution.py:514
  27.2 29.9 %collective-permute-start.7 = (bf16[128,2048]{1,0:T(8,128)(2,1)}, bf16[128,2048]{1,0:T(8,128)(2,1)S(1)}, u32[]{:S(2)}, u32[]{:S(2)}) collective-permute-start(bf16[128,2048]{1,0:T(8,128)(2,1)} %get-tuple-element.32), channel_id=1, source_target_pairs={{64,0},{128,64},{192,128},{0,192},{65,1},{129,65},{193,129},{1,193... | collective-permute-start | bytes 1572872 | tf_op jit(solution)/shard_map/ppermute | solution.py:495
  29.4 27.7 %collective-permute-start.8 = (bf16[128,2048]{1,0:T(8,128)(2,1)}, bf16[128,2048]{1,0:T(8,128)(2,1)S(1)}, u32[]{:S(2)}, u32[]{:S(2)}) collective-permute-start(bf16[128,2048]{1,0:T(8,128)(2,1)} %get-tuple-element.33), channel_id=1, source_target_pairs={{128,0},{192,64},{0,128},{64,192},{129,1},{193,65},{1,129},{65,193... | collective-permute-start | bytes 1572872 | tf_op jit(solution)/shard_map/ppermute | solution.py:495
  30.6 26.5 %collective-permute-start.9 = (bf16[128,2048]{1,0:T(8,128)(2,1)}, bf16[128,2048]{1,0:T(8,128)(2,1)S(1)}, u32[]{:S(2)}, u32[]{:S(2)}) collective-permute-start(bf16[128,2048]{1,0:T(8,128)(2,1)} %get-tuple-element.34), channel_id=1, source_target_pairs={{192,0},{0,64},{64,128},{128,192},{193,1},{1,65},{65,129},{129,193... | collective-permute-start | bytes 1572872 | tf_op jit(solution)/shard_map/ppermute | solution.py:495
  31.3 4.8 %collective-permute-start.4 = (f32[64,128]{1,0:T(8,128)S(1)}, f32[64,128]{1,0:T(8,128)S(1)}, u32[]{:S(2)}, u32[]{:S(2)}) collective-permute-start(f32[64,128]{1,0:T(8,128)S(1)} %get-tuple-element.30), channel_id=1, source_target_pairs={{0,2},{1,3},{2,0},{3,1},{4,6},{5,7},{6,4},{7,5},{8,10},{9,11},{10,... | collective-permute-start | bytes 98312 | tf_op jit(solution)/shard_map/ppermute | solution.py:514
  31.3 4.8 %collective-permute-start.3 = (f32[64,128]{1,0:T(8,128)S(1)}, f32[64,128]{1,0:T(8,128)S(1)}, u32[]{:S(2)}, u32[]{:S(2)}) collective-permute-start(f32[64,128]{1,0:T(8,128)S(1)} %get-tuple-element.30), channel_id=1, source_target_pairs={{0,1},{1,0},{2,3},{3,2},{4,5},{5,4},{6,7},{7,6},{8,9},{9,8},{10,11... | collective-permute-start | bytes 98312 | tf_op jit(solution)/shard_map/ppermute | solution.py:514
  36.1 8.1 %collective-permute-start.6 = (f32[64,128]{1,0:T(8,128)S(1)}, f32[64,128]{1,0:T(8,128)S(1)}, u32[]{:S(2)}, u32[]{:S(2)}) collective-permute-start(f32[64,128]{1,0:T(8,128)S(1)} %add_add_fusion), channel_id=1, source_target_pairs={{0,4},{1,5},{2,6},{3,7},{4,0},{5,1},{6,2},{7,3},{8,12},{9,13},{10,... | collective-permute-start | bytes 98312 | tf_op jit(solution)/shard_map/ppermute | solution.py:516
  44.2 2.2 %copy-start.2 = (bf16[1,2,128,8192]{3,2,1,0:T(8,128)(2,1)S(1)}, bf16[1,2,128,8192]{3,2,1,0:T(8,128)(2,1)}, u32[]{:S(2)}) copy-start(bf16[1,2,128,8192]{3,2,1,0:T(8,128)(2,1)} %param.14) | copy-start | bytes 12582916
  56.3 0.8 copy-start.3
  57.1 26.3 %copy-start.1 = (bf16[256,2048]{1,0:T(8,128)(2,1)S(1)}, bf16[256,2048]{1,0:T(8,128)(2,1)}, u32[]{:S(2)}) copy-start(bf16[256,2048]{1,0:T(8,128)(2,1)} %get-tuple-element.26.behind_ref.weight_ref) | copy-start | bytes 3145732
  57.1 12.4 %all-to-all-start.1 = ((bf16[4,544,128]{2,1,0:T(8,128)(2,1)}), bf16[4,544,128]{2,1,0:T(8,128)(2,1)S(1)}, u32[]{:S(2)}, u32[]{:S(2)}) async-start(bf16[4,544,128]{2,1,0:T(8,128)(2,1)} %copy-done.3), calls=%async_computation.1 | async-start | bytes 1114112 | tf_op jit(solution)/shard_map/all_to_all | solution.py:498
  61.3 13.9 %collective-permute-start.10 = (bf16[128,2048]{1,0:T(8,128)(2,1)S(1)}, bf16[128,2048]{1,0:T(8,128)(2,1)}, u32[]{:S(2)}, u32[]{:S(2)}) collective-permute-start(bf16[128,2048]{1,0:T(8,128)(2,1)S(1)} %collective-permute-done.7.refs_0_), channel_id=1, source_target_pairs={{0,8},{8,0},{16,24},{24,16},{32,40},{40,32},{48,56},{56,48},{1,9},... | collective-permute-start | bytes 1572872 | tf_op jit(solution)/shard_map/ppermute | solution.py:501
  61.3 13.9 %collective-permute-start.11 = (bf16[128,2048]{1,0:T(8,128)(2,1)S(1)}, bf16[128,2048]{1,0:T(8,128)(2,1)}, u32[]{:S(2)}, u32[]{:S(2)}) collective-permute-start(bf16[128,2048]{1,0:T(8,128)(2,1)S(1)} %collective-permute-done.8.refs_2_), channel_id=1, source_target_pairs={{0,8},{8,0},{16,24},{24,16},{32,40},{40,32},{48,56},{56,48},{1,9},... | collective-permute-start | bytes 1572872 | tf_op jit(solution)/shard_map/ppermute | solution.py:501
  61.8 13.4 %collective-permute-start.12 = (bf16[128,2048]{1,0:T(8,128)(2,1)S(1)}, bf16[128,2048]{1,0:T(8,128)(2,1)}, u32[]{:S(2)}, u32[]{:S(2)}) collective-permute-start(bf16[128,2048]{1,0:T(8,128)(2,1)S(1)} %collective-permute-done.9.refs_4_), channel_id=1, source_target_pairs={{0,8},{8,0},{16,24},{24,16},{32,40},{40,32},{48,56},{56,48},{1,9},... | collective-permute-start | bytes 1572872 | tf_op jit(solution)/shard_map/ppermute | solution.py:501
  71.7 11.6 %all-to-all-start.2 = ((bf16[4,528,128]{2,1,0:T(8,128)(2,1)}), bf16[4,528,128]{2,1,0:T(8,128)(2,1)S(1)}, u32[]{:S(2)}, u32[]{:S(2)}) async-start(bf16[4,528,128]{2,1,0:T(8,128)(2,1)} %shard_map.99), calls=%async_computation.2 | async-start | bytes 1081344 | tf_op jit(solution)/shard_map/all_to_all | solution.py:498
  86.2 17.8 %collective-permute-start.13 = (bf16[272,256]{1,0:T(8,128)(2,1)S(1)}, bf16[272,256]{1,0:T(8,128)(2,1)S(1)}, u32[]{:S(2)}, u32[]{:S(2)}) collective-permute-start(bf16[272,256]{1,0:T(8,128)(2,1)S(1)} %get-tuple-element.40), channel_id=1, source_target_pairs={{0,4},{1,5},{2,6},{3,7},{4,0},{5,1},{6,2},{7,3},{8,12},{9,13},{10,... | collective-permute-start | bytes 417800 | tf_op jit(solution)/shard_map/ppermute | solution.py:528
  90.9 15.9 %collective-permute-start.14 = (bf16[272,256]{1,0:T(8,128)(2,1)S(1)}, bf16[272,256]{1,0:T(8,128)(2,1)S(1)}, u32[]{:S(2)}, u32[]{:S(2)}) collective-permute-start(bf16[272,256]{1,0:T(8,128)(2,1)S(1)} %get-tuple-element.41), channel_id=1, source_target_pairs={{0,3},{1,4},{2,5},{3,6},{4,7},{5,0},{6,1},{7,2},{8,11},{9,12},{10,... | collective-permute-start | bytes 417800 | tf_op jit(solution)/shard_map/ppermute | solution.py:528
  92.7 19.8 %copy-start.8 = (s32[2,16]{1,0:T(2,128)S(1)}, s32[2,16]{1,0:T(2,128)}, u32[]{:S(2)}) copy-start(s32[2,16]{1,0:T(2,128)} %refs_8_.1) | copy-start | bytes 388
  92.7 14.5 %collective-permute-start.15 = (bf16[272,256]{1,0:T(8,128)(2,1)S(1)}, bf16[272,256]{1,0:T(8,128)(2,1)S(1)}, u32[]{:S(2)}, u32[]{:S(2)}) collective-permute-start(bf16[272,256]{1,0:T(8,128)(2,1)S(1)} %get-tuple-element.42), channel_id=1, source_target_pairs={{0,5},{1,6},{2,7},{3,0},{4,1},{5,2},{6,3},{7,4},{8,13},{9,14},{10,... | collective-permute-start | bytes 417800 | tf_op jit(solution)/shard_map/ppermute | solution.py:528
  99.8 8.5 %collective-permute-start.16 = (bf16[272,256]{1,0:T(8,128)(2,1)S(1)}, bf16[272,256]{1,0:T(8,128)(2,1)S(1)}, u32[]{:S(2)}, u32[]{:S(2)}) collective-permute-start(bf16[272,256]{1,0:T(8,128)(2,1)S(1)} %get-tuple-element.43), channel_id=1, source_target_pairs={{0,2},{1,3},{2,4},{3,5},{4,6},{5,7},{6,0},{7,1},{8,10},{9,11},{10,... | collective-permute-start | bytes 417800 | tf_op jit(solution)/shard_map/ppermute | solution.py:528
  102.4 8.7 %collective-permute-start.17 = (bf16[272,256]{1,0:T(8,128)(2,1)S(1)}, bf16[272,256]{1,0:T(8,128)(2,1)S(1)}, u32[]{:S(2)}, u32[]{:S(2)}) collective-permute-start(bf16[272,256]{1,0:T(8,128)(2,1)S(1)} %get-tuple-element.44), channel_id=1, source_target_pairs={{0,6},{1,7},{2,0},{3,1},{4,2},{5,3},{6,4},{7,5},{8,14},{9,15},{10,... | collective-permute-start | bytes 417800 | tf_op jit(solution)/shard_map/ppermute | solution.py:528
  104.0 7.2 %collective-permute-start.18 = (bf16[272,256]{1,0:T(8,128)(2,1)S(1)}, bf16[272,256]{1,0:T(8,128)(2,1)S(1)}, u32[]{:S(2)}, u32[]{:S(2)}) collective-permute-start(bf16[272,256]{1,0:T(8,128)(2,1)S(1)} %get-tuple-element.45), channel_id=1, source_target_pairs={{0,1},{1,2},{2,3},{3,4},{4,5},{5,6},{6,7},{7,0},{8,9},{9,10},{10,1... | collective-permute-start | bytes 417800 | tf_op jit(solution)/shard_map/ppermute | solution.py:528
  106.8 5.7 %collective-permute-start.19 = (bf16[272,256]{1,0:T(8,128)(2,1)S(1)}, bf16[272,256]{1,0:T(8,128)(2,1)S(1)}, u32[]{:S(2)}, u32[]{:S(2)}) collective-permute-start(bf16[272,256]{1,0:T(8,128)(2,1)S(1)} %get-tuple-element.46), channel_id=1, source_target_pairs={{0,7},{1,0},{2,1},{3,2},{4,3},{5,4},{6,5},{7,6},{8,15},{9,8},{10,9... | collective-permute-start | bytes 417800 | tf_op jit(solution)/shard_map/ppermute | solution.py:528

commit v5 on v4

--- a/solution.py
+++ b/solution.py
@@ -213,6 +213,7 @@
         valid = length_ref[trace_ref[place_ref[SLOT] + slot]] - place_ref[POOL] * width
         usable = position < valid
         values = prior_ref[:, pl.ds((2 * slot + 1) * block, block), :].reshape(width, size)
+        values = jnp.concatenate([values, jnp.ones_like(values)], 1)
         for tile in range(pools):
             pay = pay_ref.at[lax.rem(place_ref[POOL] + tile, pools)]
             query = query_ref[tile, slot]
@@ -234,10 +235,10 @@
                 peak = jnp.maximum(peak, jnp.max(fresh_scores, -1, keepdims=True))
             peak = jnp.maximum(peak * factor, peak_floor).astype(jnp.bfloat16).astype(jnp.float32)
             weights = jnp.exp2(scores * factor - peak)
-            total = jnp.sum(weights, -1, keepdims=True)
             blended = jnp.dot(
                 weights.astype(jnp.bfloat16), values, preferred_element_type=jnp.float32
             )
+            total, blended = blended[:, size : size + 1], blended[:, :size]
             if tile == 0:
                 fresh_weights = jnp.exp2(fresh_scores * factor - peak)
                 total = total + jnp.sum(fresh_weights, -1, keepdims=True)

time: 114 us -> 113 us (level)
  transfers between devices with their start and end apart: 23 -> 23, of which waited for: 10 -> 10; matrix products, arithmetic and copies ran while one was open for 0% -> 0% of each run, Pallas kernels for 18% -> 17%
where the time goes in v5:
time: 113 us
  starting transfers between devices  47.5 us (42%)
  waiting for transfers between devices  32.7 us (29%)
  Pallas kernels  26.9 us (24%)
  local copies, waits for them, and re-layouts  4.24 us (4%)
    all_to_all x3, waiting for transfers between devices, turn(): return lax.all_to_all(array, axes, split_axis=0, concat_axis=0, tiled=True)  15.9 us
    ppermute x7, starting transfers between devices, shards(): lax.ppermute(part, 'tp', [(n, (n + o) % tps) for n in range(tps)])  15.5 us
    all_to_all x3, starting transfers between devices, turn(): return lax.all_to_all(array, axes, split_axis=0, concat_axis=0, tiled=True)  14.2 us
    pallas_call x1, Pallas kernels, attend(): pl.pallas_call(attend_kernel, out_shape=[jax.ShapeDtypeStruct((pools, slo...  9.43 us
    ppermute x6, starting transfers between devices, from_pool(): lax.ppermute(array, 'pool', [((n + offset) % pools, n) for n in range(poo...  8.24 us
    ppermute x7, waiting for transfers between devices, shards(): lax.ppermute(part, 'tp', [(n, (n + o) % tps) for n in range(tps)])  6.85 us
    pallas_call x2, Pallas kernels, project(): pl.pallas_call(functools.partial(project_kernel, offsets), out_shape=[jax...  6.67 us
    ppermute x1, starting transfers between devices, shards(): head = head + lax.ppermute(head, 'tp', [(n, n ^ 4) for n in range(tps)])  4.79 us
  transfers between devices with their start and end apart: 23, of which 10 were waited for; matrix products, arithmetic and copies ran while one was open for 0% of the time, Pallas kernels for 17%

profile of v5, /device:TPU:8, one launch (start us, length us, event | category | flops | bytes accessed | tf_op | source)
XLA Modules:
  0.0 112.8 jit_solution(16514990730232666587)
XLA Ops:
  0.6 0.6 pad_add_fusion.place_ref
  1.3 3.5 %shard_map.95 = (bf16[8,1024,128]{2,1,0:T(8,128)(2,1)}, bf16[528,128]{1,0:T(8,128)(2,1)}) custom-call(s32[4]{0:T(128)} %pad_add_fusion.place_ref, s32[16]{0:T(128)} %trace_ref.3, bf16[16,512,128]{2,1,0:T(8,128)(2,1)} %bitcast.12, bf16[512,128]{1,0:T(8,128)(2,1)} %bitcast.13, f32[2,128]{1,0:T(2,128)} %bitcast.14), custom_call_target="tpu_custom_call" | custom-call | bytes 4194304 | tf_op jit(solution)/shard_map/pallas_call | solution.py:74
  4.8 6.5 %all-to-all-start = ((bf16[8,1024,128]{2,1,0:T(8,128)(2,1)}), bf16[8,1024,128]{2,1,0:T(8,128)(2,1)}, u32[]{:S(2)}, u32[]{:S(2)}) async-start(bf16[8,1024,128]{2,1,0:T(8,128)(2,1)} %get-tuple-element.29), calls=%async_computation | async-start | bytes 4194304 | tf_op jit(solution)/shard_map/all_to_all | solution.py:499
  11.4 0.0 collective-permute-start.2
  11.4 2.7 %collective-permute-start.1 = (bf16[528,128]{1,0:T(8,128)(2,1)S(1)}, bf16[528,128]{1,0:T(8,128)(2,1)S(1)}, u32[]{:S(2)}, u32[]{:S(2)}) collective-permute-start(bf16[528,128]{1,0:T(8,128)(2,1)S(1)} %copy-done.4), channel_id=1, source_target_pairs={{128,0},{192,64},{0,128},{64,192},{129,1},{193,65},{1,129},{65,193... | collective-permute-start | bytes 405512 | tf_op jit(solution)/shard_map/ppermute | solution.py:496
  14.1 1.4 %collective-permute-start = (bf16[528,128]{1,0:T(8,128)(2,1)S(1)}, bf16[528,128]{1,0:T(8,128)(2,1)S(1)}, u32[]{:S(2)}, u32[]{:S(2)}) collective-permute-start(bf16[528,128]{1,0:T(8,128)(2,1)S(1)} %copy-done.4), channel_id=1, source_target_pairs={{64,0},{128,64},{192,128},{0,192},{65,1},{129,65},{193,129},{1,193... | collective-permute-start | bytes 405512 | tf_op jit(solution)/shard_map/ppermute | solution.py:496
  15.5 0.0 copy-start.10
  15.6 3.6 %shard_map.96 = (bf16[128,2048]{1,0:T(8,128)(2,1)}, bf16[128,2048]{1,0:T(8,128)(2,1)}, bf16[128,2048]{1,0:T(8,128)(2,1)}, bf16[256,2048]{1,0:T(8,128)(2,1)}) custom-call(s32[4]{0:T(128)} %pad_add_fusion.place_ref, bf16[256,8192]{1,0:T(8,128)(2,1)} %bitcast.9, bf16[528,128]{1,0:T(8,128)(2,1)} %get-tuple-element.25.refs_0_.q0), custom_call_target="tpu_custom_call" | custom-call | bytes 8388608 | tf_op jit(solution)/shard_map/pallas_call | solution.py:127
  19.2 2.0 %collective-permute-done.2.q3 = bf16[528,128]{1,0:T(8,128)(2,1)S(1)} collective-permute-done((bf16[528,128]{1,0:T(8,128)(2,1)S(1)}, bf16[528,128]{1,0:T(8,128)(2,1)S(1)}, u32[]{:S(2)}, u32[]{:S(2)}) %collective-permute-start.2) | collective-permute-done | bytes 135200 | tf_op jit(solution)/shard_map/ppermute | solution.py:496
  21.1 0.0 collective-permute-done.1.q2
  21.1 0.6 collective-permute-done.q1
  21.7 1.2 %copy-done = bf16[256,2048]{1,0:T(8,128)(2,1)S(1)} copy-done((bf16[256,2048]{1,0:T(8,128)(2,1)S(1)}, bf16[256,2048]{1,0:T(8,128)(2,1)}, u32[]{:S(2)}) %copy-start) | copy-done | bytes 1048600
  22.9 0.6 shard_map.97
  23.5 3.6 %collective-permute-start.5 = (f32[64,128]{1,0:T(8,128)S(1)}, f32[64,128]{1,0:T(8,128)S(1)}, u32[]{:S(2)}, u32[]{:S(2)}) collective-permute-start(f32[64,128]{1,0:T(8,128)S(1)} %get-tuple-element.30), channel_id=1, source_target_pairs={{0,3},{1,2},{2,1},{3,0},{4,7},{5,6},{6,5},{7,4},{8,11},{9,10},{10,... | collective-permute-start | bytes 98312 | tf_op jit(solution)/shard_map/ppermute | solution.py:515
  27.2 2.3 %collective-permute-start.7 = (bf16[128,2048]{1,0:T(8,128)(2,1)}, bf16[128,2048]{1,0:T(8,128)(2,1)S(1)}, u32[]{:S(2)}, u32[]{:S(2)}) collective-permute-start(bf16[128,2048]{1,0:T(8,128)(2,1)} %get-tuple-element.32), channel_id=1, source_target_pairs={{64,0},{128,64},{192,128},{0,192},{65,1},{129,65},{193,129},{1,193... | collective-permute-start | bytes 1572872 | tf_op jit(solution)/shard_map/ppermute | solution.py:496
  29.4 1.1 %collective-permute-start.8 = (bf16[128,2048]{1,0:T(8,128)(2,1)}, bf16[128,2048]{1,0:T(8,128)(2,1)S(1)}, u32[]{:S(2)}, u32[]{:S(2)}) collective-permute-start(bf16[128,2048]{1,0:T(8,128)(2,1)} %get-tuple-element.33), channel_id=1, source_target_pairs={{128,0},{192,64},{0,128},{64,192},{129,1},{193,65},{1,129},{65,193... | collective-permute-start | bytes 1572872 | tf_op jit(solution)/shard_map/ppermute | solution.py:496
  30.6 0.7 collective-permute-start.9
  31.3 0.0 collective-permute-start.4
  31.3 0.0 collective-permute-done.5
  31.3 0.7 collective-permute-start.3
  31.9 4.2 %collective-permute-done.4 = f32[64,128]{1,0:T(8,128)S(1)} collective-permute-done((f32[64,128]{1,0:T(8,128)S(1)}, f32[64,128]{1,0:T(8,128)S(1)}, u32[]{:S(2)}, u32[]{:S(2)}) %collective-permute-start.4) | collective-permute-done | bytes 32800 | tf_op jit(solution)/shard_map/ppermute | solution.py:515
  36.1 0.0 collective-permute-done.3
  36.1 4.8 %collective-permute-start.6 = (f32[64,128]{1,0:T(8,128)S(1)}, f32[64,128]{1,0:T(8,128)S(1)}, u32[]{:S(2)}, u32[]{:S(2)}) collective-permute-start(f32[64,128]{1,0:T(8,128)S(1)} %add_add_fusion), channel_id=1, source_target_pairs={{0,4},{1,5},{2,6},{3,7},{4,0},{5,1},{6,2},{7,3},{8,12},{9,13},{10,... | collective-permute-start | bytes 98312 | tf_op jit(solution)/shard_map/ppermute | solution.py:517
  40.9 3.3 %collective-permute-done.6 = f32[64,128]{1,0:T(8,128)S(1)} collective-permute-done((f32[64,128]{1,0:T(8,128)S(1)}, f32[64,128]{1,0:T(8,128)S(1)}, u32[]{:S(2)}, u32[]{:S(2)}) %collective-permute-start.6) | collective-permute-done | bytes 32800 | tf_op jit(solution)/shard_map/ppermute | solution.py:517
  44.2 0.0 copy-start.2
  44.2 2.2 %copy-done.2 = bf16[1,2,128,8192]{3,2,1,0:T(8,128)(2,1)S(1)} copy-done((bf16[1,2,128,8192]{3,2,1,0:T(8,128)(2,1)S(1)}, bf16[1,2,128,8192]{3,2,1,0:T(8,128)(2,1)}, u32[]{:S(2)}) %copy-start.2) | copy-done | bytes 4194328
  46.4 9.4 %shard_map.98 = (bf16[4,544,128]{2,1,0:T(8,128)(2,1)S(1)}, f32[8,128]{1,0:T(8,128)S(1)}) custom-call(s32[4]{0:T(128)S(1)} %copy-done.7, s32[16]{0:T(128)S(1)} %copy-done.9, s32[16]{0:T(128)S(1)} %copy-done.10, bf16[4,2,256,128]{3,2,1,0:T(8,128)(2,1)S(1)} %get-tuple-element.27.query_ref, bf16[2,2,128,128]{3,2,1,0:T(8,128)(2,1)S(1)} %get-tuple-element.28.new_ref, ...), custom_call_target="tpu_custom_call" | custom-call | flops 2147483648 | bytes 2097152 | tf_op jit(solution)/shard_map/pallas_call | solution.py:275
  55.9 0.8 copy-done.3
  56.7 4.2 %all-to-all-start.1 = ((bf16[4,544,128]{2,1,0:T(8,128)(2,1)}), bf16[4,544,128]{2,1,0:T(8,128)(2,1)S(1)}, u32[]{:S(2)}, u32[]{:S(2)}) async-start(bf16[4,544,128]{2,1,0:T(8,128)(2,1)} %copy-done.3), calls=%async_computation.1 | async-start | bytes 1114112 | tf_op jit(solution)/shard_map/all_to_all | solution.py:499
  60.9 0.5 collective-permute-start.11
  61.4 7.7 %all-to-all-done.1.pay_ref = bf16[4,544,128]{2,1,0:T(8,128)(2,1)S(1)} async-done(((bf16[4,544,128]{2,1,0:T(8,128)(2,1)}), bf16[4,544,128]{2,1,0:T(8,128)(2,1)S(1)}, u32[]{:S(2)}, u32[]{:S(2)}) %all-to-all-start.1) | async-done | bytes 557088 | tf_op jit(solution)/shard_map/all_to_all | solution.py:499
  69.1 2.2 %shard_map.99 = bf16[4,528,128]{2,1,0:T(8,128)(2,1)} custom-call(bf16[4,544,128]{2,1,0:T(8,128)(2,1)S(1)} %all-to-all-done.1.pay_ref, f32[8,128]{1,0:T(8,128)S(1)} %get-tuple-element.36.seen_ref), custom_call_target="tpu_custom_call" | custom-call | bytes 655360 | tf_op jit(solution)/shard_map/pallas_call | solution.py:359
  71.3 3.5 %all-to-all-start.2 = ((bf16[4,528,128]{2,1,0:T(8,128)(2,1)}), bf16[4,528,128]{2,1,0:T(8,128)(2,1)S(1)}, u32[]{:S(2)}, u32[]{:S(2)}) async-start(bf16[4,528,128]{2,1,0:T(8,128)(2,1)} %shard_map.99), calls=%async_computation.2 | async-start | bytes 1081344 | tf_op jit(solution)/shard_map/all_to_all | solution.py:499
  74.8 8.1 %all-to-all-done.2.attended_ref = bf16[4,528,128]{2,1,0:T(8,128)(2,1)S(1)} async-done(((bf16[4,528,128]{2,1,0:T(8,128)(2,1)}), bf16[4,528,128]{2,1,0:T(8,128)(2,1)S(1)}, u32[]{:S(2)}, u32[]{:S(2)}) %all-to-all-start.2) | async-done | bytes 540704 | tf_op jit(solution)/shard_map/all_to_all | solution.py:499
  82.9 2.8 %shard_map.100 = (bf16[272,256]{1,0:T(8,128)(2,1)S(1)}, bf16[272,256]{1,0:T(8,128)(2,1)S(1)}, bf16[272,256]{1,0:T(8,128)(2,1)S(1)}) custom-call(s32[4]{0:T(128)S(1)} %copy-done.7, bf16[4,528,128]{2,1,0:T(8,128)(2,1)S(1)} %all-to-all-done.2.attended_ref, bf16[256,2048]{1,0:T(8,128)(2,1)S(1)} %copy-done.1, ...), custom_call_target="tpu_custom_call" | custom-call | flops 402653184 | bytes 1572864 | tf_op jit(solution)/shard_map/pallas_call | solution.py:425
  85.8 4.5 %collective-permute-start.13 = (bf16[272,256]{1,0:T(8,128)(2,1)S(1)}, bf16[272,256]{1,0:T(8,128)(2,1)S(1)}, u32[]{:S(2)}, u32[]{:S(2)}) collective-permute-start(bf16[272,256]{1,0:T(8,128)(2,1)S(1)} %get-tuple-element.40), channel_id=1, source_target_pairs={{0,4},{1,5},{2,6},{3,7},{4,0},{5,1},{6,2},{7,3},{8,12},{9,13},{10,... | collective-permute-start | bytes 417800 | tf_op jit(solution)/shard_map/ppermute | solution.py:529
  90.2 1.8 %collective-permute-start.14 = (bf16[272,256]{1,0:T(8,128)(2,1)S(1)}, bf16[272,256]{1,0:T(8,128)(2,1)S(1)}, u32[]{:S(2)}, u32[]{:S(2)}) collective-permute-start(bf16[272,256]{1,0:T(8,128)(2,1)S(1)} %get-tuple-element.41), channel_id=1, source_target_pairs={{0,3},{1,4},{2,5},{3,6},{4,7},{5,0},{6,1},{7,2},{8,11},{9,12},{10,... | collective-permute-start | bytes 417800 | tf_op jit(solution)/shard_map/ppermute | solution.py:529
  92.1 3.2 %collective-permute-start.15 = (bf16[272,256]{1,0:T(8,128)(2,1)S(1)}, bf16[272,256]{1,0:T(8,128)(2,1)S(1)}, u32[]{:S(2)}, u32[]{:S(2)}) collective-permute-start(bf16[272,256]{1,0:T(8,128)(2,1)S(1)} %get-tuple-element.42), channel_id=1, source_target_pairs={{0,5},{1,6},{2,7},{3,0},{4,1},{5,2},{6,3},{7,4},{8,13},{9,14},{10,... | collective-permute-start | bytes 417800 | tf_op jit(solution)/shard_map/ppermute | solution.py:529
  95.3 3.8 %shard_map.101 = (bf16[272,256]{1,0:T(8,128)(2,1)S(1)}, bf16[272,256]{1,0:T(8,128)(2,1)S(1)}, bf16[272,256]{1,0:T(8,128)(2,1)S(1)}, bf16[272,256]{1,0:T(8,128)(2,1)S(1)}, bf16[272,256]{1,0:T(8,128)(2,1)S(1)}) custom-call(s32[4]{0:T(128)S(1)} %copy-done.7, bf16[4,528,128]{2,1,0:T(8,128)(2,1)S(1)} %all-to-all-done.2.attended_ref, ...), custom_call_target="tpu_custom_call" | custom-call | flops 671088640 | bytes 2621440 | tf_op jit(solution)/shard_map/pallas_call | solution.py:425
  99.1 2.6 %collective-permute-start.16 = (bf16[272,256]{1,0:T(8,128)(2,1)S(1)}, bf16[272,256]{1,0:T(8,128)(2,1)S(1)}, u32[]{:S(2)}, u32[]{:S(2)}) collective-permute-start(bf16[272,256]{1,0:T(8,128)(2,1)S(1)} %get-tuple-element.43), channel_id=1, source_target_pairs={{0,2},{1,3},{2,4},{3,5},{4,6},{5,7},{6,0},{7,1},{8,10},{9,11},{10,... | collective-permute-start | bytes 417800 | tf_op jit(solution)/shard_map/ppermute | solution.py:529
  101.7 1.6 %collective-permute-start.17 = (bf16[272,256]{1,0:T(8,128)(2,1)S(1)}, bf16[272,256]{1,0:T(8,128)(2,1)S(1)}, u32[]{:S(2)}, u32[]{:S(2)}) collective-permute-start(bf16[272,256]{1,0:T(8,128)(2,1)S(1)} %get-tuple-element.44), channel_id=1, source_target_pairs={{0,6},{1,7},{2,0},{3,1},{4,2},{5,3},{6,4},{7,5},{8,14},{9,15},{10,... | collective-permute-start | bytes 417800 | tf_op jit(solution)/shard_map/ppermute | solution.py:529
  103.3 1.4 %collective-permute-start.18 = (bf16[272,256]{1,0:T(8,128)(2,1)S(1)}, bf16[272,256]{1,0:T(8,128)(2,1)S(1)}, u32[]{:S(2)}, u32[]{:S(2)}) collective-permute-start(bf16[272,256]{1,0:T(8,128)(2,1)S(1)} %get-tuple-element.45), channel_id=1, source_target_pairs={{0,1},{1,2},{2,3},{3,4},{4,5},{5,6},{6,7},{7,0},{8,9},{9,10},{10,1... | collective-permute-start | bytes 417800 | tf_op jit(solution)/shard_map/ppermute | solution.py:529
  104.8 1.5 %collective-permute-done.14.refs_1_ = bf16[272,256]{1,0:T(8,128)(2,1)S(1)} collective-permute-done((bf16[272,256]{1,0:T(8,128)(2,1)S(1)}, bf16[272,256]{1,0:T(8,128)(2,1)S(1)}, u32[]{:S(2)}, u32[]{:S(2)}) %collective-permute-start.14) | collective-permute-done | bytes 139296 | tf_op jit(solution)/shard_map/ppermute | solution.py:529
  106.3 0.3 collective-permute-start.19
  106.6 1.1 collective-permute-done.16.refs_3_
  107.7 3.2 %collective-permute-done.17.refs_4_ = bf16[272,256]{1,0:T(8,128)(2,1)S(1)} collective-permute-done((bf16[272,256]{1,0:T(8,128)(2,1)S(1)}, bf16[272,256]{1,0:T(8,128)(2,1)S(1)}, u32[]{:S(2)}, u32[]{:S(2)}) %collective-permute-start.17) | collective-permute-done | bytes 139296 | tf_op jit(solution)/shard_map/ppermute | solution.py:529
  110.8 1.1 collective-permute-done.19.refs_6_
  111.9 0.9 shard_map.102
  (31 shorter events, 0.1 us)
Async XLA Ops:
  4.8 6.6 %copy-start.4 = (bf16[528,128]{1,0:T(8,128)(2,1)S(1)}, bf16[528,128]{1,0:T(8,128)(2,1)}, u32[]{:S(2)}) copy-start(bf16[528,128]{1,0:T(8,128)(2,1)} %get-tuple-element.25.refs_0_.q0) | copy-start | bytes 405508
  4.8 39.4 %all-to-all-start = ((bf16[8,1024,128]{2,1,0:T(8,128)(2,1)}), bf16[8,1024,128]{2,1,0:T(8,128)(2,1)}, u32[]{:S(2)}, u32[]{:S(2)}) async-start(bf16[8,1024,128]{2,1,0:T(8,128)(2,1)} %get-tuple-element.29), calls=%async_computation | async-start | bytes 4194304 | tf_op jit(solution)/shard_map/all_to_all | solution.py:499
  11.4 9.7 %collective-permute-start.2 = (bf16[528,128]{1,0:T(8,128)(2,1)S(1)}, bf16[528,128]{1,0:T(8,128)(2,1)S(1)}, u32[]{:S(2)}, u32[]{:S(2)}) collective-permute-start(bf16[528,128]{1,0:T(8,128)(2,1)S(1)} %copy-done.4), channel_id=1, source_target_pairs={{192,0},{0,64},{64,128},{128,192},{193,1},{1,65},{65,129},{129,193... | collective-permute-start | bytes 405512 | tf_op jit(solution)/shard_map/ppermute | solution.py:496
  11.4 9.7 %collective-permute-start.1 = (bf16[528,128]{1,0:T(8,128)(2,1)S(1)}, bf16[528,128]{1,0:T(8,128)(2,1)S(1)}, u32[]{:S(2)}, u32[]{:S(2)}) collective-permute-start(bf16[528,128]{1,0:T(8,128)(2,1)S(1)} %copy-done.4), channel_id=1, source_target_pairs={{128,0},{192,64},{0,128},{64,192},{129,1},{193,65},{1,129},{65,193... | collective-permute-start | bytes 405512 | tf_op jit(solution)/shard_map/ppermute | solution.py:496
  14.1 7.6 %collective-permute-start = (bf16[528,128]{1,0:T(8,128)(2,1)S(1)}, bf16[528,128]{1,0:T(8,128)(2,1)S(1)}, u32[]{:S(2)}, u32[]{:S(2)}) collective-permute-start(bf16[528,128]{1,0:T(8,128)(2,1)S(1)} %copy-done.4), channel_id=1, source_target_pairs={{64,0},{128,64},{192,128},{0,192},{65,1},{129,65},{193,129},{1,193... | collective-permute-start | bytes 405512 | tf_op jit(solution)/shard_map/ppermute | solution.py:496
  15.5 6.2 %copy-start.5 = (bf16[528,128]{1,0:T(8,128)(2,1)S(1)}, bf16[528,128]{1,0:T(8,128)(2,1)}, u32[]{:S(2)}) copy-start(bf16[528,128]{1,0:T(8,128)(2,1)} %get-tuple-element.25.refs_0_.q0) | copy-start | bytes 405508
  15.5 6.2 %copy-start.6 = (bf16[2,128,1,2,128]{4,3,2,1,0:T(2,128)(2,1)S(1)}, bf16[2,128,1,2,128]{4,3,2,1,0:T(2,128)(2,1)}, u32[]{:S(2)}) copy-start(bf16[2,128,1,2,128]{4,3,2,1,0:T(2,128)(2,1)} %param.12) | copy-start | bytes 393220
  15.5 6.2 %copy-start.7 = (s32[4]{0:T(128)S(1)}, s32[4]{0:T(128)}, u32[]{:S(2)}) copy-start(s32[4]{0:T(128)} %pad_add_fusion.place_ref) | copy-start | bytes 52
  15.5 28.7 %copy-start.9 = (s32[16]{0:T(128)S(1)}, s32[16]{0:T(128)}, u32[]{:S(2)}) copy-start(s32[16]{0:T(128)} %trace_ref.3) | copy-start | bytes 196
  15.5 28.7 %copy-start.10 = (s32[16]{0:T(128)S(1)}, s32[16]{0:T(128)}, u32[]{:S(2)}) copy-start(s32[16]{0:T(128)} %length_ref.1) | copy-start | bytes 196
  21.7 1.2 %copy-start = (bf16[256,2048]{1,0:T(8,128)(2,1)S(1)}, bf16[256,2048]{1,0:T(8,128)(2,1)}, u32[]{:S(2)}) copy-start(bf16[256,2048]{1,0:T(8,128)(2,1)} %get-tuple-element.26.behind_ref.weight_ref) | copy-start | bytes 3145732
  23.5 7.7 %collective-permute-start.5 = (f32[64,128]{1,0:T(8,128)S(1)}, f32[64,128]{1,0:T(8,128)S(1)}, u32[]{:S(2)}, u32[]{:S(2)}) collective-permute-start(f32[64,128]{1,0:T(8,128)S(1)} %get-tuple-element.30), channel_id=1, source_target_pairs={{0,3},{1,2},{2,1},{3,0},{4,7},{5,6},{6,5},{7,4},{8,11},{9,10},{10,... | collective-permute-start | bytes 98312 | tf_op jit(solution)/shard_map/ppermute | solution.py:515
  27.2 29.5 %collective-permute-start.7 = (bf16[128,2048]{1,0:T(8,128)(2,1)}, bf16[128,2048]{1,0:T(8,128)(2,1)S(1)}, u32[]{:S(2)}, u32[]{:S(2)}) collective-permute-start(bf16[128,2048]{1,0:T(8,128)(2,1)} %get-tuple-element.32), channel_id=1, source_target_pairs={{64,0},{128,64},{192,128},{0,192},{65,1},{129,65},{193,129},{1,193... | collective-permute-start | bytes 1572872 | tf_op jit(solution)/shard_map/ppermute | solution.py:496
  29.4 27.2 %collective-permute-start.8 = (bf16[128,2048]{1,0:T(8,128)(2,1)}, bf16[128,2048]{1,0:T(8,128)(2,1)S(1)}, u32[]{:S(2)}, u32[]{:S(2)}) collective-permute-start(bf16[128,2048]{1,0:T(8,128)(2,1)} %get-tuple-element.33), channel_id=1, source_target_pairs={{128,0},{192,64},{0,128},{64,192},{129,1},{193,65},{1,129},{65,193... | collective-permute-start | bytes 1572872 | tf_op jit(solution)/shard_map/ppermute | solution.py:496
  30.6 26.1 %collective-permute-start.9 = (bf16[128,2048]{1,0:T(8,128)(2,1)}, bf16[128,2048]{1,0:T(8,128)(2,1)S(1)}, u32[]{:S(2)}, u32[]{:S(2)}) collective-permute-start(bf16[128,2048]{1,0:T(8,128)(2,1)} %get-tuple-element.34), channel_id=1, source_target_pairs={{192,0},{0,64},{64,128},{128,192},{193,1},{1,65},{65,129},{129,193... | collective-permute-start | bytes 1572872 | tf_op jit(solution)/shard_map/ppermute | solution.py:496
  31.3 4.8 %collective-permute-start.4 = (f32[64,128]{1,0:T(8,128)S(1)}, f32[64,128]{1,0:T(8,128)S(1)}, u32[]{:S(2)}, u32[]{:S(2)}) collective-permute-start(f32[64,128]{1,0:T(8,128)S(1)} %get-tuple-element.30), channel_id=1, source_target_pairs={{0,2},{1,3},{2,0},{3,1},{4,6},{5,7},{6,4},{7,5},{8,10},{9,11},{10,... | collective-permute-start | bytes 98312 | tf_op jit(solution)/shard_map/ppermute | solution.py:515
  31.3 4.8 %collective-permute-start.3 = (f32[64,128]{1,0:T(8,128)S(1)}, f32[64,128]{1,0:T(8,128)S(1)}, u32[]{:S(2)}, u32[]{:S(2)}) collective-permute-start(f32[64,128]{1,0:T(8,128)S(1)} %get-tuple-element.30), channel_id=1, source_target_pairs={{0,1},{1,0},{2,3},{3,2},{4,5},{5,4},{6,7},{7,6},{8,9},{9,8},{10,11... | collective-permute-start | bytes 98312 | tf_op jit(solution)/shard_map/ppermute | solution.py:515
  36.1 8.1 %collective-permute-start.6 = (f32[64,128]{1,0:T(8,128)S(1)}, f32[64,128]{1,0:T(8,128)S(1)}, u32[]{:S(2)}, u32[]{:S(2)}) collective-permute-start(f32[64,128]{1,0:T(8,128)S(1)} %add_add_fusion), channel_id=1, source_target_pairs={{0,4},{1,5},{2,6},{3,7},{4,0},{5,1},{6,2},{7,3},{8,12},{9,13},{10,... | collective-permute-start | bytes 98312 | tf_op jit(solution)/shard_map/ppermute | solution.py:517
  44.2 2.2 %copy-start.2 = (bf16[1,2,128,8192]{3,2,1,0:T(8,128)(2,1)S(1)}, bf16[1,2,128,8192]{3,2,1,0:T(8,128)(2,1)}, u32[]{:S(2)}) copy-start(bf16[1,2,128,8192]{3,2,1,0:T(8,128)(2,1)} %param.14) | copy-start | bytes 12582916
  55.9 0.8 copy-start.3
  56.7 26.3 %copy-start.1 = (bf16[256,2048]{1,0:T(8,128)(2,1)S(1)}, bf16[256,2048]{1,0:T(8,128)(2,1)}, u32[]{:S(2)}) copy-start(bf16[256,2048]{1,0:T(8,128)(2,1)} %get-tuple-element.26.behind_ref.weight_ref) | copy-start | bytes 3145732
  56.7 12.4 %all-to-all-start.1 = ((bf16[4,544,128]{2,1,0:T(8,128)(2,1)}), bf16[4,544,128]{2,1,0:T(8,128)(2,1)S(1)}, u32[]{:S(2)}, u32[]{:S(2)}) async-start(bf16[4,544,128]{2,1,0:T(8,128)(2,1)} %copy-done.3), calls=%async_computation.1 | async-start | bytes 1114112 | tf_op jit(solution)/shard_map/all_to_all | solution.py:499
  60.9 13.9 %collective-permute-start.10 = (bf16[128,2048]{1,0:T(8,128)(2,1)S(1)}, bf16[128,2048]{1,0:T(8,128)(2,1)}, u32[]{:S(2)}, u32[]{:S(2)}) collective-permute-start(bf16[128,2048]{1,0:T(8,128)(2,1)S(1)} %collective-permute-done.7.refs_0_), channel_id=1, source_target_pairs={{0,8},{8,0},{16,24},{24,16},{32,40},{40,32},{48,56},{56,48},{1,9},... | collective-permute-start | bytes 1572872 | tf_op jit(solution)/shard_map/ppermute | solution.py:502
  60.9 13.9 %collective-permute-start.11 = (bf16[128,2048]{1,0:T(8,128)(2,1)S(1)}, bf16[128,2048]{1,0:T(8,128)(2,1)}, u32[]{:S(2)}, u32[]{:S(2)}) collective-permute-start(bf16[128,2048]{1,0:T(8,128)(2,1)S(1)} %collective-permute-done.8.refs_2_), channel_id=1, source_target_pairs={{0,8},{8,0},{16,24},{24,16},{32,40},{40,32},{48,56},{56,48},{1,9},... | collective-permute-start | bytes 1572872 | tf_op jit(solution)/shard_map/ppermute | solution.py:502
  61.4 13.4 %collective-permute-start.12 = (bf16[128,2048]{1,0:T(8,128)(2,1)S(1)}, bf16[128,2048]{1,0:T(8,128)(2,1)}, u32[]{:S(2)}, u32[]{:S(2)}) collective-permute-start(bf16[128,2048]{1,0:T(8,128)(2,1)S(1)} %collective-permute-done.9.refs_4_), channel_id=1, source_target_pairs={{0,8},{8,0},{16,24},{24,16},{32,40},{40,32},{48,56},{56,48},{1,9},... | collective-permute-start | bytes 1572872 | tf_op jit(solution)/shard_map/ppermute | solution.py:502
  71.3 11.6 %all-to-all-start.2 = ((bf16[4,528,128]{2,1,0:T(8,128)(2,1)}), bf16[4,528,128]{2,1,0:T(8,128)(2,1)S(1)}, u32[]{:S(2)}, u32[]{:S(2)}) async-start(bf16[4,528,128]{2,1,0:T(8,128)(2,1)} %shard_map.99), calls=%async_computation.2 | async-start | bytes 1081344 | tf_op jit(solution)/shard_map/all_to_all | solution.py:499
  85.8 17.6 %collective-permute-start.13 = (bf16[272,256]{1,0:T(8,128)(2,1)S(1)}, bf16[272,256]{1,0:T(8,128)(2,1)S(1)}, u32[]{:S(2)}, u32[]{:S(2)}) collective-permute-start(bf16[272,256]{1,0:T(8,128)(2,1)S(1)} %get-tuple-element.40), channel_id=1, source_target_pairs={{0,4},{1,5},{2,6},{3,7},{4,0},{5,1},{6,2},{7,3},{8,12},{9,13},{10,... | collective-permute-start | bytes 417800 | tf_op jit(solution)/shard_map/ppermute | solution.py:529
  90.2 16.0 %collective-permute-start.14 = (bf16[272,256]{1,0:T(8,128)(2,1)S(1)}, bf16[272,256]{1,0:T(8,128)(2,1)S(1)}, u32[]{:S(2)}, u32[]{:S(2)}) collective-permute-start(bf16[272,256]{1,0:T(8,128)(2,1)S(1)} %get-tuple-element.41), channel_id=1, source_target_pairs={{0,3},{1,4},{2,5},{3,6},{4,7},{5,0},{6,1},{7,2},{8,11},{9,12},{10,... | collective-permute-start | bytes 417800 | tf_op jit(solution)/shard_map/ppermute | solution.py:529
  92.1 19.9 %copy-start.8 = (s32[2,16]{1,0:T(2,128)S(1)}, s32[2,16]{1,0:T(2,128)}, u32[]{:S(2)}) copy-start(s32[2,16]{1,0:T(2,128)} %refs_8_.1) | copy-start | bytes 388
  92.1 14.5 %collective-permute-start.15 = (bf16[272,256]{1,0:T(8,128)(2,1)S(1)}, bf16[272,256]{1,0:T(8,128)(2,1)S(1)}, u32[]{:S(2)}, u32[]{:S(2)}) collective-permute-start(bf16[272,256]{1,0:T(8,128)(2,1)S(1)} %get-tuple-element.42), channel_id=1, source_target_pairs={{0,5},{1,6},{2,7},{3,0},{4,1},{5,2},{6,3},{7,4},{8,13},{9,14},{10,... | collective-permute-start | bytes 417800 | tf_op jit(solution)/shard_map/ppermute | solution.py:529
  99.1 8.5 %collective-permute-start.16 = (bf16[272,256]{1,0:T(8,128)(2,1)S(1)}, bf16[272,256]{1,0:T(8,128)(2,1)S(1)}, u32[]{:S(2)}, u32[]{:S(2)}) collective-permute-start(bf16[272,256]{1,0:T(8,128)(2,1)S(1)} %get-tuple-element.43), channel_id=1, source_target_pairs={{0,2},{1,3},{2,4},{3,5},{4,6},{5,7},{6,0},{7,1},{8,10},{9,11},{10,... | collective-permute-start | bytes 417800 | tf_op jit(solution)/shard_map/ppermute | solution.py:529
  101.7 9.1 %collective-permute-start.17 = (bf16[272,256]{1,0:T(8,128)(2,1)S(1)}, bf16[272,256]{1,0:T(8,128)(2,1)S(1)}, u32[]{:S(2)}, u32[]{:S(2)}) collective-permute-start(bf16[272,256]{1,0:T(8,128)(2,1)S(1)} %get-tuple-element.44), channel_id=1, source_target_pairs={{0,6},{1,7},{2,0},{3,1},{4,2},{5,3},{6,4},{7,5},{8,14},{9,15},{10,... | collective-permute-start | bytes 417800 | tf_op jit(solution)/shard_map/ppermute | solution.py:529
  103.3 7.5 %collective-permute-start.18 = (bf16[272,256]{1,0:T(8,128)(2,1)S(1)}, bf16[272,256]{1,0:T(8,128)(2,1)S(1)}, u32[]{:S(2)}, u32[]{:S(2)}) collective-permute-start(bf16[272,256]{1,0:T(8,128)(2,1)S(1)} %get-tuple-element.45), channel_id=1, source_target_pairs={{0,1},{1,2},{2,3},{3,4},{4,5},{5,6},{6,7},{7,0},{8,9},{9,10},{10,1... | collective-permute-start | bytes 417800 | tf_op jit(solution)/shard_map/ppermute | solution.py:529
  106.3 5.6 %collective-permute-start.19 = (bf16[272,256]{1,0:T(8,128)(2,1)S(1)}, bf16[272,256]{1,0:T(8,128)(2,1)S(1)}, u32[]{:S(2)}, u32[]{:S(2)}) collective-permute-start(bf16[272,256]{1,0:T(8,128)(2,1)S(1)} %get-tuple-element.46), channel_id=1, source_target_pairs={{0,7},{1,0},{2,1},{3,2},{4,3},{5,4},{6,5},{7,6},{8,15},{9,8},{10,9... | collective-permute-start | bytes 417800 | tf_op jit(solution)/shard_map/ppermute | solution.py:529
